TPU v7x, 32 devices: a whole 2x2x4 slice. The times are simulated.
32 devices in a mesh: tile: 16 (over z, y, core), head: 2 (over x).
Axes of the slice: x: 2, y: 2, z: 4, core: 2. Of those that a mesh axis runs over, the one named last changes fastest.
Arguments:
- vision_rows: bfloat16 [512, 8, 768], P(('tile', 'head')), may hold values from -6 to 6
- positions: int32 [3, 512], P(None, ('tile', 'head')), may hold values from 0 to 63
- destination: int32 [512, 1], replicated, may hold values from 0 to 15; in each aligned block of 16 rows (0 to 15, 16 to 31, ...) at most 2 rows name the same one
- out_grad: bfloat16 [1024, 8, 512], P(('tile', 'head')), may hold values from -6 to 6
Outputs:
- row_grads: bfloat16 [512, 8, 768], P(('tile', 'head'))
Inputs may be any that keep to these rules, and one draw needn't show every extreme that they name: `destination`: among the 16 tokens of one device (aligned blocks of rows) no tile is named more than 2 times, and some block names a tile exactly 2 times.
All inputs are finite; a program needn't handle non-finite values.
Results may differ from a plain program's by a relative error of at most 0.01.
Values may be sent and summed in bfloat16 or wider, within the bound.
No kernel may reach another device: no remote copies, remote signals or barrier semaphores. Data moves between devices by JAX's collectives and lax.ppermute only.
A program may use at most 64 MiB of HBM per device.

v0:
```python
import jax
import jax.numpy as jnp
from jax import lax
from jax.sharding import PartitionSpec as P

KV = 8
HD = 128
C = 2
QPK = 4


def rope_parts(positions):
    half = HD // 2
    slots = jnp.arange(half, dtype=jnp.int32)
    first = half // 4
    second = (half - first) // 2
    section = jnp.where(slots < first, 0, jnp.where(slots < first + second, 1, 2))
    picks = (section[:, None] == jnp.arange(3, dtype=jnp.int32)[None, :]).astype(jnp.float32)
    chosen = jnp.dot(picks, positions.astype(jnp.float32), precision=lax.Precision.HIGHEST)
    freq = jnp.exp(-(2.0 * slots.astype(jnp.float32) / HD) * jnp.log(jnp.float32(1000000.0)))
    angle = jnp.transpose(chosen) * freq[None, :]
    return (jnp.cos(angle), jnp.sin(angle))


def rotate(x, cosv, sinv):
    half = x.shape[-1] // 2
    first, second = (x[..., :half], x[..., half:])
    return jnp.concatenate([first * cosv - second * sinv, second * cosv + first * sinv], -1)


def unrotate(x, cosv, sinv):
    half = x.shape[-1] // 2
    first, second = (x[..., :half], x[..., half:])
    return jnp.concatenate([first * cosv + second * sinv, second * cosv - first * sinv], -1)


def turn_rows(rows, cosv, sinv, turner):
    count = rows.shape[0]
    groups = rows.shape[1]
    query = rows[:, :, : QPK * HD].reshape(count, groups, QPK, HD)
    query = turner(query, cosv[:, None, None, :], sinv[:, None, None, :]).reshape(
        count, groups, QPK * HD
    )
    key = turner(rows[:, :, QPK * HD : (QPK + 1) * HD], cosv[:, None, :], sinv[:, None, :])
    return jnp.concatenate([query, key, rows[:, :, (QPK + 1) * HD :]], 2)


def block_terms(query, key, value, cot, valid, first):
    count = query.shape[0]
    length = key.shape[0]
    scale = HD ** (-0.5)
    score = jnp.einsum("iqd,jd->qij", query, key, preferred_element_type=jnp.float32) * scale
    rows_at = first + jnp.arange(count, dtype=jnp.int32)
    cols = jnp.arange(length, dtype=jnp.int32)
    allowed = (cols[None, :] <= rows_at[:, None]) & valid[None, :]
    score = jnp.where(allowed[None], score, -1e30)
    top = jnp.max(score, axis=-1, keepdims=True)
    weight = jnp.exp(score - top)
    probs = (weight / jnp.sum(weight, axis=-1, keepdims=True)).astype(jnp.bfloat16)
    output = jnp.einsum("qij,jd->iqd", probs, value, preferred_element_type=jnp.float32).astype(
        jnp.bfloat16
    )
    dvalue = jnp.einsum("qij,iqd->jd", probs, cot, preferred_element_type=jnp.float32)
    dprob = jnp.einsum("iqd,jd->qij", cot, value, preferred_element_type=jnp.float32)
    delta = jnp.transpose(jnp.sum(cot.astype(jnp.float32) * output.astype(jnp.float32), axis=-1))
    dscore = (probs.astype(jnp.float32) * (dprob - delta[:, :, None])).astype(jnp.bfloat16)
    dquery = (
        jnp.einsum("qij,jd->iqd", dscore, key, preferred_element_type=jnp.float32) * scale
    ).astype(jnp.bfloat16)
    dkey = jnp.einsum("qij,iqd->jd", dscore, query, preferred_element_type=jnp.float32) * scale
    return (dquery, dkey, dvalue)


def body(vision_rows, positions, destination, out_grad):
    tiles = lax.axis_size("tile")
    heads = lax.axis_size("head")
    tile_pos = lax.axis_index("tile")
    head_pos = lax.axis_index("head")
    vis_dev = vision_rows.shape[0]
    width = vision_rows.shape[2]
    qcols = QPK * HD
    cosv, sinv = rope_parts(positions)
    rotated = turn_rows(vision_rows.astype(jnp.float32), cosv, sinv, rotate).astype(jnp.bfloat16)
    routes = destination[:, 0].reshape(tiles, heads, vis_dev)
    own = lax.dynamic_slice(routes, (tile_pos, head_pos, jnp.int32(0)), (1, 1, vis_dev))[0, 0]
    targets = jnp.arange(tiles, dtype=jnp.int32)
    onehot = (own[:, None] == targets[None, :]).astype(jnp.int32)
    rank = jnp.sum(onehot * (jnp.cumsum(onehot, 0) - onehot), 1)
    slot = own * C + rank
    pack = (jnp.arange(tiles * C, dtype=jnp.int32)[:, None] == slot[None, :]).astype(jnp.bfloat16)
    outgoing = jnp.dot(
        pack, rotated.reshape(vis_dev, KV * width), preferred_element_type=jnp.float32
    )
    outgoing = outgoing.astype(jnp.bfloat16).reshape(tiles, C, KV, width)
    counts = jnp.sum((routes == tile_pos).astype(jnp.int32), 2)
    valid = (
        jnp.arange(C, dtype=jnp.int32)[None, None, :] < jnp.transpose(counts)[:, :, None]
    ).reshape(-1)
    seq = heads * tiles * C
    kv_local = KV // heads
    incoming_cot = lax.all_to_all(out_grad, "head", split_axis=1, concat_axis=0, tiled=True)
    seq_rows = lax.all_to_all(
        lax.all_to_all(outgoing, "tile", split_axis=0, concat_axis=0, tiled=True),
        "head",
        split_axis=2,
        concat_axis=0,
        tiled=True,
    ).reshape(seq, kv_local, width)
    masked_cot = jnp.where(valid[:, None, None], incoming_cot, jnp.zeros((), jnp.bfloat16))
    block = min(512, seq)
    results = []
    for group in range(kv_local):
        rows = seq_rows[:, group]
        query = rows[:, :qcols].reshape(seq, QPK, HD)
        key = rows[:, qcols : qcols + HD]
        value = rows[:, qcols + HD :]
        cot = masked_cot[:, group].reshape(seq, QPK, HD)
        dkey_sum = jnp.zeros((seq, HD), jnp.float32)
        dvalue_sum = jnp.zeros((seq, HD), jnp.float32)
        pieces = []
        for first in range(0, seq, block):
            dquery, dkey, dvalue = block_terms(
                query[first : first + block], key, value, cot[first : first + block], valid, first
            )
            pieces.append(dquery.reshape(block, qcols))
            dkey_sum = dkey_sum + dkey
            dvalue_sum = dvalue_sum + dvalue
        results.append(
            jnp.concatenate(
                [
                    jnp.concatenate(pieces, 0),
                    dkey_sum.astype(jnp.bfloat16),
                    dvalue_sum.astype(jnp.bfloat16),
                ],
                1,
            )
        )
    grads = jnp.stack(results, 1).reshape(heads, tiles, C, kv_local, width)
    returned = lax.all_to_all(
        lax.all_to_all(grads, "tile", split_axis=1, concat_axis=1, tiled=True),
        "head",
        split_axis=0,
        concat_axis=3,
        tiled=True,
    )
    received = returned.reshape(tiles * C, KV * width)
    row_terms = jnp.einsum("sr,sc->rc", pack, received, preferred_element_type=jnp.float32)
    return turn_rows(row_terms.reshape(vis_dev, KV, width), cosv, sinv, unrotate).astype(
        jnp.bfloat16
    )


def solution(mesh):
    return jax.shard_map(
        body,
        mesh=mesh,
        in_specs=(
            P(("tile", "head"), None, None),
            P(None, ("tile", "head")),
            P(),
            P(("tile", "head"), None, None),
        ),
        out_specs=P(("tile", "head"), None, None),
        check_vma=False,
    )
```

profile of v0, /device:TPU:0, one launch (start us, length us, event | category | flops | bytes accessed | tf_op | source)
XLA Modules:
  0.0 78.0 jit_solution(1018780172801245527)
XLA Ops:
  0.0 1.7 %copy.180 = bf16[32,8,512]{2,0,1:T(8,128)(2,1)} copy(bf16[32,8,512]{2,1,0:T(8,128)(2,1)} %param.7) | data formatting | bytes 524288 | tf_op args[3]
  1.7 4.3 %all-to-all-start.2 = ((bf16[32,8,512]{2,0,1:T(8,128)(2,1)}), bf16[32,8,512]{2,0,1:T(8,128)(2,1)S(1)}, u32[]{:S(2)}, u32[]{:S(2)}) async-start(bf16[32,8,512]{2,0,1:T(8,128)(2,1)} %copy.180), calls=%async_computation.2 | async-start | bytes 524288 | tf_op jit(solution)/shard_map/all_to_all | solution.py:101
  6.2 0.5 broadcast.144
  6.8 0.7 reduce.3
  8.1 0.6 copy-done.2
  8.6 0.3 cosine_bitcast_fusion
  9.0 0.3 subtract_convert_fusion.1
  9.6 0.7 slice-done
  10.5 0.4 convolution_convert_fusion
  10.9 1.0 %copy.175 = bf16[16,2,8,768]{3,1,2,0:T(2,128)(2,1)} copy(bf16[16,2,8,768]{3,2,1,0:T(8,128)(2,1)S(1)} %bitcast.345) | data formatting | bytes 786432 | tf_op jit(solution)/shard_map/reshape | solution.py:94
  12.0 6.7 %all-to-all-start = ((bf16[16,2,8,768]{3,1,2,0:T(2,128)(2,1)}), bf16[16,2,8,768]{3,1,2,0:T(2,128)(2,1)S(1)}, u32[]{:S(2)}, u32[]{:S(2)}) async-start(bf16[16,2,8,768]{3,1,2,0:T(2,128)(2,1)} %copy.175), calls=%async_computation | async-start | bytes 786432 | tf_op jit(solution)/shard_map/all_to_all | solution.py:103
  18.6 0.3 fusion.96
  19.5 11.4 %all-to-all-done = bf16[16,2,8,768]{3,1,2,0:T(2,128)(2,1)S(1)} async-done(((bf16[16,2,8,768]{3,1,2,0:T(2,128)(2,1)}), bf16[16,2,8,768]{3,1,2,0:T(2,128)(2,1)S(1)}, u32[]{:S(2)}, u32[]{:S(2)}) %all-to-all-start) | async-done | bytes 393248 | tf_op jit(solution)/shard_map/all_to_all | solution.py:103
  30.8 1.0 %copy.176 = bf16[16,2,8,768]{3,1,0,2:T(2,128)(2,1)} copy(bf16[16,2,8,768]{3,1,2,0:T(2,128)(2,1)S(1)} %all-to-all-done) | data formatting | bytes 786432 | tf_op jit(solution)/shard_map/all_to_all | solution.py:103
  31.9 3.5 %all-to-all-start.1 = ((bf16[16,2,8,768]{3,1,0,2:T(2,128)(2,1)}), bf16[16,2,8,768]{3,1,0,2:T(2,128)(2,1)S(1)}, u32[]{:S(2)}, u32[]{:S(2)}) async-start(bf16[16,2,8,768]{3,1,0,2:T(2,128)(2,1)} %copy.176), calls=%async_computation.1 | async-start | bytes 786432 | tf_op jit(solution)/shard_map/all_to_all | solution.py:102
  35.5 7.2 %all-to-all-done.1 = bf16[16,2,8,768]{3,1,0,2:T(2,128)(2,1)S(1)} async-done(((bf16[16,2,8,768]{3,1,0,2:T(2,128)(2,1)}), bf16[16,2,8,768]{3,1,0,2:T(2,128)(2,1)S(1)}, u32[]{:S(2)}, u32[]{:S(2)}) %all-to-all-start.1) | async-done | bytes 393248 | tf_op jit(solution)/shard_map/all_to_all | solution.py:102
  42.7 0.3 copy.320
  43.2 0.2 fusion.133
  43.5 0.3 fusion.51
  43.8 0.2 fusion.67
  44.2 0.2 fusion.66
  44.4 0.2 fusion.52
  44.6 0.2 fusion.136
  44.9 0.3 fusion.50
  45.2 0.2 fusion.65
  45.4 0.2 fusion.45
  45.6 0.2 fusion.64
  45.8 0.2 fusion.53
  46.0 0.2 fusion.139
  46.3 0.3 fusion.49
  46.6 0.2 fusion.63
  47.0 0.2 fusion.62
  47.2 0.2 fusion.54
  47.4 0.2 fusion.142
  47.7 0.3 fusion.48
  48.0 0.2 fusion.61
  48.4 0.2 fusion.60
  48.6 0.2 fusion.55
  49.3 0.4 maximum_maximum_fusion
  49.7 0.3 copy.213
  50.0 15.7 %all_to_all.58 = bf16[2,16,2,4,768]{4,2,0,3,1:T(2,128)(2,1)S(1)} all-to-all(bf16[2,16,2,4,768]{4,2,0,3,1:T(2,128)(2,1)S(1)} %copy.213), channel_id=1, replica_groups=mesh['tile'=16,'head'=2] {'tile'}, dimensions={1} | all-to-all | bytes 786432 | tf_op jit(solution)/shard_map/all_to_all | solution.py:140
  65.7 0.3 copy.214
  66.0 9.5 %all_to_all.59 = bf16[2,16,2,4,768]{4,2,1,3,0:T(2,128)(2,1)S(1)} all-to-all(bf16[2,16,2,4,768]{4,2,1,3,0:T(2,128)(2,1)S(1)} %copy.214), channel_id=1, replica_groups=mesh['tile'=16,'head'=2] {'head'}, dimensions={0} | all-to-all | bytes 786432 | tf_op jit(solution)/shard_map/all_to_all | solution.py:139
  75.5 0.3 copy.215
  75.8 0.3 reshape.175
  76.1 0.3 fusion.68
  76.6 0.3 add_convert_fusion
  77.2 0.8 pad_maximum_fusion.1
  (65 shorter events, 3.6 us)
Async XLA Ops:
  1.7 4.4 %copy-start = (bf16[16,8,768]{2,1,0:T(8,128)(2,1)S(1)}, bf16[16,8,768]{2,1,0:T(8,128)(2,1)}, u32[]{:S(2)}) copy-start(bf16[16,8,768]{2,1,0:T(8,128)(2,1)} %param.4) | copy-start | bytes 589828
  1.7 10.2 %all-to-all-start.2 = ((bf16[32,8,512]{2,0,1:T(8,128)(2,1)}), bf16[32,8,512]{2,0,1:T(8,128)(2,1)S(1)}, u32[]{:S(2)}, u32[]{:S(2)}) async-start(bf16[32,8,512]{2,0,1:T(8,128)(2,1)} %copy.180), calls=%async_computation.2 | async-start | bytes 524288 | tf_op jit(solution)/shard_map/all_to_all | solution.py:101
  6.1 0.7 copy-start.1
  7.9 0.7 copy-start.2
  9.6 0.8 slice-start
  12.0 18.9 %all-to-all-start = ((bf16[16,2,8,768]{3,1,2,0:T(2,128)(2,1)}), bf16[16,2,8,768]{3,1,2,0:T(2,128)(2,1)S(1)}, u32[]{:S(2)}, u32[]{:S(2)}) async-start(bf16[16,2,8,768]{3,1,2,0:T(2,128)(2,1)} %copy.175), calls=%async_computation | async-start | bytes 786432 | tf_op jit(solution)/shard_map/all_to_all | solution.py:103
  31.9 10.8 %all-to-all-start.1 = ((bf16[16,2,8,768]{3,1,0,2:T(2,128)(2,1)}), bf16[16,2,8,768]{3,1,0,2:T(2,128)(2,1)S(1)}, u32[]{:S(2)}, u32[]{:S(2)}) async-start(bf16[16,2,8,768]{3,1,0,2:T(2,128)(2,1)} %copy.176), calls=%async_computation.1 | async-start | bytes 786432 | tf_op jit(solution)/shard_map/all_to_all | solution.py:102
where the time goes:
time: 78.5 us; the launch traced here: 78 us
  blocking collectives  25.2 us (32%)
  waiting for transfers between devices  18.6 us (24%)
  starting transfers between devices  14.5 us (18%)
  local copies, waits for them, and re-layouts  8.76 us (11%)
  matrix products  6.34 us (8%)
  other arithmetic  4.06 us (5%)
    all_to_all x1, blocking collectives, body(): lax.all_to_all(grads, 'tile', split_axis=1, concat_axis=1, tiled=True)  15.7 us
    all_to_all x1, waiting for transfers between devices, body(): lax.all_to_all(outgoing, 'tile', split_axis=0, concat_axis=0, tiled=True)  11.4 us
    all_to_all x1, blocking collectives, body(): lax.all_to_all(lax.all_to_all(grads, 'tile', split_axis=1, concat_axis=1,...  9.53 us
    all_to_all x1, waiting for transfers between devices, body(): lax.all_to_all(lax.all_to_all(outgoing, 'tile', split_axis=0, concat_axis...  7.23 us
    all_to_all x1, starting transfers between devices, body(): lax.all_to_all(outgoing, 'tile', split_axis=0, concat_axis=0, tiled=True)  6.65 us
    all_to_all x1, starting transfers between devices, body(): lax.all_to_all(out_grad, 'head', split_axis=1, concat_axis=0, tiled=True)  4.34 us
    all_to_all x1, starting transfers between devices, body(): lax.all_to_all(lax.all_to_all(outgoing, 'tile', split_axis=0, concat_axis...  3.46 us
    unnamed x12, local copies, waits for them, and re-layouts  3.11 us
  transfers between devices with their start and end apart: 3, of which 2 were waited for; matrix products, arithmetic and copies ran while one was open for 7% of the time, Pallas kernels for 0%

commit v1 on v0

v1 whole, which is shorter than its diff:
```python
import functools
import math

import jax
import jax.numpy as jnp
from jax import lax
from jax.experimental import pallas as pl
from jax.experimental.pallas import tpu as pltpu
from jax.sharding import PartitionSpec as P

KV = 8
HD = 128
C = 2
QPK = 4
LANES = 128
F32 = jnp.float32
BF16 = jnp.bfloat16
NEG = -1e30
VMEM = pl.BlockSpec(memory_space=pltpu.VMEM)


def nt(a, b):
    return lax.dot_general(a, b, (((1,), (1,)), ((), ())), preferred_element_type=F32)


def iota(shape, dim):
    return lax.broadcasted_iota(jnp.int32, shape, dim)


def rope_tables(pos_ref):
    tokens = pos_ref.shape[1]
    half = HD // 2
    slots = iota((tokens, HD), 1) % half
    first = half // 4
    second = (half - first) // 2
    eye = (iota((tokens, tokens), 0) == iota((tokens, tokens), 1)).astype(BF16)
    column = [
        nt(eye, jnp.broadcast_to(pos_ref[s : s + 1, :].astype(F32).astype(BF16), (HD, tokens)))
        for s in range(3)
    ]
    chosen = jnp.where(
        slots < first, column[0], jnp.where(slots < first + second, column[1], column[2])
    )
    freq = jnp.exp(-(2.0 * slots.astype(F32) / HD) * math.log(1000000.0))
    angle = chosen * freq
    sign = jnp.where(iota((tokens, HD), 1) < half, -1.0, 1.0)
    return jnp.cos(angle), jnp.sin(angle) * sign


def per_group(table):
    tokens = table.shape[0]
    return jnp.broadcast_to(table[:, None, :], (tokens, KV, HD)).reshape(tokens * KV, HD)


def own_row(dest_ref, tokens):
    start = (lax.axis_index("tile") * lax.axis_size("head") + lax.axis_index("head")) * tokens
    row = dest_ref[pl.ds(start // LANES, 1), :].astype(F32).astype(BF16)
    return row, start % LANES


def own_targets(dest_ref, tokens, rows):
    row, off = own_row(dest_ref, tokens)
    count = tokens * KV
    wide = (iota((count, LANES), 1) == off + iota((count, LANES), 0) // KV).astype(BF16)
    narrow = (iota((tokens, LANES), 1) == off + iota((tokens, LANES), 0)).astype(BF16)
    along = nt(jnp.broadcast_to(row, (8, LANES)), wide)[:1]
    down = nt(narrow, jnp.broadcast_to(row, (rows, LANES)))
    return along, down


def slot_keys(dest_ref, tokens):
    count = tokens * KV
    along, down = own_targets(dest_ref, tokens, count)
    lane = iota((tokens, count), 1)
    earlier = (down == along) & (iota((tokens, count), 0) < lane // KV)
    rank = jnp.sum(earlier.astype(F32), axis=0, keepdims=True)
    return ((along * C + rank) * KV).astype(jnp.int32) + iota((1, count), 1) % KV


def row_keys(shape, dim, tiles, local):
    at = iota(shape, dim)
    slots = tiles * C
    return ((at // local) % slots) * KV + (at // (slots * local)) * local + at % local


def pack_kernel(vis_ref, pos_ref, dest_ref, out_ref, *, tiles, local):
    count, width = vis_ref.shape
    tokens = count // KV
    total = out_ref.shape[0]
    cosv, sinv = rope_tables(pos_ref)
    cosv, sinv = per_group(cosv), per_group(sinv)
    place = (row_keys((total, count), 0, tiles, local) == slot_keys(dest_ref, tokens)).astype(BF16)
    for at in range(0, width, HD):
        x = vis_ref[:, at : at + HD]
        if at < (QPK + 1) * HD:
            x = x.astype(F32)
            x = (x * cosv + pltpu.roll(x, HD // 2, 1) * sinv).astype(BF16)
        out_ref[:, at : at + HD] = jnp.dot(place, x, preferred_element_type=F32).astype(BF16)


def side_kernel(
    pos_ref, dest_ref, after_ref, cos_ref, sin_ref, gather_ref, bias_ref, valid_ref, *, tiles, heads, local
):
    del after_ref
    tokens = pos_ref.shape[1]
    count = tokens * KV
    total = heads * tiles * C * local
    cosv, sinv = rope_tables(pos_ref)
    cos_ref[...] = per_group(cosv)
    sin_ref[...] = per_group(sinv)
    place = row_keys((total, count), 0, tiles, local) == slot_keys(dest_ref, tokens)
    gather_ref[...] = jnp.transpose(place.astype(F32)).astype(BF16)
    mine = lax.axis_index("tile")
    at = iota((total, LANES), 0)
    slots = tiles * C
    device = ((at // (C * local)) % tiles) * heads + at // (slots * local)

    def tally(block, sums):
        hit = (dest_ref[pl.ds(block, 1), :] == mine).astype(F32).astype(BF16)
        source = (block * LANES + iota((total, LANES), 1)) // tokens
        return sums + nt((source == device).astype(F32).astype(BF16), jnp.broadcast_to(hit, (LANES, LANES)))

    counts = lax.fori_loop(0, dest_ref.shape[0], tally, jnp.zeros((total, LANES), F32))
    valid = counts > ((at // local) % C).astype(F32)
    valid_ref[...] = valid.astype(F32)
    key_ok = jnp.where(valid, 0.0, NEG)
    key = iota((total, LANES), 0)
    for first in range(0, total, LANES):
        query = first + iota((total, LANES), 1)
        seen = (key // local <= query // local) & (key % local == query % local)
        bias_ref[:, first : first + LANES] = jnp.where(seen, key_ok, NEG)


def split_kernel(cot_ref, own_ref, other_ref, *, local):
    head = lax.axis_index("head")
    total, count = own_ref.shape[0], cot_ref.shape[0]
    row, lane = iota((total, count), 0), iota((total, count), 1)
    base = (row // local) * KV + row % local
    cot = cot_ref[...]
    for ref, group in ((own_ref, head), (other_ref, 1 - head)):
        pick = (lane == base + group * local).astype(BF16)
        ref[...] = jnp.dot(pick, cot, preferred_element_type=F32).astype(BF16)


def attend_kernel(rows_ref, bias_ref, valid_ref, *refs, pair):
    cot_refs, (out_ref, cot_at, dkey_at, dvalue_at) = refs[: 1 + pair], refs[1 + pair :]
    total = rows_ref.shape[0]
    block = min(256, total)
    qcols = QPK * HD
    scale = HD ** (-0.5)
    if pair:
        half = total // 2
        head = lax.axis_index("head")
        cot_at[pl.ds(pl.multiple_of(head * half, half), half), :] = cot_refs[0][...]
        cot_at[pl.ds(pl.multiple_of((1 - head) * half, half), half), :] = cot_refs[1][...]
    else:
        cot_at[...] = cot_refs[0][...]
    key = rows_ref[:, qcols : qcols + HD]
    value = rows_ref[:, qcols + HD :]

    def step(at):
        rows = pl.ds(at, block)
        ok = valid_ref[rows, :] > 0.0
        dkey = jnp.zeros((total, HD), F32)
        dvalue = jnp.zeros((total, HD), F32)
        for q in range(QPK):
            cols = slice(q * HD, (q + 1) * HD)
            query = rows_ref[rows, cols]
            cot = jnp.where(ok, cot_at[rows, cols].astype(F32), 0.0).astype(BF16)
            score = nt(key, query) * scale + bias_ref[:, pl.ds(at, block)]
            weight = jnp.exp(score - jnp.max(score, axis=0, keepdims=True))
            probs = (weight * (1.0 / jnp.sum(weight, axis=0, keepdims=True))).astype(BF16)
            dprob = nt(value, cot)
            wide = probs.astype(F32)
            delta = jnp.sum(wide * dprob, axis=0, keepdims=True)
            dscore = (wide * (dprob - delta)).astype(BF16)
            dvalue += jnp.dot(probs, cot, preferred_element_type=F32)
            dkey += jnp.dot(dscore, query, preferred_element_type=F32)
            dquery = lax.dot_general(
                dscore, key, (((0,), (0,)), ((), ())), preferred_element_type=F32
            )
            out_ref[rows, cols] = (dquery * scale).astype(BF16)
        return dkey, dvalue

    if total == block:
        dkey, dvalue = step(0)
    else:
        dkey_at[...] = jnp.zeros((total, HD), F32)
        dvalue_at[...] = jnp.zeros((total, HD), F32)

        @pl.loop(0, total // block)
        def _(index):
            dkey, dvalue = step(pl.multiple_of(index * block, block))
            dkey_at[...] += dkey
            dvalue_at[...] += dvalue

        dkey, dvalue = dkey_at[...], dvalue_at[...]
    out_ref[:, qcols : qcols + HD] = (dkey * scale).astype(BF16)
    out_ref[:, qcols + HD :] = dvalue.astype(BF16)


def gather_kernel(rows_ref, gather_ref, cos_ref, sin_ref, out_ref):
    width = rows_ref.shape[1]
    pick = gather_ref[...]
    for at in range(0, width, HD):
        x = jnp.dot(pick, rows_ref[:, at : at + HD], preferred_element_type=F32)
        if at < (QPK + 1) * HD:
            x = x * cos_ref[...] - pltpu.roll(x, HD // 2, 1) * sin_ref[...]
        out_ref[:, at : at + HD] = x.astype(BF16)


def call(kernel, outs, *args, scratch=()):
    shapes = [jax.ShapeDtypeStruct(s, d) for s, d in outs]
    single = len(shapes) == 1
    return pl.pallas_call(
        kernel,
        out_shape=shapes[0] if single else shapes,
        in_specs=[VMEM] * len(args),
        out_specs=VMEM if single else [VMEM] * len(shapes),
        scratch_shapes=list(scratch),
        compiler_params=pltpu.CompilerParams(vmem_limit_bytes=48 * 2**20),
    )(*args)


def body(vision_rows, positions, destination, out_grad):
    tiles = lax.axis_size("tile")
    heads = lax.axis_size("head")
    tokens, groups, width = vision_rows.shape
    local = groups // heads
    count = tokens * groups
    total = heads * tiles * C * local
    qcols = QPK * HD
    targets = destination.reshape(-1, LANES)
    outgoing = call(
        functools.partial(pack_kernel, tiles=tiles, local=local),
        [((total, width), BF16)],
        vision_rows.reshape(count, width),
        positions,
        targets,
    )

    def swap(rows):
        parts = rows.reshape(heads * tiles, C * local, width)
        parts = lax.all_to_all(parts, ("head", "tile"), split_axis=0, concat_axis=0, tiled=True)
        return parts.reshape(total, width)

    incoming = swap(outgoing)
    if heads == 2:
        slots = out_grad.shape[0]
        own, other = call(
            functools.partial(split_kernel, local=local),
            [((slots * local, qcols), BF16)] * 2,
            out_grad.reshape(slots * groups, qcols),
        )
        cots = [own, lax.ppermute(other, "head", [(0, 1), (1, 0)])]
    else:
        moved = lax.all_to_all(out_grad, "head", split_axis=1, concat_axis=0, tiled=True)
        cots = [moved.reshape(total, qcols)]
    cosv, sinv, gather, bias, valid = call(
        functools.partial(side_kernel, tiles=tiles, heads=heads, local=local),
        [
            ((count, HD), F32),
            ((count, HD), F32),
            ((count, total), BF16),
            ((total, total), F32),
            ((total, LANES), F32),
        ],
        positions,
        targets,
        outgoing[:16, :LANES],
    )
    grads = call(
        functools.partial(attend_kernel, pair=heads == 2),
        [((total, width), BF16)],
        incoming,
        bias,
        valid,
        *cots,
        scratch=(
            pltpu.VMEM((total, qcols), BF16),
            pltpu.VMEM((total, HD), F32),
            pltpu.VMEM((total, HD), F32),
        ),
    )
    result = call(gather_kernel, [((count, width), BF16)], swap(grads), gather, cosv, sinv)
    return result.reshape(tokens, groups, width)


def solution(mesh):
    return jax.shard_map(
        body,
        mesh=mesh,
        in_specs=(
            P(("tile", "head"), None, None),
            P(None, ("tile", "head")),
            P(),
            P(("tile", "head"), None, None),
        ),
        out_specs=P(("tile", "head"), None, None),
        check_vma=False,
    )
```

time: 78.5 us -> 42.2 us (0.54)
  blocking collectives: 25.2 us -> 15.2 us
  waiting for transfers between devices: 18.6 us -> 9.2 us
  matrix products: 6.34 us -> 0 us
  local copies, waits for them, and re-layouts: 8.76 us -> 2.97 us
  starting transfers between devices: 14.5 us -> 9.13 us
  Pallas kernels: 0 us -> 5.36 us
  other arithmetic: 4.06 us -> 0 us
    all_to_all x3 -> x1, waiting for transfers between devices: 18.6 us -> 4.26 us  [swap(): lax.all_to_all(parts, ('head', 'tile'), split_axis=0, concat_axis=0, tile...]
    all_to_all x2 -> x1, blocking collectives: 25.2 us -> 15.2 us  [swap(): lax.all_to_all(parts, ('head', 'tile'), split_axis=0, concat_axis=0, tile...]
    all_to_all x3 -> x1, starting transfers between devices: 14.5 us -> 7.3 us  [swap(): lax.all_to_all(parts, ('head', 'tile'), split_axis=0, concat_axis=0, tile...]
    dot_general x23 -> x0, matrix products: 5.38 us -> none  [the longest x4 1.27 us: block_terms(): jnp.einsum('qij,jd->iqd', probs, value, preferred_element_type=jnp.float32)]
    pallas_call x0 -> x5, Pallas kernels: none -> 5.36 us  [call(): pl.pallas_call(kernel, out_shape=shapes[0] if single else shapes, in_spec...]
    ppermute x0 -> x1, waiting for transfers between devices: none -> 4.94 us  [body(): cots = [own, lax.ppermute(other, 'head', [(0, 1), (1, 0)])]]
    all_to_all x5 -> x0, local copies, waits for them, and re-layouts: 1.91 us -> none  [the longest x1 1.04 us: body(): lax.all_to_all(outgoing, 'tile', split_axis=0, concat_axis=0, tiled=True)]
    ppermute x0 -> x1, starting transfers between devices: none -> 1.83 us  [body(): cots = [own, lax.ppermute(other, 'head', [(0, 1), (1, 0)])]]
  transfers between devices with their start and end apart: 3 -> 2, of which waited for: 2 -> 2; matrix products, arithmetic and copies ran while one was open for 7% -> 2% of each run, Pallas kernels for 0% -> 3%
where the time goes in v1:
time: 42.2 us; the launch traced here: 41.9 us
  blocking collectives  15.2 us (36%)
  waiting for transfers between devices  9.2 us (22%)
  starting transfers between devices  9.13 us (22%)
  Pallas kernels  5.36 us (13%)
  local copies, waits for them, and re-layouts  2.97 us (7%)
    all_to_all x1, blocking collectives, swap(): lax.all_to_all(parts, ('head', 'tile'), split_axis=0, concat_axis=0, tile...  15.2 us
    all_to_all x1, starting transfers between devices, swap(): lax.all_to_all(parts, ('head', 'tile'), split_axis=0, concat_axis=0, tile...  7.3 us
    pallas_call x5, Pallas kernels, call(): pl.pallas_call(kernel, out_shape=shapes[0] if single else shapes, in_spec...  5.36 us
    ppermute x1, waiting for transfers between devices, body(): cots = [own, lax.ppermute(other, 'head', [(0, 1), (1, 0)])]  4.94 us
    all_to_all x1, waiting for transfers between devices, swap(): lax.all_to_all(parts, ('head', 'tile'), split_axis=0, concat_axis=0, tile...  4.26 us
    unnamed x10, local copies, waits for them, and re-layouts  2.3 us
    ppermute x1, starting transfers between devices, body(): cots = [own, lax.ppermute(other, 'head', [(0, 1), (1, 0)])]  1.83 us
  transfers between devices with their start and end apart: 2, of which 2 were waited for; matrix products, arithmetic and copies ran while one was open for 2% of the time, Pallas kernels for 3%

profile of v1, /device:TPU:0, one launch (start us, length us, event | category | flops | bytes accessed | tf_op | source)
XLA Modules:
  0.0 41.9 jit_solution(11052004412712338241)
XLA Ops:
  0.0 0.0 copy-start.2
  0.0 0.7 %copy-done.2 = s32[3,16]{1,0:T(4,128)S(1)} copy-done((s32[3,16]{1,0:T(4,128)S(1)}, s32[3,16]{1,0:T(4,128)}, u32[]{:S(2)}) %copy-start.2) | copy-done | bytes 216
  0.7 0.0 copy-start.1
  0.7 0.9 %copy-done.1 = bf16[16,8,768]{2,1,0:T(8,128)(2,1)S(1)} copy-done((bf16[16,8,768]{2,1,0:T(8,128)(2,1)S(1)}, bf16[16,8,768]{2,1,0:T(8,128)(2,1)}, u32[]{:S(2)}) %copy-start.1) | copy-done | bytes 196632
  1.6 0.0 copy-start.3
  1.6 0.7 %copy-done.3 = s32[512,1]{0,1:T(1,128)S(1)} copy-done((s32[512,1]{0,1:T(1,128)S(1)}, s32[512,1]{0,1:T(1,128)}, u32[]{:S(2)}) %copy-start.3) | copy-done | bytes 2072
  2.3 1.3 %shard_map.46 = bf16[256,768]{1,0:T(8,128)(2,1)} custom-call(bf16[128,768]{1,0:T(8,128)(2,1)S(1)} %bitcast.12, s32[3,16]{1,0:T(4,128)S(1)} %copy-done.2, s32[4,128]{1,0:T(4,128)S(1)} %bitcast.13), custom_call_target="tpu_custom_call" | custom-call | tf_op jit(solution)/shard_map/pallas_call | solution.py:215
  3.6 0.0 copy-start
  3.6 7.3 %all-to-all-start = ((bf16[32,8,768]{2,1,0:T(8,128)(2,1)}), bf16[32,8,768]{2,1,0:T(8,128)(2,1)S(1)}, u32[]{:S(2)}, u32[]{:S(2)}) async-start(bf16[32,8,768]{2,1,0:T(8,128)(2,1)} %bitcast.2), calls=%async_computation | async-start | bytes 786432 | tf_op jit(solution)/shard_map/all_to_all | solution.py:244
  10.9 0.0 copy-done
  10.9 0.2 shard_map.48
  11.2 0.0 copy-start.4
  11.2 1.8 %collective-permute-start = (bf16[128,512]{1,0:T(8,128)(2,1)S(1)}, bf16[128,512]{1,0:T(8,128)(2,1)S(1)}, u32[]{:S(2)}, u32[]{:S(2)}) collective-permute-start(bf16[128,512]{1,0:T(8,128)(2,1)S(1)} %get-tuple-element.15), channel_id=1, source_target_pairs={{0,1},{1,0},{2,3},{3,2},{4,5},{5,4},{6,7},{7,6},{8,9},{9,8},{10,11... | collective-permute-start | bytes 393224 | tf_op jit(solution)/shard_map/ppermute | solution.py:255
  13.0 0.7 %slice.4.after_ref = bf16[16,128]{1,0:T(8,128)(2,1)S(1)} slice(bf16[256,768]{1,0:T(8,128)(2,1)} %shard_map.46), slice={[0:16], [0:128]} | slice | bytes 8192 | tf_op jit(solution)/shard_map/slice | solution.py:270
  13.7 0.0 copy-done.4
  13.7 1.1 %shard_map.47 = (f32[128,128]{1,0:T(8,128)S(1)}, f32[128,128]{1,0:T(8,128)S(1)}, bf16[128,256]{1,0:T(8,128)(2,1)S(1)}, f32[256,256]{1,0:T(8,128)S(1)}, f32[256,128]{1,0:T(8,128)S(1)}) custom-call(s32[3,16]{1,0:T(4,128)S(1)} %copy-done.2, s32[4,128]{1,0:T(4,128)S(1)} %bitcast.14, bf16[16,128]{1,0:T(8,128)(2,1)S(1)} %slice.4.after_ref), custom_call_target="tpu_custom_call" | custom-call | tf_op jit(solution)/shard_map/pallas_call | solution.py:215
  14.8 4.9 %collective-permute-done.refs_1_ = bf16[128,512]{1,0:T(8,128)(2,1)S(1)} collective-permute-done((bf16[128,512]{1,0:T(8,128)(2,1)S(1)}, bf16[128,512]{1,0:T(8,128)(2,1)S(1)}, u32[]{:S(2)}, u32[]{:S(2)}) %collective-permute-start) | collective-permute-done | bytes 131104 | tf_op jit(solution)/shard_map/ppermute | solution.py:255
  19.7 4.3 %all-to-all-done = bf16[32,8,768]{2,1,0:T(8,128)(2,1)S(1)} async-done(((bf16[32,8,768]{2,1,0:T(8,128)(2,1)}), bf16[32,8,768]{2,1,0:T(8,128)(2,1)S(1)}, u32[]{:S(2)}, u32[]{:S(2)}) %all-to-all-start) | async-done | bytes 393248 | tf_op jit(solution)/shard_map/all_to_all | solution.py:244
  24.0 1.7 %shard_map.49 = bf16[256,768]{1,0:T(8,128)(2,1)S(1)} custom-call(bf16[256,768]{1,0:T(8,128)(2,1)S(1)} %bitcast.9, f32[256,256]{1,0:T(8,128)S(1)} %get-tuple-element.12.bias_ref, f32[256,128]{1,0:T(8,128)S(1)} %get-tuple-element.13.valid_ref, bf16[128,512]{1,0:T(8,128)(2,1)S(1)} %get-tuple-element.14.refs_0_, bf16[128,512]{1,0:T(8,128)(2,1)S(1)} %collective-permute-done.refs_1_), custom_call_target="tpu_custom_call" | custom-call | tf_op jit(solution)/shard_map/pallas_call | solution.py:215
  25.7 15.2 %all_to_all.10 = bf16[32,8,768]{2,1,0:T(8,128)(2,1)S(1)} all-to-all(bf16[32,8,768]{2,1,0:T(8,128)(2,1)S(1)} %bitcast.10), channel_id=1, replica_groups=mesh['tile'=16,'head'=2] {'head','tile'}, dimensions={0} | all-to-all | bytes 786432 | tf_op jit(solution)/shard_map/all_to_all | solution.py:244
  40.9 1.0 %shard_map.50 = bf16[128,768]{1,0:T(8,128)(2,1)} custom-call(bf16[256,768]{1,0:T(8,128)(2,1)S(1)} %bitcast.8, bf16[128,256]{1,0:T(8,128)(2,1)S(1)} %get-tuple-element.16.gather_ref, f32[128,128]{1,0:T(8,128)S(1)} %get-tuple-element.17.cos_ref, f32[128,128]{1,0:T(8,128)S(1)} %get-tuple-element.18.sin_ref), custom_call_target="tpu_custom_call" | custom-call | tf_op jit(solution)/shard_map/pallas_call | solution.py:215
Async XLA Ops:
  0.0 0.7 %copy-start.2 = (s32[3,16]{1,0:T(4,128)S(1)}, s32[3,16]{1,0:T(4,128)}, u32[]{:S(2)}) copy-start(s32[3,16]{1,0:T(4,128)} %pos_ref.3) | copy-start | bytes 580
  0.7 0.9 %copy-start.1 = (bf16[16,8,768]{2,1,0:T(8,128)(2,1)S(1)}, bf16[16,8,768]{2,1,0:T(8,128)(2,1)}, u32[]{:S(2)}) copy-start(bf16[16,8,768]{2,1,0:T(8,128)(2,1)} %param.4) | copy-start | bytes 589828
  1.6 0.7 %copy-start.3 = (s32[512,1]{0,1:T(1,128)S(1)}, s32[512,1]{0,1:T(1,128)}, u32[]{:S(2)}) copy-start(s32[512,1]{0,1:T(1,128)} %param.6) | copy-start | bytes 6148
  3.6 7.3 %copy-start = (bf16[32,8,512]{2,1,0:T(8,128)(2,1)S(1)}, bf16[32,8,512]{2,1,0:T(8,128)(2,1)}, u32[]{:S(2)}) copy-start(bf16[32,8,512]{2,1,0:T(8,128)(2,1)} %param.7) | copy-start | bytes 786436
  3.6 20.4 %all-to-all-start = ((bf16[32,8,768]{2,1,0:T(8,128)(2,1)}), bf16[32,8,768]{2,1,0:T(8,128)(2,1)S(1)}, u32[]{:S(2)}, u32[]{:S(2)}) async-start(bf16[32,8,768]{2,1,0:T(8,128)(2,1)} %bitcast.2), calls=%async_computation | async-start | bytes 786432 | tf_op jit(solution)/shard_map/all_to_all | solution.py:244
  11.2 2.5 %copy-start.4 = (s32[512,1]{0,1:T(1,128)S(1)}, s32[512,1]{0,1:T(1,128)}, u32[]{:S(2)}) copy-start(s32[512,1]{0,1:T(1,128)} %param.6) | copy-start | bytes 6148
  11.2 8.6 %collective-permute-start = (bf16[128,512]{1,0:T(8,128)(2,1)S(1)}, bf16[128,512]{1,0:T(8,128)(2,1)S(1)}, u32[]{:S(2)}, u32[]{:S(2)}) collective-permute-start(bf16[128,512]{1,0:T(8,128)(2,1)S(1)} %get-tuple-element.15), channel_id=1, source_target_pairs={{0,1},{1,0},{2,3},{3,2},{4,5},{5,4},{6,7},{7,6},{8,9},{9,8},{10,11... | collective-permute-start | bytes 393224 | tf_op jit(solution)/shard_map/ppermute | solution.py:255

commit v2 on v1

v2 whole, which is shorter than its diff:
```python
import functools
import math

import jax
import jax.numpy as jnp
from jax import lax
from jax.experimental import pallas as pl
from jax.experimental.pallas import tpu as pltpu
from jax.sharding import PartitionSpec as P

KV = 8
HD = 128
C = 2
QPK = 4
LANES = 128
BLOCK = 64
F32 = jnp.float32
BF16 = jnp.bfloat16
NEG = -1e30
VMEM = pl.BlockSpec(memory_space=pltpu.VMEM)


def nt(a, b):
    return lax.dot_general(a, b, (((1,), (1,)), ((), ())), preferred_element_type=F32)


def iota(shape, dim):
    return lax.broadcasted_iota(jnp.int32, shape, dim)


def rope_tables(pos_ref):
    tokens = pos_ref.shape[1]
    half = HD // 2
    slots = iota((tokens, HD), 1) % half
    first = half // 4
    second = (half - first) // 2
    eye = (iota((tokens, tokens), 0) == iota((tokens, tokens), 1)).astype(BF16)
    column = [
        nt(eye, jnp.broadcast_to(pos_ref[s : s + 1, :].astype(F32).astype(BF16), (HD, tokens)))
        for s in range(3)
    ]
    chosen = jnp.where(
        slots < first, column[0], jnp.where(slots < first + second, column[1], column[2])
    )
    freq = jnp.exp(-(2.0 * slots.astype(F32) / HD) * math.log(1000000.0))
    angle = chosen * freq
    sign = jnp.where(iota((tokens, HD), 1) < half, -1.0, 1.0)
    return jnp.cos(angle), jnp.sin(angle) * sign


def per_group(table):
    tokens = table.shape[0]
    return jnp.broadcast_to(table[:, None, :], (tokens, KV, HD)).reshape(tokens * KV, HD)


def own_row(dest_ref, tokens):
    start = (lax.axis_index("tile") * lax.axis_size("head") + lax.axis_index("head")) * tokens
    row = dest_ref[pl.ds(start // LANES, 1), :].astype(F32).astype(BF16)
    return row, start % LANES


def own_targets(dest_ref, tokens, rows):
    row, off = own_row(dest_ref, tokens)
    count = tokens * KV
    wide = (iota((count, LANES), 1) == off + iota((count, LANES), 0) // KV).astype(BF16)
    narrow = (iota((tokens, LANES), 1) == off + iota((tokens, LANES), 0)).astype(BF16)
    along = nt(jnp.broadcast_to(row, (8, LANES)), wide)[:1]
    down = nt(narrow, jnp.broadcast_to(row, (rows, LANES)))
    return along, down


def slot_keys(dest_ref, tokens):
    count = tokens * KV
    along, down = own_targets(dest_ref, tokens, count)
    lane = iota((tokens, count), 1)
    earlier = (down == along) & (iota((tokens, count), 0) < lane // KV)
    rank = jnp.sum(earlier.astype(F32), axis=0, keepdims=True)
    return ((along * C + rank) * KV).astype(jnp.int32) + iota((1, count), 1) % KV


def row_keys(shape, dim, tiles, local):
    at = iota(shape, dim)
    slots = tiles * C
    return ((at // local) % slots) * KV + (at // (slots * local)) * local + at % local


def pack_kernel(vis_hbm, pos_hbm, dest_hbm, out_ref, vis_ref, pos_ref, dest_ref, sems, *, tiles, local):
    pairs = ((dest_hbm, dest_ref), (pos_hbm, pos_ref), (vis_hbm, vis_ref))
    loads = [pltpu.make_async_copy(a, b, sems.at[n]) for n, (a, b) in enumerate(pairs)]
    for load in loads:
        load.start()
    count, width = vis_ref.shape
    tokens = count // KV
    total = out_ref.shape[0]
    keys = row_keys((total, count), 0, tiles, local)
    loads[0].wait()
    place = (keys == slot_keys(dest_ref, tokens)).astype(BF16)
    loads[1].wait()
    cosv, sinv = rope_tables(pos_ref)
    cosv, sinv = per_group(cosv), per_group(sinv)
    loads[2].wait()
    for at in range(0, width, HD):
        x = vis_ref[:, at : at + HD]
        if at < (QPK + 1) * HD:
            x = x.astype(F32)
            x = (x * cosv + pltpu.roll(x, HD // 2, 1) * sinv).astype(BF16)
        out_ref[:, at : at + HD] = jnp.dot(place, x, preferred_element_type=F32).astype(BF16)


def side_kernel(
    pos_ref, dest_ref, after_ref, cos_ref, sin_ref, gather_ref, valid_ref, *order_refs, tiles, heads, local
):
    del after_ref
    tokens = pos_ref.shape[1]
    count = tokens * KV
    seq = heads * tiles * C
    total = seq * local
    cosv, sinv = rope_tables(pos_ref)
    cos_ref[...] = per_group(cosv)
    sin_ref[...] = per_group(sinv)
    place = row_keys((total, count), 0, tiles, local) == slot_keys(dest_ref, tokens)
    gather_ref[...] = jnp.transpose(place.astype(F32)).astype(BF16)
    mine = lax.axis_index("tile")
    slot = iota((seq, LANES), 0)
    device = ((slot // C) % tiles) * heads + slot // (tiles * C)

    def tally(block, sums):
        hit = (dest_ref[pl.ds(block, 1), :] == mine).astype(F32).astype(BF16)
        source = (block * LANES + iota((seq, LANES), 1)) // tokens
        return sums + nt((source == device).astype(F32).astype(BF16), jnp.broadcast_to(hit, (LANES, LANES)))

    counts = lax.fori_loop(0, dest_ref.shape[0], tally, jnp.zeros((seq, LANES), F32))
    valid_ref[...] = (counts > (slot % C).astype(F32)).astype(F32)
    if order_refs:
        by_group, by_slot = iota((total, total), 0), iota((total, total), 1)
        order_refs[0][...] = (by_group % seq * local + by_group // seq == by_slot).astype(BF16)
        by_slot, by_group = by_group, by_slot
        order_refs[1][...] = (by_group % seq * local + by_group // seq == by_slot).astype(BF16)


def split_kernel(cot_ref, own_ref, other_ref, *, local):
    head = lax.axis_index("head")
    total, count = own_ref.shape[0], cot_ref.shape[0]
    slots = total // local
    row, lane = iota((total, count), 0), iota((total, count), 1)
    base = (row % slots) * KV + row // slots
    cot = cot_ref[...]
    for ref, group in ((own_ref, head), (other_ref, 1 - head)):
        pick = (lane == base + group * local).astype(BF16)
        ref[...] = jnp.dot(pick, cot, preferred_element_type=F32).astype(BF16)


def join_kernel(valid_ref, *refs, local):
    cot_refs, (out_ref, whole) = refs[:-2], refs[-2:]
    seq = valid_ref.shape[0]
    block = min(BLOCK, seq)
    if len(cot_refs) == 2:
        half = seq // 2
        head = lax.axis_index("head")
        for ref, place in zip(cot_refs, (head, 1 - head)):
            for g in range(local):
                at = pl.multiple_of(g * seq + place * half, half)
                whole[pl.ds(at, half), :] = ref[g * half : (g + 1) * half, :]
    else:
        whole[...] = cot_refs[0][...]
    for first in range(0, seq, block):
        ok = valid_ref[first : first + block, :] > 0.0
        for g in range(local):
            for q in range(QPK):
                part = whole[g * seq + first : g * seq + first + block, q * HD : (q + 1) * HD]
                at = (g * seq + first) * QPK + q * block
                out_ref[at : at + block, :] = jnp.where(ok, part.astype(F32), 0.0).astype(BF16)


def attend_kernel(rows_ref, valid_ref, cot_ref, *refs, local):
    order_refs, (out_ref, rows_at, grads_at, dkey_at, dvalue_at) = refs[:-5], refs[-5:]
    total, width = rows_ref.shape
    seq = total // local
    block = min(BLOCK, seq)
    wide = QPK * block
    qcols = QPK * HD
    scale = HD ** (-0.5)
    if order_refs:
        for at in range(0, width, 2 * HD):
            cols = slice(at, at + 2 * HD)
            rows_at[:, cols] = jnp.dot(
                order_refs[0][...], rows_ref[:, cols], preferred_element_type=F32
            ).astype(BF16)
    else:
        rows_at, grads_at = rows_ref, out_ref
    key_ok = jnp.where(valid_ref[:, :1] > 0.0, 0.0, NEG)

    def step(group, first, bias):
        rows = pl.ds(group * seq + first, block)
        every = slice(group * seq, (group + 1) * seq)
        key = rows_at[every, qcols : qcols + HD]
        value = rows_at[every, qcols + HD :]
        query = jnp.concatenate([rows_at[rows, q * HD : (q + 1) * HD] for q in range(QPK)], 0)
        cot = cot_ref[pl.ds((group * seq + first) * QPK, wide), :]
        score = nt(key, query) * scale + bias
        weight = jnp.exp(score - jnp.max(score, axis=0, keepdims=True))
        probs = (weight * (1.0 / jnp.sum(weight, axis=0, keepdims=True))).astype(BF16)
        dprob = nt(value, cot)
        broad = probs.astype(F32)
        delta = jnp.sum(broad * dprob, axis=0, keepdims=True)
        dscore = (broad * (dprob - delta)).astype(BF16)
        dvalue = jnp.dot(probs, cot, preferred_element_type=F32)
        dkey = jnp.dot(dscore, query, preferred_element_type=F32)
        dquery = lax.dot_general(dscore, key, (((0,), (0,)), ((), ())), preferred_element_type=F32)
        dquery = (dquery * scale).astype(BF16)
        for q in range(QPK):
            grads_at[rows, q * HD : (q + 1) * HD] = dquery[q * block : (q + 1) * block]
        return dkey, dvalue

    def mask(first):
        seen = iota((seq, wide), 0) <= first + iota((seq, wide), 1) % block
        return jnp.where(seen, key_ok, NEG)

    bias = mask(0) if seq == block else None
    for group in range(local):
        every = slice(group * seq, (group + 1) * seq)
        if seq == block:
            dkey, dvalue = step(group, 0, bias)
        else:
            dkey_at[...] = jnp.zeros((seq, HD), F32)
            dvalue_at[...] = jnp.zeros((seq, HD), F32)

            @pl.loop(0, seq // block)
            def _(index):
                first = pl.multiple_of(index * block, block)
                dkey, dvalue = step(group, first, mask(first))
                dkey_at[...] += dkey
                dvalue_at[...] += dvalue

            dkey, dvalue = dkey_at[...], dvalue_at[...]
        grads_at[every, qcols : qcols + HD] = (dkey * scale).astype(BF16)
        grads_at[every, qcols + HD :] = dvalue.astype(BF16)
    if order_refs:
        for at in range(0, width, 2 * HD):
            cols = slice(at, at + 2 * HD)
            out_ref[:, cols] = jnp.dot(
                order_refs[1][...], grads_at[:, cols], preferred_element_type=F32
            ).astype(BF16)


def gather_kernel(rows_ref, gather_ref, cos_ref, sin_ref, out_ref):
    width = rows_ref.shape[1]
    pick = gather_ref[...]
    for at in range(0, width, HD):
        x = jnp.dot(pick, rows_ref[:, at : at + HD], preferred_element_type=F32)
        if at < (QPK + 1) * HD:
            x = x * cos_ref[...] - pltpu.roll(x, HD // 2, 1) * sin_ref[...]
        out_ref[:, at : at + HD] = x.astype(BF16)


def call(kernel, outs, *args, scratch=(), specs=None):
    shapes = [jax.ShapeDtypeStruct(s, d) for s, d in outs]
    single = len(shapes) == 1
    return pl.pallas_call(
        kernel,
        out_shape=shapes[0] if single else shapes,
        in_specs=specs or [VMEM] * len(args),
        out_specs=VMEM if single else [VMEM] * len(shapes),
        scratch_shapes=list(scratch),
        compiler_params=pltpu.CompilerParams(vmem_limit_bytes=48 * 2**20),
    )(*args)


def body(vision_rows, positions, destination, out_grad):
    tiles = lax.axis_size("tile")
    heads = lax.axis_size("head")
    tokens, groups, width = vision_rows.shape
    local = groups // heads
    count = tokens * groups
    seq = heads * tiles * C
    total = seq * local
    qcols = QPK * HD
    targets = destination.reshape(-1, LANES)
    rows = vision_rows.reshape(count, width)
    outgoing = call(
        functools.partial(pack_kernel, tiles=tiles, local=local),
        [((total, width), BF16)],
        *(pltpu.with_memory_space_constraint(x, pltpu.HBM) for x in (rows, positions, targets)),
        specs=[pl.BlockSpec(memory_space=pltpu.HBM)] * 3,
        scratch=(
            pltpu.VMEM(rows.shape, BF16),
            pltpu.VMEM(positions.shape, jnp.int32),
            pltpu.VMEM(targets.shape, jnp.int32),
            pltpu.SemaphoreType.DMA((3,)),
        ),
    )

    def swap(rows):
        parts = rows.reshape(heads * tiles, C * local, width)
        parts = lax.all_to_all(parts, ("head", "tile"), split_axis=0, concat_axis=0, tiled=True)
        return parts.reshape(total, width)

    incoming = swap(outgoing)
    if heads == 2:
        slots = out_grad.shape[0]
        own, other = call(
            functools.partial(split_kernel, local=local),
            [((slots * local, qcols), BF16)] * 2,
            out_grad.reshape(slots * groups, qcols),
        )
        cots = [own, lax.ppermute(other, "head", [(0, 1), (1, 0)])]
    else:
        moved = lax.all_to_all(out_grad, "head", split_axis=1, concat_axis=0, tiled=True)
        cots = [jnp.swapaxes(moved, 0, 1).reshape(total, qcols)]
    cosv, sinv, gather, valid, *orders = call(
        functools.partial(side_kernel, tiles=tiles, heads=heads, local=local),
        [
            ((count, HD), F32),
            ((count, HD), F32),
            ((count, total), BF16),
            ((seq, LANES), F32),
        ]
        + [((total, total), BF16)] * (2 if local > 1 else 0),
        positions,
        targets,
        outgoing[:16, :LANES],
    )
    cot = call(
        functools.partial(join_kernel, local=local),
        [((total * QPK, HD), BF16)],
        valid,
        *cots,
        scratch=(pltpu.VMEM((total, qcols), BF16),),
    )
    grads = call(
        functools.partial(attend_kernel, local=local),
        [((total, width), BF16)],
        incoming,
        valid,
        cot,
        *orders,
        scratch=(
            pltpu.VMEM((total, width), BF16),
            pltpu.VMEM((total, width), BF16),
            pltpu.VMEM((seq, HD), F32),
            pltpu.VMEM((seq, HD), F32),
        ),
    )
    result = call(gather_kernel, [((count, width), BF16)], swap(grads), gather, cosv, sinv)
    return result.reshape(tokens, groups, width)


def solution(mesh):
    return jax.shard_map(
        body,
        mesh=mesh,
        in_specs=(
            P(("tile", "head"), None, None),
            P(None, ("tile", "head")),
            P(),
            P(("tile", "head"), None, None),
        ),
        out_specs=P(("tile", "head"), None, None),
        check_vma=False,
    )
```

time: 42.2 us -> 40.8 us (0.967)
  local copies, waits for them, and re-layouts: 2.97 us -> 0.69 us
  Pallas kernels: 5.36 us -> 6.18 us
    unnamed x10 -> x6, local copies, waits for them, and re-layouts: 2.3 us -> 0.02 us
    pallas_call x5 -> x6, Pallas kernels: 5.36 us -> 6.18 us  [call(): pl.pallas_call(kernel, out_shape=shapes[0] if single else shapes, in_spec...]
where the time goes in v2:
time: 40.8 us; the launch traced here: 40.5 us
  blocking collectives  15.2 us (37%)
  waiting for transfers between devices  9.18 us (22%)
  starting transfers between devices  9.14 us (22%)
  Pallas kernels  6.18 us (15%)
  local copies, waits for them, and re-layouts  0.69 us (2%)
    all_to_all x1, blocking collectives, swap(): lax.all_to_all(parts, ('head', 'tile'), split_axis=0, concat_axis=0, tile...  15.2 us
    all_to_all x1, starting transfers between devices, swap(): lax.all_to_all(parts, ('head', 'tile'), split_axis=0, concat_axis=0, tile...  7.31 us
    pallas_call x6, Pallas kernels, call(): pl.pallas_call(kernel, out_shape=shapes[0] if single else shapes, in_spec...  6.18 us
    ppermute x1, waiting for transfers between devices, body(): cots = [own, lax.ppermute(other, 'head', [(0, 1), (1, 0)])]  4.99 us
    all_to_all x1, waiting for transfers between devices, swap(): lax.all_to_all(parts, ('head', 'tile'), split_axis=0, concat_axis=0, tile...  4.18 us
    ppermute x1, starting transfers between devices, body(): cots = [own, lax.ppermute(other, 'head', [(0, 1), (1, 0)])]  1.83 us
  transfers between devices with their start and end apart: 2, of which 2 were waited for; matrix products, arithmetic and copies ran while one was open for 2% of the time, Pallas kernels for 3%

profile of v2, /device:TPU:0, one launch (start us, length us, event | category | flops | bytes accessed | tf_op | source)
XLA Modules:
  0.0 40.5 jit_solution(15473325741474338251)
XLA Ops:
  0.0 2.2 %shard_map.46 = bf16[256,768]{1,0:T(8,128)(2,1)} custom-call(bf16[128,768]{1,0:T(8,128)(2,1)} %bitcast.14, s32[3,16]{1,0:T(4,128)} %pos_ref.1, s32[4,128]{1,0:T(4,128)} %bitcast.12), custom_call_target="tpu_custom_call" | custom-call | tf_op jit(solution)/shard_map/pallas_call | solution.py:259
  2.2 0.0 copy-start
  2.2 7.3 %all-to-all-start = ((bf16[32,8,768]{2,1,0:T(8,128)(2,1)}), bf16[32,8,768]{2,1,0:T(8,128)(2,1)S(1)}, u32[]{:S(2)}, u32[]{:S(2)}) async-start(bf16[32,8,768]{2,1,0:T(8,128)(2,1)} %bitcast.2), calls=%async_computation | async-start | bytes 786432 | tf_op jit(solution)/shard_map/all_to_all | solution.py:295
  9.6 0.0 copy-done
  9.6 0.2 shard_map.48
  9.8 0.0 copy-start.1
  9.8 0.0 copy-start.2
  9.8 1.8 %collective-permute-start = (bf16[128,512]{1,0:T(8,128)(2,1)S(1)}, bf16[128,512]{1,0:T(8,128)(2,1)S(1)}, u32[]{:S(2)}, u32[]{:S(2)}) collective-permute-start(bf16[128,512]{1,0:T(8,128)(2,1)S(1)} %get-tuple-element.15), channel_id=1, source_target_pairs={{0,1},{1,0},{2,3},{3,2},{4,5},{5,4},{6,7},{7,6},{8,9},{9,8},{10,11... | collective-permute-start | bytes 393224 | tf_op jit(solution)/shard_map/ppermute | solution.py:306
  11.7 0.7 %slice.4.after_ref = bf16[16,128]{1,0:T(8,128)(2,1)S(1)} slice(bf16[256,768]{1,0:T(8,128)(2,1)} %shard_map.46), slice={[0:16], [0:128]} | slice | bytes 8192 | tf_op jit(solution)/shard_map/slice | solution.py:321
  12.3 0.0 copy-done.1
  12.3 0.0 copy-done.2
  12.3 1.0 %shard_map.47 = (f32[128,128]{1,0:T(8,128)S(1)}, f32[128,128]{1,0:T(8,128)S(1)}, bf16[128,256]{1,0:T(8,128)(2,1)S(1)}, f32[64,128]{1,0:T(8,128)S(1)}, bf16[256,2...) custom-call(s32[3,16]{1,0:T(4,128)S(1)} %copy-done.1, s32[4,128]{1,0:T(4,128)S(1)} %bitcast.13, ...), custom_call_target="tpu_custom_call" | custom-call | tf_op jit(solution)/shard_map/pallas_call | solution.py:259
  13.4 5.0 %collective-permute-done.refs_1_ = bf16[128,512]{1,0:T(8,128)(2,1)S(1)} collective-permute-done((bf16[128,512]{1,0:T(8,128)(2,1)S(1)}, bf16[128,512]{1,0:T(8,128)(2,1)S(1)}, u32[]{:S(2)}, u32[]{:S(2)}) %collective-permute-start) | collective-permute-done | bytes 131104 | tf_op jit(solution)/shard_map/ppermute | solution.py:306
  18.4 0.1 shard_map.49.cot_ref
  18.5 4.2 %all-to-all-done = bf16[32,8,768]{2,1,0:T(8,128)(2,1)S(1)} async-done(((bf16[32,8,768]{2,1,0:T(8,128)(2,1)}), bf16[32,8,768]{2,1,0:T(8,128)(2,1)S(1)}, u32[]{:S(2)}, u32[]{:S(2)}) %all-to-all-start) | async-done | bytes 393248 | tf_op jit(solution)/shard_map/all_to_all | solution.py:295
  22.6 1.6 %shard_map.50 = bf16[256,768]{1,0:T(8,128)(2,1)S(1)} custom-call(bf16[256,768]{1,0:T(8,128)(2,1)S(1)} %bitcast.9, f32[64,128]{1,0:T(8,128)S(1)} %get-tuple-element.13.valid_ref, bf16[1024,128]{1,0:T(8,128)(2,1)S(1)} %shard_map.49.cot_ref, bf16[256,256]{1,0:T(8,128)(2,1)S(1)} %get-tuple-element.16.refs_0_, bf16[256,256]{1,0:T(8,128)(2,1)S(1)} %get-tuple-element.17.refs_1_), custom_call_target="tpu_custom_call" | custom-call | tf_op jit(solution)/shard_map/pallas_call | solution.py:259
  24.3 15.2 %all_to_all.10 = bf16[32,8,768]{2,1,0:T(8,128)(2,1)S(1)} all-to-all(bf16[32,8,768]{2,1,0:T(8,128)(2,1)S(1)} %bitcast.10), channel_id=1, replica_groups=mesh['tile'=16,'head'=2] {'head','tile'}, dimensions={0} | all-to-all | bytes 786432 | tf_op jit(solution)/shard_map/all_to_all | solution.py:295
  39.5 1.0 %shard_map.51 = bf16[128,768]{1,0:T(8,128)(2,1)} custom-call(bf16[256,768]{1,0:T(8,128)(2,1)S(1)} %bitcast.8, bf16[128,256]{1,0:T(8,128)(2,1)S(1)} %get-tuple-element.18.gather_ref, f32[128,128]{1,0:T(8,128)S(1)} %get-tuple-element.19.cos_ref, f32[128,128]{1,0:T(8,128)S(1)} %get-tuple-element.20.sin_ref), custom_call_target="tpu_custom_call" | custom-call | tf_op jit(solution)/shard_map/pallas_call | solution.py:259
Async XLA Ops:
  2.2 7.3 %copy-start = (bf16[32,8,512]{2,1,0:T(8,128)(2,1)S(1)}, bf16[32,8,512]{2,1,0:T(8,128)(2,1)}, u32[]{:S(2)}) copy-start(bf16[32,8,512]{2,1,0:T(8,128)(2,1)} %param.7) | copy-start | bytes 786436
  2.2 20.4 %all-to-all-start = ((bf16[32,8,768]{2,1,0:T(8,128)(2,1)}), bf16[32,8,768]{2,1,0:T(8,128)(2,1)S(1)}, u32[]{:S(2)}, u32[]{:S(2)}) async-start(bf16[32,8,768]{2,1,0:T(8,128)(2,1)} %bitcast.2), calls=%async_computation | async-start | bytes 786432 | tf_op jit(solution)/shard_map/all_to_all | solution.py:295
  9.8 2.5 %copy-start.1 = (s32[3,16]{1,0:T(4,128)S(1)}, s32[3,16]{1,0:T(4,128)}, u32[]{:S(2)}) copy-start(s32[3,16]{1,0:T(4,128)} %pos_ref.1) | copy-start | bytes 580
  9.8 2.5 %copy-start.2 = (s32[512,1]{0,1:T(1,128)S(1)}, s32[512,1]{0,1:T(1,128)}, u32[]{:S(2)}) copy-start(s32[512,1]{0,1:T(1,128)} %param.6) | copy-start | bytes 6148
  9.8 8.6 %collective-permute-start = (bf16[128,512]{1,0:T(8,128)(2,1)S(1)}, bf16[128,512]{1,0:T(8,128)(2,1)S(1)}, u32[]{:S(2)}, u32[]{:S(2)}) collective-permute-start(bf16[128,512]{1,0:T(8,128)(2,1)S(1)} %get-tuple-element.15), channel_id=1, source_target_pairs={{0,1},{1,0},{2,3},{3,2},{4,5},{5,4},{6,7},{7,6},{8,9},{9,8},{10,11... | collective-permute-start | bytes 393224 | tf_op jit(solution)/shard_map/ppermute | solution.py:306

commit v3 on v2

v3 whole, which is shorter than its diff:
```python
import functools
import math

import jax
import jax.numpy as jnp
from jax import lax
from jax.experimental import pallas as pl
from jax.experimental.pallas import tpu as pltpu
from jax.sharding import PartitionSpec as P

KV = 8
HD = 128
C = 2
QPK = 4
LANES = 128
BLOCK = 64
PIECES = 2
F32 = jnp.float32
BF16 = jnp.bfloat16
NEG = -1e30
VMEM = pl.BlockSpec(memory_space=pltpu.VMEM)
HBM = pl.BlockSpec(memory_space=pltpu.HBM)


def nt(a, b):
    return lax.dot_general(a, b, (((1,), (1,)), ((), ())), preferred_element_type=F32)


def iota(shape, dim):
    return lax.broadcasted_iota(jnp.int32, shape, dim)


def rope_tables(pos_ref):
    tokens = pos_ref.shape[1]
    half = HD // 2
    slots = iota((tokens, HD), 1) % half
    first = half // 4
    second = (half - first) // 2
    eye = (iota((tokens, tokens), 0) == iota((tokens, tokens), 1)).astype(BF16)
    column = [
        nt(eye, jnp.broadcast_to(pos_ref[s : s + 1, :].astype(F32).astype(BF16), (HD, tokens)))
        for s in range(3)
    ]
    chosen = jnp.where(
        slots < first, column[0], jnp.where(slots < first + second, column[1], column[2])
    )
    freq = jnp.exp(-(2.0 * slots.astype(F32) / HD) * math.log(1000000.0))
    angle = chosen * freq
    sign = jnp.where(iota((tokens, HD), 1) < half, -1.0, 1.0)
    return jnp.cos(angle), jnp.sin(angle) * sign


def per_group(table):
    tokens = table.shape[0]
    return jnp.broadcast_to(table[:, None, :], (tokens, KV, HD)).reshape(tokens * KV, HD)


def token_slots(dest_ref, tokens, tile):
    start = (tile * lax.axis_size("head") + lax.axis_index("head")) * tokens
    count = tokens * KV
    off = start % LANES
    row = dest_ref[pl.ds(start // LANES, 1), :].astype(F32).astype(BF16)
    wide = (iota((count, LANES), 1) == off + iota((count, LANES), 0) // KV).astype(BF16)
    narrow = (iota((tokens, LANES), 1) == off + iota((tokens, LANES), 0)).astype(BF16)
    along = nt(jnp.broadcast_to(row, (8, LANES)), wide)[:1]
    down = nt(narrow, jnp.broadcast_to(row, (count, LANES)))
    lane = iota((tokens, count), 1)
    earlier = (down == along) & (iota((tokens, count), 0) < lane // KV)
    rank = jnp.sum(earlier.astype(F32), axis=0, keepdims=True)
    return (along * C + rank).astype(jnp.int32)


def row_parts(at, tiles, local, sides):
    group, at = at % local, at // local
    rank, at = at % C, at // C
    side, at = at % sides, at // sides
    units = tiles // sides
    order = unit_order(units, sides)
    place, head = at % units, at // units
    unit = place
    if order != list(range(units)):
        unit = sum(jnp.where(place == n, order[n], 0) for n in range(units))
    return head, unit, side, rank, group


def unit_order(units, sides):
    if sides == 2 and units == 8:
        return [z * 2 + y for y in (0, 1) for z in (2, 1, 0, 3)]
    return list(range(units))


def placement(dest_ref, tokens, tiles, local, sides, total):
    count = tokens * KV
    tile = lax.axis_index("tile")
    side = tile % sides
    head, unit, at_side, rank, group = row_parts(iota((total, LANES), 0), tiles, local, sides)
    target = unit * sides + side
    rows = (((target * C + rank) * sides + at_side) * KV + head * local + group)[:, :1]
    parts = []
    for other in range(sides):
        from_side = side + other - 2 * side * other
        slots = token_slots(dest_ref, tokens, tile - side + from_side)
        lanes = (slots * sides + from_side) * KV + iota((1, count), 1) % KV
        parts.append((rows == lanes).astype(F32))
    return parts[0] if sides == 1 else jnp.concatenate(parts, 1)


def ready_kernel(
    vis_hbm, pos_hbm, dest_hbm, rows_ref, place_ref, vis_ref, pos_ref, dest_ref, sems, *, tiles, local, sides
):
    pairs = ((dest_hbm, dest_ref), (pos_hbm, pos_ref), (vis_hbm, vis_ref))
    loads = [pltpu.make_async_copy(a, b, sems.at[n]) for n, (a, b) in enumerate(pairs)]
    for load in loads:
        load.start()
    tokens = pos_ref.shape[1]
    loads[0].wait()
    place_ref[...] = placement(dest_ref, tokens, tiles, local, sides, place_ref.shape[0]).astype(BF16)
    loads[1].wait()
    cosv, sinv = rope_tables(pos_ref)
    loads[2].wait()
    turn(vis_ref, rows_ref, per_group(cosv), per_group(sinv))


def turn(from_ref, to_ref, cosv, sinv):
    for at in range(0, from_ref.shape[1], HD):
        x = from_ref[:, at : at + HD]
        if at < (QPK + 1) * HD:
            x = x.astype(F32)
            x = (x * cosv + pltpu.roll(x, HD // 2, 1) * sinv).astype(BF16)
        to_ref[:, at : at + HD] = x


def pack_kernel(rows_ref, place_ref, *refs):
    others, (out_hbm, both_ref, out_ref, out_sems) = refs[:-4], refs[-4:]
    count = rows_ref.shape[0]
    if others:
        vis_ref, pos_ref = others
        both_ref[:count, :] = rows_ref[...]
        cosv, sinv = rope_tables(pos_ref)
        turn(vis_ref, both_ref.at[count:, :], per_group(cosv), per_group(sinv))
    else:
        both_ref = rows_ref
    stores = Stores(out_ref, out_hbm, out_sems)
    for at in stores.pieces():
        out_ref[at, :] = jnp.dot(place_ref[at, :], both_ref[...], preferred_element_type=F32).astype(BF16)
        stores.start(at)
    stores.wait()


class Stores:
    def __init__(self, source, target, sems):
        self.source, self.target, self.sems, self.copies = source, target, sems, []

    def pieces(self):
        size = self.source.shape[0] // PIECES
        return [slice(n * size, (n + 1) * size) for n in range(PIECES)]

    def start(self, at):
        sem = self.sems.at[len(self.copies)]
        copy = pltpu.make_async_copy(self.source.at[at, :], self.target.at[at, :], sem)
        copy.start()
        self.copies.append(copy)

    def wait(self):
        for copy in self.copies:
            copy.wait()


def side_kernel(
    pos_ref, dest_ref, after_ref, cos_ref, sin_ref, gather_ref, valid_ref, *order_refs, tiles, heads, local, sides
):
    del after_ref
    tokens = pos_ref.shape[1]
    seq = heads * tiles * C
    total = seq * local
    cosv, sinv = rope_tables(pos_ref)
    cos_ref[...] = per_group(cosv)
    sin_ref[...] = per_group(sinv)
    place = placement(dest_ref, tokens, tiles, local, sides, total)
    gather_ref[...] = jnp.transpose(place).astype(BF16)
    mine = lax.axis_index("tile")
    slot = iota((seq, LANES), 0)
    device = ((slot // C) % tiles) * heads + slot // (tiles * C)

    def tally(block, sums):
        hit = (dest_ref[pl.ds(block, 1), :] == mine).astype(F32).astype(BF16)
        source = (block * LANES + iota((seq, LANES), 1)) // tokens
        return sums + nt((source == device).astype(F32).astype(BF16), jnp.broadcast_to(hit, (LANES, LANES)))

    counts = lax.fori_loop(0, dest_ref.shape[0], tally, jnp.zeros((seq, LANES), F32))
    valid_ref[...] = (counts > (slot % C).astype(F32)).astype(F32)
    if order_refs:
        for ref, dim in zip(order_refs, (1, 0)):
            at = iota((total, total), dim)
            head, unit, side, rank, group = row_parts(at, tiles, local, sides)
            by_group = group * seq + (head * tiles + unit * sides + side) * C + rank
            ref[...] = (by_group == iota((total, total), 1 - dim)).astype(BF16)


def split_kernel(cot_ref, own_ref, other_ref, *, local):
    head = lax.axis_index("head")
    total, count = own_ref.shape[0], cot_ref.shape[0]
    slots = total // local
    row, lane = iota((total, count), 0), iota((total, count), 1)
    base = (row % slots) * KV + row // slots
    cot = cot_ref[...]
    for ref, group in ((own_ref, head), (other_ref, 1 - head)):
        pick = (lane == base + group * local).astype(BF16)
        ref[...] = jnp.dot(pick, cot, preferred_element_type=F32).astype(BF16)


def join_kernel(valid_ref, *refs, local):
    cot_refs, (out_ref, whole) = refs[:-2], refs[-2:]
    seq = valid_ref.shape[0]
    block = min(BLOCK, seq)
    if len(cot_refs) == 2:
        half = seq // 2
        head = lax.axis_index("head")
        for ref, place in zip(cot_refs, (head, 1 - head)):
            for g in range(local):
                at = pl.multiple_of(g * seq + place * half, half)
                whole[pl.ds(at, half), :] = ref[g * half : (g + 1) * half, :]
    else:
        whole[...] = cot_refs[0][...]
    for first in range(0, seq, block):
        ok = valid_ref[first : first + block, :] > 0.0
        for g in range(local):
            for q in range(QPK):
                part = whole[g * seq + first : g * seq + first + block, q * HD : (q + 1) * HD]
                at = (g * seq + first) * QPK + q * block
                out_ref[at : at + block, :] = jnp.where(ok, part.astype(F32), 0.0).astype(BF16)


def attend_kernel(rows_ref, valid_ref, cot_ref, *refs, local):
    order_refs, (out_ref, rows_at, grads_at, sums_at) = refs[:-4], refs[-4:]
    total, width = rows_ref.shape
    seq = total // local
    block = min(BLOCK, seq)
    wide = QPK * block
    qcols = QPK * HD
    scale = HD ** (-0.5)
    if order_refs:
        for at in range(0, width, 2 * HD):
            cols = slice(at, at + 2 * HD)
            rows_at[:, cols] = jnp.dot(
                order_refs[0][...], rows_ref[:, cols], preferred_element_type=F32
            ).astype(BF16)
    else:
        rows_at, grads_at = rows_ref, out_ref
    key_ok = jnp.where(valid_ref[:, :1] > 0.0, 0.0, NEG)

    every = [slice(group * seq, (group + 1) * seq) for group in range(local)]

    def step(first):
        seen = iota((seq, wide), 0) <= first + iota((seq, wide), 1) % block
        bias = jnp.where(seen, key_ok, NEG)
        rows = [pl.ds(group * seq + first, block) for group in range(local)]
        keys = [rows_at[at, qcols : qcols + HD] for at in every]
        values = [rows_at[at, qcols + HD :] for at in every]
        queries = [
            jnp.concatenate([rows_at[at, q * HD : (q + 1) * HD] for q in range(QPK)], 0) for at in rows
        ]
        cots = [cot_ref[pl.ds((group * seq + first) * QPK, wide), :] for group in range(local)]
        scores = [nt(key, query) * scale + bias for key, query in zip(keys, queries)]
        dprobs = [nt(value, cot) for value, cot in zip(values, cots)]
        weights = [jnp.exp(x - jnp.max(x, axis=0, keepdims=True)) for x in scores]
        probs = [
            (x * (1.0 / jnp.sum(x, axis=0, keepdims=True))).astype(BF16) for x in weights
        ]
        broad = [x.astype(F32) for x in probs]
        deltas = [jnp.sum(x * y, axis=0, keepdims=True) for x, y in zip(broad, dprobs)]
        dscores = [(x * (y - z)).astype(BF16) for x, y, z in zip(broad, dprobs, deltas)]
        for at, dscore, key in zip(rows, dscores, keys):
            dquery = lax.dot_general(
                dscore, key, (((0,), (0,)), ((), ())), preferred_element_type=F32
            )
            dquery = (dquery * scale).astype(BF16)
            for q in range(QPK):
                grads_at[at, q * HD : (q + 1) * HD] = dquery[q * block : (q + 1) * block]
        dkeys = [jnp.dot(x, y, preferred_element_type=F32) for x, y in zip(dscores, queries)]
        dvalues = [jnp.dot(x, y, preferred_element_type=F32) for x, y in zip(probs, cots)]
        return dkeys, dvalues

    if seq == block:
        dkeys, dvalues = step(0)
    else:
        sums_at[...] = jnp.zeros(sums_at.shape, F32)

        @pl.loop(0, seq // block)
        def _(index):
            dkeys, dvalues = step(pl.multiple_of(index * block, block))
            for group, at in enumerate(every):
                sums_at[at, :HD] += dkeys[group]
                sums_at[at, HD:] += dvalues[group]

        dkeys, dvalues = [sums_at[at, :HD] for at in every], [sums_at[at, HD:] for at in every]
    for at, dkey, dvalue in zip(every, dkeys, dvalues):
        grads_at[at, qcols : qcols + HD] = (dkey * scale).astype(BF16)
        grads_at[at, qcols + HD :] = dvalue.astype(BF16)
    if order_refs:
        for at in range(0, width, 2 * HD):
            cols = slice(at, at + 2 * HD)
            out_ref[:, cols] = jnp.dot(
                order_refs[1][...], grads_at[:, cols], preferred_element_type=F32
            ).astype(BF16)


def gather_kernel(rows_ref, gather_ref, out_ref, *, part):
    count = out_ref.shape[0]
    pick = gather_ref[part * count : (part + 1) * count, :]
    out_ref[...] = jnp.dot(pick, rows_ref[...], preferred_element_type=F32).astype(BF16)


def finish_kernel(cos_ref, sin_ref, *refs):
    parts, (out_hbm, out_ref, out_sems) = refs[:-3], refs[-3:]
    stores = Stores(out_ref, out_hbm, out_sems)
    for at in stores.pieces():
        cosv, sinv = cos_ref[at, :], sin_ref[at, :]
        for first in range(0, out_ref.shape[1], HD):
            cols = slice(first, first + HD)
            x = sum(ref[at, cols].astype(F32) for ref in parts)
            if first < (QPK + 1) * HD:
                x = x * cosv - pltpu.roll(x, HD // 2, 1) * sinv
            out_ref[at, cols] = x.astype(BF16)
        stores.start(at)
    stores.wait()


def call(kernel, outs, *args, scratch=(), specs=None, out_spec=VMEM):
    shapes = [jax.ShapeDtypeStruct(s, d) for s, d in outs]
    single = len(shapes) == 1
    return pl.pallas_call(
        kernel,
        out_shape=shapes[0] if single else shapes,
        in_specs=specs or [VMEM] * len(args),
        out_specs=out_spec if single else [out_spec] * len(shapes),
        scratch_shapes=list(scratch),
        compiler_params=pltpu.CompilerParams(vmem_limit_bytes=48 * 2**20),
    )(*args)


def body(vision_rows, positions, destination, out_grad):
    tiles = lax.axis_size("tile")
    heads = lax.axis_size("head")
    tokens, groups, width = vision_rows.shape
    local = groups // heads
    count = tokens * groups
    seq = heads * tiles * C
    total = seq * local
    qcols = QPK * HD
    sides = 2 if heads == 2 and tiles % 2 == 0 else 1
    targets = destination.reshape(-1, LANES)
    rows = vision_rows.reshape(count, width)
    kernel = functools.partial

    def to_pair(x):
        return lax.ppermute(x, "tile", [(t, t ^ 1) for t in range(tiles)])

    others = [to_pair(rows), to_pair(positions)] if sides == 2 else []
    turned, place = call(
        kernel(ready_kernel, tiles=tiles, local=local, sides=sides),
        [((count, width), BF16), ((total, sides * count), BF16)],
        *(pltpu.with_memory_space_constraint(x, pltpu.HBM) for x in (rows, positions, targets)),
        specs=[HBM] * 3,
        scratch=(
            pltpu.VMEM(rows.shape, BF16),
            pltpu.VMEM(positions.shape, jnp.int32),
            pltpu.VMEM(targets.shape, jnp.int32),
            pltpu.SemaphoreType.DMA((3,)),
        ),
    )
    outgoing = call(
        pack_kernel,
        [((total, width), BF16)],
        turned,
        place,
        *others,
        out_spec=HBM,
        scratch=(
            pltpu.VMEM((sides * count, width), BF16),
            pltpu.VMEM((total, width), BF16),
            pltpu.SemaphoreType.DMA((PIECES,)),
        ),
    )

    def swap(rows):
        units = tiles // sides
        parts = rows.reshape(heads * units, -1, width)
        if sides == 1:
            axes, groups = ("head", "tile"), None
        else:
            axes, order = ("tile", "head"), unit_order(units, sides)
            groups = [
                [(unit * sides + side) * heads + head for head in range(heads) for unit in order]
                for side in range(sides)
            ]
        parts = lax.all_to_all(
            parts, axes, split_axis=0, concat_axis=0, tiled=True, axis_index_groups=groups
        )
        return parts.reshape(total, width)

    incoming = swap(outgoing)
    if heads == 2:
        slots = out_grad.shape[0]
        own, other = call(
            kernel(split_kernel, local=local),
            [((slots * local, qcols), BF16)] * 2,
            out_grad.reshape(slots * groups, qcols),
        )
        cots = [own, lax.ppermute(other, "head", [(0, 1), (1, 0)])]
    else:
        moved = lax.all_to_all(out_grad, "head", split_axis=1, concat_axis=0, tiled=True)
        cots = [jnp.swapaxes(moved, 0, 1).reshape(total, qcols)]
    cosv, sinv, gather, valid, *orders = call(
        kernel(side_kernel, tiles=tiles, heads=heads, local=local, sides=sides),
        [
            ((count, HD), F32),
            ((count, HD), F32),
            ((sides * count, total), BF16),
            ((seq, LANES), F32),
        ]
        + [((total, total), BF16)] * (2 if local * sides > 1 else 0),
        positions,
        targets,
        outgoing[:16, :LANES],
    )
    cot = call(
        kernel(join_kernel, local=local),
        [((total * QPK, HD), BF16)],
        valid,
        *cots,
        scratch=(pltpu.VMEM((total, qcols), BF16),),
    )
    grads = call(
        kernel(attend_kernel, local=local),
        [((total, width), BF16)],
        incoming,
        valid,
        cot,
        *orders,
        scratch=(
            pltpu.VMEM((total, width), BF16),
            pltpu.VMEM((total, width), BF16),
            pltpu.VMEM((total, 2 * HD) if seq > BLOCK else (8, 2 * HD), F32),
        ),
    )
    back = swap(grads)

    def gathered(part):
        return call(kernel(gather_kernel, part=part), [((count, width), BF16)], back, gather)

    parts = [to_pair(gathered(1))] if sides == 2 else []
    parts.append(gathered(0))
    result = call(
        finish_kernel,
        [((count, width), BF16)],
        cosv,
        sinv,
        *parts,
        out_spec=HBM,
        scratch=(pltpu.VMEM((count, width), BF16), pltpu.SemaphoreType.DMA((PIECES,))),
    )
    return result.reshape(tokens, groups, width)


def solution(mesh):
    return jax.shard_map(
        body,
        mesh=mesh,
        in_specs=(
            P(("tile", "head"), None, None),
            P(None, ("tile", "head")),
            P(),
            P(("tile", "head"), None, None),
        ),
        out_specs=P(("tile", "head"), None, None),
        check_vma=False,
    )
```

time: 40.8 us -> 39.4 us (0.966)
  waiting for transfers between devices: 9.18 us -> 6.54 us
  starting transfers between devices: 9.14 us -> 11 us
  blocking collectives: 15.2 us -> 14.1 us
  Pallas kernels: 6.18 us -> 6.65 us
    all_to_all x1, waiting for transfers between devices: 4.18 us -> 0.15 us  [swap(): lax.all_to_all(parts, axes, split_axis=0, concat_axis=0, tiled=True, axis...]
    all_to_all x1, starting transfers between devices: 7.31 us -> 8.93 us  [swap(): lax.all_to_all(parts, axes, split_axis=0, concat_axis=0, tiled=True, axis...]
    ppermute x0 -> x3, waiting for transfers between devices: none -> 1.21 us  [to_pair(): return lax.ppermute(x, 'tile', [(t, t ^ 1) for t in range(tiles)])]
    all_to_all x1, blocking collectives: 15.2 us -> 14.1 us  [swap(): lax.all_to_all(parts, axes, split_axis=0, concat_axis=0, tiled=True, axis...]
    ppermute x0 -> x3, starting transfers between devices: none -> 0.58 us  [to_pair(): return lax.ppermute(x, 'tile', [(t, t ^ 1) for t in range(tiles)])]
    pallas_call x6 -> x9, Pallas kernels: 6.18 us -> 6.65 us  [call(): pl.pallas_call(kernel, out_shape=shapes[0] if single else shapes, in_spec...]
  transfers between devices with their start and end apart: 2 -> 5, of which waited for: 2 -> 3; matrix products, arithmetic and copies ran while one was open for 2% -> 2% of each run, Pallas kernels for 3% -> 8%
where the time goes in v3:
time: 39.4 us; the launch traced here: 39.1 us
  blocking collectives  14.1 us (36%)
  starting transfers between devices  11 us (28%)
  Pallas kernels  6.65 us (17%)
  waiting for transfers between devices  6.54 us (17%)
  local copies, waits for them, and re-layouts  0.69 us (2%)
    all_to_all x1, blocking collectives, swap(): lax.all_to_all(parts, axes, split_axis=0, concat_axis=0, tiled=True, axis...  14.1 us
    all_to_all x1, starting transfers between devices, swap(): lax.all_to_all(parts, axes, split_axis=0, concat_axis=0, tiled=True, axis...  8.93 us
    pallas_call x9, Pallas kernels, call(): pl.pallas_call(kernel, out_shape=shapes[0] if single else shapes, in_spec...  6.65 us
    ppermute x1, waiting for transfers between devices, body(): cots = [own, lax.ppermute(other, 'head', [(0, 1), (1, 0)])]  5.18 us
    ppermute x1, starting transfers between devices, body(): cots = [own, lax.ppermute(other, 'head', [(0, 1), (1, 0)])]  1.53 us
    ppermute x3, waiting for transfers between devices, to_pair(): return lax.ppermute(x, 'tile', [(t, t ^ 1) for t in range(tiles)])  1.21 us
  transfers between devices with their start and end apart: 5, of which 3 were waited for; matrix products, arithmetic and copies ran while one was open for 2% of the time, Pallas kernels for 8%

profile of v3, /device:TPU:0, one launch (start us, length us, event | category | flops | bytes accessed | tf_op | source)
XLA Modules:
  0.0 39.1 jit_solution(695307447739118031)
XLA Ops:
  0.0 0.5 %collective-permute-start = (bf16[128,768]{1,0:T(8,128)(2,1)}, bf16[128,768]{1,0:T(8,128)(2,1)S(1)}, u32[]{:S(2)}, u32[]{:S(2)}) collective-permute-start(bf16[128,768]{1,0:T(8,128)(2,1)} %bitcast.15), channel_id=1, source_target_pairs={{0,2},{2,0},{4,6},{6,4},{8,10},{10,8},{12,14},{14,12},{16,18},{18,... | collective-permute-start | bytes 589832 | tf_op jit(solution)/shard_map/ppermute | solution.py:357
  0.5 0.1 collective-permute-start.1
  0.5 1.4 %shard_map.46 = (bf16[128,768]{1,0:T(8,128)(2,1)S(1)}, bf16[256,256]{1,0:T(8,128)(2,1)S(1)}) custom-call(bf16[128,768]{1,0:T(8,128)(2,1)} %bitcast.16, s32[3,16]{1,0:T(4,128)} %pos_ref.1, s32[4,128]{1,0:T(4,128)} %bitcast.13), custom_call_target="tpu_custom_call" | custom-call | tf_op jit(solution)/shard_map/pallas_call | solution.py:332
  1.9 0.0 collective-permute-done.1.refs_1_
  2.0 0.0 collective-permute-done.refs_0_
  2.0 1.3 %shard_map.47 = bf16[256,768]{1,0:T(8,128)(2,1)} custom-call(bf16[128,768]{1,0:T(8,128)(2,1)S(1)} %get-tuple-element.15.rows_ref, bf16[256,256]{1,0:T(8,128)(2,1)S(1)} %get-tuple-element.16.place_ref, bf16[128,768]{1,0:T(8,128)(2,1)S(1)} %collective-permute-done.refs_0_, s32[3,16]{1,0:T(4,128)S(1)} %collective-permute-done.1.refs_1_), custom_call_target="tpu_custom_call" | custom-call | tf_op jit(solution)/shard_map/pallas_call | solution.py:332
  3.2 0.0 copy-start
  3.3 8.9 %all-to-all-start = ((bf16[16,16,768]{2,1,0:T(8,128)(2,1)}), bf16[16,16,768]{2,1,0:T(8,128)(2,1)S(1)}, u32[]{:S(2)}, u32[]{:S(2)}) async-start(bf16[16,16,768]{2,1,0:T(8,128)(2,1)} %bitcast.2), calls=%async_computation | async-start | bytes 786432 | tf_op jit(solution)/shard_map/all_to_all | solution.py:397
  12.2 0.0 copy-done
  12.2 0.2 shard_map.49
  12.4 0.0 copy-start.1
  12.4 0.0 copy-start.2
  12.4 1.5 %collective-permute-start.2 = (bf16[128,512]{1,0:T(8,128)(2,1)S(1)}, bf16[128,512]{1,0:T(8,128)(2,1)S(1)}, u32[]{:S(2)}, u32[]{:S(2)}) collective-permute-start(bf16[128,512]{1,0:T(8,128)(2,1)S(1)} %get-tuple-element.21), channel_id=1, source_target_pairs={{0,1},{1,0},{2,3},{3,2},{4,5},{5,4},{6,7},{7,6},{8,9},{9,8},{10,11... | collective-permute-start | bytes 393224 | tf_op jit(solution)/shard_map/ppermute | solution.py:410
  14.0 0.7 %slice.4.after_ref = bf16[16,128]{1,0:T(8,128)(2,1)S(1)} slice(bf16[256,768]{1,0:T(8,128)(2,1)} %shard_map.47), slice={[0:16], [0:128]} | slice | bytes 8192 | tf_op jit(solution)/shard_map/slice | solution.py:425
  14.7 0.0 copy-done.1
  14.7 0.0 copy-done.2
  14.7 1.3 %shard_map.48 = (f32[128,128]{1,0:T(8,128)S(1)}, f32[128,128]{1,0:T(8,128)S(1)}, bf16[256,256]{1,0:T(8,128)(2,1)S(1)}, f32[64,128]{1,0:T(8,128)S(1)}, bf16[256,2...) custom-call(s32[3,16]{1,0:T(4,128)S(1)} %copy-done.1, s32[4,128]{1,0:T(4,128)S(1)} %bitcast.14, ...), custom_call_target="tpu_custom_call" | custom-call | tf_op jit(solution)/shard_map/pallas_call | solution.py:332
  16.0 5.2 %collective-permute-done.2.refs_1_ = bf16[128,512]{1,0:T(8,128)(2,1)S(1)} collective-permute-done((bf16[128,512]{1,0:T(8,128)(2,1)S(1)}, bf16[128,512]{1,0:T(8,128)(2,1)S(1)}, u32[]{:S(2)}, u32[]{:S(2)}) %collective-permute-start.2) | collective-permute-done | bytes 131104 | tf_op jit(solution)/shard_map/ppermute | solution.py:410
  21.2 0.1 shard_map.50.cot_ref
  21.2 0.2 all-to-all-done
  21.4 1.1 %shard_map.51 = bf16[256,768]{1,0:T(8,128)(2,1)S(1)} custom-call(bf16[256,768]{1,0:T(8,128)(2,1)S(1)} %bitcast.10, f32[64,128]{1,0:T(8,128)S(1)} %get-tuple-element.19.valid_ref, bf16[1024,128]{1,0:T(8,128)(2,1)S(1)} %shard_map.50.cot_ref, bf16[256,256]{1,0:T(8,128)(2,1)S(1)} %get-tuple-element.22.refs_0_, bf16[256,256]{1,0:T(8,128)(2,1)S(1)} %get-tuple-element.23.refs_1_), custom_call_target="tpu_custom_call" | custom-call | tf_op jit(solution)/shard_map/pallas_call | solution.py:332
  22.5 14.1 %all_to_all.10 = bf16[16,16,768]{2,1,0:T(8,128)(2,1)S(1)} all-to-all(bf16[16,16,768]{2,1,0:T(8,128)(2,1)S(1)} %bitcast.11), channel_id=1, replica_groups={{16,8,0,24,20,12,4,28,17,9,1,25,21,13,5,29},{18,10,2,26,22,14,6,30,19,1..., dimensions={0} | all-to-all | bytes 786432 | tf_op jit(solution)/shard_map/all_to_all | solution.py:397
  36.6 0.2 shard_map.52
  36.8 0.1 collective-permute-start.3
  36.9 0.2 shard_map.53.refs_1_
  37.1 1.2 %collective-permute-done.3.refs_0_ = bf16[128,768]{1,0:T(8,128)(2,1)S(1)} collective-permute-done((bf16[128,768]{1,0:T(8,128)(2,1)S(1)}, bf16[128,768]{1,0:T(8,128)(2,1)S(1)}, u32[]{:S(2)}, u32[]{:S(2)}) %collective-permute-start.3) | collective-permute-done | bytes 196640 | tf_op jit(solution)/shard_map/ppermute | solution.py:357
  38.3 0.8 %shard_map.54 = bf16[128,768]{1,0:T(8,128)(2,1)} custom-call(f32[128,128]{1,0:T(8,128)S(1)} %get-tuple-element.17.cos_ref, f32[128,128]{1,0:T(8,128)S(1)} %get-tuple-element.18.sin_ref, bf16[128,768]{1,0:T(8,128)(2,1)S(1)} %collective-permute-done.3.refs_0_, bf16[128,768]{1,0:T(8,128)(2,1)S(1)} %shard_map.53.refs_1_), custom_call_target="tpu_custom_call" | custom-call | tf_op jit(solution)/shard_map/pallas_call | solution.py:332
Async XLA Ops:
  0.0 2.0 %collective-permute-start = (bf16[128,768]{1,0:T(8,128)(2,1)}, bf16[128,768]{1,0:T(8,128)(2,1)S(1)}, u32[]{:S(2)}, u32[]{:S(2)}) collective-permute-start(bf16[128,768]{1,0:T(8,128)(2,1)} %bitcast.15), channel_id=1, source_target_pairs={{0,2},{2,0},{4,6},{6,4},{8,10},{10,8},{12,14},{14,12},{16,18},{18,... | collective-permute-start | bytes 589832 | tf_op jit(solution)/shard_map/ppermute | solution.py:357
  0.5 1.5 %collective-permute-start.1 = (s32[3,16]{1,0:T(4,128)}, s32[3,16]{1,0:T(4,128)S(1)}, u32[]{:S(2)}, u32[]{:S(2)}) collective-permute-start(s32[3,16]{1,0:T(4,128)} %pos_ref.1), channel_id=1, source_target_pairs={{0,2},{2,0},{4,6},{6,4},{8,10},{10,8},{12,14},{14,12},{16,18},{18,... | collective-permute-start | bytes 584 | tf_op jit(solution)/shard_map/ppermute | solution.py:357
  3.2 8.9 %copy-start = (bf16[32,8,512]{2,1,0:T(8,128)(2,1)S(1)}, bf16[32,8,512]{2,1,0:T(8,128)(2,1)}, u32[]{:S(2)}) copy-start(bf16[32,8,512]{2,1,0:T(8,128)(2,1)} %param.7) | copy-start | bytes 786436
  3.3 18.1 %all-to-all-start = ((bf16[16,16,768]{2,1,0:T(8,128)(2,1)}), bf16[16,16,768]{2,1,0:T(8,128)(2,1)S(1)}, u32[]{:S(2)}, u32[]{:S(2)}) async-start(bf16[16,16,768]{2,1,0:T(8,128)(2,1)} %bitcast.2), calls=%async_computation | async-start | bytes 786432 | tf_op jit(solution)/shard_map/all_to_all | solution.py:397
  12.4 2.2 %copy-start.1 = (s32[3,16]{1,0:T(4,128)S(1)}, s32[3,16]{1,0:T(4,128)}, u32[]{:S(2)}) copy-start(s32[3,16]{1,0:T(4,128)} %pos_ref.1) | copy-start | bytes 580
  12.4 2.2 %copy-start.2 = (s32[512,1]{0,1:T(1,128)S(1)}, s32[512,1]{0,1:T(1,128)}, u32[]{:S(2)}) copy-start(s32[512,1]{0,1:T(1,128)} %param.6) | copy-start | bytes 6148
  12.4 8.7 %collective-permute-start.2 = (bf16[128,512]{1,0:T(8,128)(2,1)S(1)}, bf16[128,512]{1,0:T(8,128)(2,1)S(1)}, u32[]{:S(2)}, u32[]{:S(2)}) collective-permute-start(bf16[128,512]{1,0:T(8,128)(2,1)S(1)} %get-tuple-element.21), channel_id=1, source_target_pairs={{0,1},{1,0},{2,3},{3,2},{4,5},{5,4},{6,7},{7,6},{8,9},{9,8},{10,11... | collective-permute-start | bytes 393224 | tf_op jit(solution)/shard_map/ppermute | solution.py:410
  36.8 1.5 %collective-permute-start.3 = (bf16[128,768]{1,0:T(8,128)(2,1)S(1)}, bf16[128,768]{1,0:T(8,128)(2,1)S(1)}, u32[]{:S(2)}, u32[]{:S(2)}) collective-permute-start(bf16[128,768]{1,0:T(8,128)(2,1)S(1)} %shard_map.52), channel_id=1, source_target_pairs={{0,2},{2,0},{4,6},{6,4},{8,10},{10,8},{12,14},{14,12},{16,18},{18,... | collective-permute-start | bytes 589832 | tf_op jit(solution)/shard_map/ppermute | solution.py:357

commit v4 on v3

--- a/solution.py
+++ b/solution.py
@@ -130,7 +130,8 @@
         to_ref[:, at : at + HD] = x
 
 
-def pack_kernel(rows_ref, place_ref, *refs):
+def pack_kernel(rows_ref, place_ref, after_ref, *refs):
+    del after_ref
     others, (out_hbm, both_ref, out_ref, out_sems) = refs[:-4], refs[-4:]
     count = rows_ref.shape[0]
     if others:
@@ -166,10 +167,8 @@
             copy.wait()
 
 
-def side_kernel(
-    pos_ref, dest_ref, after_ref, cos_ref, sin_ref, gather_ref, valid_ref, *order_refs, tiles, heads, local, sides
-):
-    del after_ref
+def fill_tables(pos_ref, dest_ref, table_refs, tiles, heads, local, sides):
+    cos_ref, sin_ref, gather_ref, valid_ref, *order_refs = table_refs
     tokens = pos_ref.shape[1]
     seq = heads * tiles * C
     total = seq * local
@@ -197,7 +196,7 @@
             ref[...] = (by_group == iota((total, total), 1 - dim)).astype(BF16)
 
 
-def split_kernel(cot_ref, own_ref, other_ref, *, local):
+def split_cots(cot_ref, own_ref, other_ref, local):
     head = lax.axis_index("head")
     total, count = own_ref.shape[0], cot_ref.shape[0]
     slots = total // local
@@ -207,6 +206,53 @@
     for ref, group in ((own_ref, head), (other_ref, 1 - head)):
         pick = (lane == base + group * local).astype(BF16)
         ref[...] = jnp.dot(pick, cot, preferred_element_type=F32).astype(BF16)
+
+
+def is_late(sides):
+    return lax.axis_index("tile") % sides == 0
+
+
+def early_kernel(cot_hbm, pos_hbm, dest_hbm, *refs, tiles, heads, local, sides):
+    *out_refs, cot_ref, pos_ref, dest_ref, sems = refs
+
+    @pl.when(is_late(sides))
+    def _():
+        pairs = ((dest_hbm, dest_ref), (pos_hbm, pos_ref), (cot_hbm, cot_ref))
+        loads = [pltpu.make_async_copy(a, b, sems.at[n]) for n, (a, b) in enumerate(pairs)]
+        for load in loads:
+            load.start()
+        for load in loads:
+            load.wait()
+        split_cots(cot_ref, *out_refs[:2], local)
+        fill_tables(pos_ref, dest_ref, out_refs[2:], tiles, heads, local, sides)
+
+
+def table_kernel(pos_ref, dest_ref, after_ref, *refs, tiles, heads, local, sides):
+    del after_ref
+    if sides == 1:
+        fill_tables(pos_ref, dest_ref, refs, tiles, heads, local, sides)
+        return
+    early_refs, out_refs = refs[: len(refs) // 2], refs[len(refs) // 2 :]
+
+    @pl.when(is_late(sides))
+    def _():
+        for from_ref, to_ref in zip(early_refs, out_refs):
+            to_ref[...] = from_ref[...]
+
+    @pl.when(jnp.logical_not(is_late(sides)))
+    def _():
+        fill_tables(pos_ref, dest_ref, out_refs, tiles, heads, local, sides)
+
+
+def split_kernel(cot_ref, own_early, other_early, own_ref, other_ref, *, local, sides):
+    @pl.when(is_late(sides))
+    def _():
+        own_ref[...] = own_early[...]
+        other_ref[...] = other_early[...]
+
+    @pl.when(jnp.logical_not(is_late(sides)))
+    def _():
+        split_cots(cot_ref, own_ref, other_ref, local)
 
 
 def join_kernel(valid_ref, *refs, local):
@@ -369,11 +415,35 @@
             pltpu.SemaphoreType.DMA((3,)),
         ),
     )
+    slots = out_grad.shape[0]
+    cot_rows = out_grad.reshape(slots * groups, qcols)
+    split_outs = [((slots * local, qcols), BF16)] * 2
+    table_outs = [
+        ((count, HD), F32),
+        ((count, HD), F32),
+        ((sides * count, total), BF16),
+        ((seq, LANES), F32),
+    ] + [((total, total), BF16)] * (2 if local * sides > 1 else 0)
+    early = []
+    if sides == 2:
+        early = call(
+            kernel(early_kernel, tiles=tiles, heads=heads, local=local, sides=sides),
+            split_outs + table_outs,
+            *(pltpu.with_memory_space_constraint(x, pltpu.HBM) for x in (cot_rows, positions, targets)),
+            specs=[HBM] * 3,
+            scratch=(
+                pltpu.VMEM(cot_rows.shape, BF16),
+                pltpu.VMEM(positions.shape, jnp.int32),
+                pltpu.VMEM(targets.shape, jnp.int32),
+                pltpu.SemaphoreType.DMA((3,)),
+            ),
+        )
     outgoing = call(
         pack_kernel,
         [((total, width), BF16)],
         turned,
         place,
+        early[0][:16, :LANES] if early else place[:16, :LANES],
         *others,
         out_spec=HBM,
         scratch=(
@@ -400,29 +470,19 @@
         return parts.reshape(total, width)
 
     incoming = swap(outgoing)
-    if heads == 2:
-        slots = out_grad.shape[0]
-        own, other = call(
-            kernel(split_kernel, local=local),
-            [((slots * local, qcols), BF16)] * 2,
-            out_grad.reshape(slots * groups, qcols),
-        )
+    if sides == 2:
+        own, other = call(kernel(split_kernel, local=local, sides=sides), split_outs, cot_rows, *early[:2])
         cots = [own, lax.ppermute(other, "head", [(0, 1), (1, 0)])]
     else:
         moved = lax.all_to_all(out_grad, "head", split_axis=1, concat_axis=0, tiled=True)
         cots = [jnp.swapaxes(moved, 0, 1).reshape(total, qcols)]
     cosv, sinv, gather, valid, *orders = call(
-        kernel(side_kernel, tiles=tiles, heads=heads, local=local, sides=sides),
-        [
-            ((count, HD), F32),
-            ((count, HD), F32),
-            ((sides * count, total), BF16),
-            ((seq, LANES), F32),
-        ]
-        + [((total, total), BF16)] * (2 if local * sides > 1 else 0),
+        kernel(table_kernel, tiles=tiles, heads=heads, local=local, sides=sides),
+        table_outs,
         positions,
         targets,
         outgoing[:16, :LANES],
+        *early[2:],
     )
     cot = call(
         kernel(join_kernel, local=local),

time: 39.4 us -> 38.1 us (0.967)
  waiting for transfers between devices: 6.54 us -> 4.96 us
  blocking collectives: 14.1 us -> 12.7 us
  Pallas kernels: 6.65 us -> 7.6 us
  local copies, waits for them, and re-layouts: 0.69 us -> 1.38 us
    ppermute x1, waiting for transfers between devices: 5.18 us -> 3.72 us  [body(): cots = [own, lax.ppermute(other, 'head', [(0, 1), (1, 0)])]]
    all_to_all x1, blocking collectives: 14.1 us -> 12.7 us  [swap(): lax.all_to_all(parts, axes, split_axis=0, concat_axis=0, tiled=True, axis...]
    pallas_call x9 -> x10, Pallas kernels: 6.65 us -> 7.6 us  [call(): pl.pallas_call(kernel, out_shape=shapes[0] if single else shapes, in_spec...]
    unnamed x6, local copies, waits for them, and re-layouts: 0.02 us -> 0.7 us
  transfers between devices with their start and end apart: 5 -> 5, of which waited for: 3 -> 2; matrix products, arithmetic and copies ran while one was open for 2% -> 2% of each run, Pallas kernels for 8% -> 11%
where the time goes in v4:
time: 38.1 us; the launch traced here: 37.8 us
  blocking collectives  12.7 us (33%)
  starting transfers between devices  11 us (29%)
  Pallas kernels  7.6 us (20%)
  waiting for transfers between devices  4.96 us (13%)
  local copies, waits for them, and re-layouts  1.38 us (4%)
    all_to_all x1, blocking collectives, swap(): lax.all_to_all(parts, axes, split_axis=0, concat_axis=0, tiled=True, axis...  12.7 us
    all_to_all x1, starting transfers between devices, swap(): lax.all_to_all(parts, axes, split_axis=0, concat_axis=0, tiled=True, axis...  8.93 us
    pallas_call x10, Pallas kernels, call(): pl.pallas_call(kernel, out_shape=shapes[0] if single else shapes, in_spec...  7.6 us
    ppermute x1, waiting for transfers between devices, body(): cots = [own, lax.ppermute(other, 'head', [(0, 1), (1, 0)])]  3.72 us
    ppermute x1, starting transfers between devices, body(): cots = [own, lax.ppermute(other, 'head', [(0, 1), (1, 0)])]  1.53 us
    ppermute x3, waiting for transfers between devices, to_pair(): return lax.ppermute(x, 'tile', [(t, t ^ 1) for t in range(tiles)])  1.21 us
  transfers between devices with their start and end apart: 5, of which 2 were waited for; matrix products, arithmetic and copies ran while one was open for 2% of the time, Pallas kernels for 11%

profile of v4, /device:TPU:0, one launch (start us, length us, event | category | flops | bytes accessed | tf_op | source)
XLA Modules:
  0.0 37.8 jit_solution(5984612300986604226)
XLA Ops:
  0.0 0.5 %collective-permute-start = (bf16[128,768]{1,0:T(8,128)(2,1)}, bf16[128,768]{1,0:T(8,128)(2,1)S(1)}, u32[]{:S(2)}, u32[]{:S(2)}) collective-permute-start(bf16[128,768]{1,0:T(8,128)(2,1)} %bitcast.17), channel_id=1, source_target_pairs={{0,2},{2,0},{4,6},{6,4},{8,10},{10,8},{12,14},{14,12},{16,18},{18,... | collective-permute-start | bytes 589832 | tf_op jit(solution)/shard_map/ppermute | solution.py:403
  0.5 0.1 collective-permute-start.1
  0.5 1.4 %shard_map.46 = (bf16[128,768]{1,0:T(8,128)(2,1)S(1)}, bf16[256,256]{1,0:T(8,128)(2,1)S(1)}) custom-call(bf16[128,768]{1,0:T(8,128)(2,1)} %bitcast.18, s32[3,16]{1,0:T(4,128)} %pos_ref.1, s32[4,128]{1,0:T(4,128)} %bitcast.14), custom_call_target="tpu_custom_call" | custom-call | tf_op jit(solution)/shard_map/pallas_call | solution.py:378
  1.9 2.4 %shard_map.47 = (bf16[128,512]{1,0:T(8,128)(2,1)S(1)}, bf16[128,512]{1,0:T(8,128)(2,1)S(1)}, f32[128,128]{1,0:T(8,128)S(1)}, f32[128,128]{1,0:T(8,128)S(1)}, bf1...) custom-call(bf16[256,512]{1,0:T(8,128)(2,1)} %bitcast.12, ...), custom_call_target="tpu_custom_call" | custom-call | tf_op jit(solution)/shard_map/pallas_call | solution.py:378
  4.4 0.0 collective-permute-done.1.refs_1_
  4.4 0.0 collective-permute-done.refs_0_
  4.4 1.3 %shard_map.48 = bf16[256,768]{1,0:T(8,128)(2,1)} custom-call(bf16[128,768]{1,0:T(8,128)(2,1)S(1)} %get-tuple-element.23.rows_ref, bf16[256,256]{1,0:T(8,128)(2,1)S(1)} %get-tuple-element.24.place_ref, bf16[16,128]{1,0:T(8,128)(2,1)S(1)} %slice.6.after_ref, bf16[128,768]{1,0:T(8,128)(2,1)S(1)} %collective-permute-done.refs_0_, ...), custom_call_target="tpu_custom_call" | custom-call | tf_op jit(solution)/shard_map/pallas_call | solution.py:378
  5.7 0.0 copy-start
  5.7 8.9 %all-to-all-start = ((bf16[16,16,768]{2,1,0:T(8,128)(2,1)}), bf16[16,16,768]{2,1,0:T(8,128)(2,1)S(1)}, u32[]{:S(2)}, u32[]{:S(2)}) async-start(bf16[16,16,768]{2,1,0:T(8,128)(2,1)} %bitcast.3), calls=%async_computation | async-start | bytes 786432 | tf_op jit(solution)/shard_map/all_to_all | solution.py:467
  14.6 0.0 copy-done
  14.7 1.5 %collective-permute-start.2 = (bf16[128,512]{1,0:T(8,128)(2,1)S(1)}, bf16[128,512]{1,0:T(8,128)(2,1)S(1)}, u32[]{:S(2)}, u32[]{:S(2)}) collective-permute-start(bf16[128,512]{1,0:T(8,128)(2,1)S(1)} %get-tuple-element.37), channel_id=1, source_target_pairs={{0,1},{1,0},{2,3},{3,2},{4,5},{5,4},{6,7},{7,6},{8,9},{9,8},{10,11... | collective-permute-start | bytes 393224 | tf_op jit(solution)/shard_map/ppermute | solution.py:475
  16.2 0.7 %slice.8.after_ref = bf16[16,128]{1,0:T(8,128)(2,1)S(1)} slice(bf16[256,768]{1,0:T(8,128)(2,1)} %shard_map.48), slice={[0:16], [0:128]} | slice | bytes 8192 | tf_op jit(solution)/shard_map/slice | solution.py:484
  16.9 0.0 copy-start.2
  16.9 0.0 copy-start.1
  16.9 0.7 %copy-done.2 = s32[512,1]{0,1:T(1,128)S(1)} copy-done((s32[512,1]{0,1:T(1,128)S(1)}, s32[512,1]{0,1:T(1,128)}, u32[]{:S(2)}) %copy-start.2) | copy-done | bytes 2072
  17.6 0.0 copy-done.1
  17.6 3.7 %collective-permute-done.2.refs_1_ = bf16[128,512]{1,0:T(8,128)(2,1)S(1)} collective-permute-done((bf16[128,512]{1,0:T(8,128)(2,1)S(1)}, bf16[128,512]{1,0:T(8,128)(2,1)S(1)}, u32[]{:S(2)}, u32[]{:S(2)}) %collective-permute-start.2) | collective-permute-done | bytes 131104 | tf_op jit(solution)/shard_map/ppermute | solution.py:475
  21.3 0.1 shard_map.51.cot_ref
  21.4 0.0 all-to-all-done
  21.5 1.1 %shard_map.52 = bf16[256,768]{1,0:T(8,128)(2,1)S(1)} custom-call(bf16[256,768]{1,0:T(8,128)(2,1)S(1)} %bitcast.10, f32[64,128]{1,0:T(8,128)S(1)} %get-tuple-element.34.valid_ref, bf16[1024,128]{1,0:T(8,128)(2,1)S(1)} %shard_map.51.cot_ref, bf16[256,256]{1,0:T(8,128)(2,1)S(1)} %get-tuple-element.38.refs_0_, bf16[256,256]{1,0:T(8,128)(2,1)S(1)} %get-tuple-element.39.refs_1_), custom_call_target="tpu_custom_call" | custom-call | tf_op jit(solution)/shard_map/pallas_call | solution.py:378
  22.6 12.7 %all_to_all.10 = bf16[16,16,768]{2,1,0:T(8,128)(2,1)S(1)} all-to-all(bf16[16,16,768]{2,1,0:T(8,128)(2,1)S(1)} %bitcast.11), channel_id=1, replica_groups={{16,8,0,24,20,12,4,28,17,9,1,25,21,13,5,29},{18,10,2,26,22,14,6,30,19,1..., dimensions={0} | all-to-all | bytes 786432 | tf_op jit(solution)/shard_map/all_to_all | solution.py:467
  35.2 0.2 shard_map.53
  35.5 0.1 collective-permute-start.3
  35.5 0.2 shard_map.54.refs_1_
  35.8 1.2 %collective-permute-done.3.refs_0_ = bf16[128,768]{1,0:T(8,128)(2,1)S(1)} collective-permute-done((bf16[128,768]{1,0:T(8,128)(2,1)S(1)}, bf16[128,768]{1,0:T(8,128)(2,1)S(1)}, u32[]{:S(2)}, u32[]{:S(2)}) %collective-permute-start.3) | collective-permute-done | bytes 196640 | tf_op jit(solution)/shard_map/ppermute | solution.py:403
  37.0 0.8 %shard_map.55 = bf16[128,768]{1,0:T(8,128)(2,1)} custom-call(f32[128,128]{1,0:T(8,128)S(1)} %get-tuple-element.32.cos_ref, f32[128,128]{1,0:T(8,128)S(1)} %get-tuple-element.33.sin_ref, bf16[128,768]{1,0:T(8,128)(2,1)S(1)} %collective-permute-done.3.refs_0_, bf16[128,768]{1,0:T(8,128)(2,1)S(1)} %shard_map.54.refs_1_), custom_call_target="tpu_custom_call" | custom-call | tf_op jit(solution)/shard_map/pallas_call | solution.py:378
  (3 shorter events, 0.1 us)
Async XLA Ops:
  0.0 4.4 %collective-permute-start = (bf16[128,768]{1,0:T(8,128)(2,1)}, bf16[128,768]{1,0:T(8,128)(2,1)S(1)}, u32[]{:S(2)}, u32[]{:S(2)}) collective-permute-start(bf16[128,768]{1,0:T(8,128)(2,1)} %bitcast.17), channel_id=1, source_target_pairs={{0,2},{2,0},{4,6},{6,4},{8,10},{10,8},{12,14},{14,12},{16,18},{18,... | collective-permute-start | bytes 589832 | tf_op jit(solution)/shard_map/ppermute | solution.py:403
  0.5 3.9 %collective-permute-start.1 = (s32[3,16]{1,0:T(4,128)}, s32[3,16]{1,0:T(4,128)S(1)}, u32[]{:S(2)}, u32[]{:S(2)}) collective-permute-start(s32[3,16]{1,0:T(4,128)} %pos_ref.1), channel_id=1, source_target_pairs={{0,2},{2,0},{4,6},{6,4},{8,10},{10,8},{12,14},{14,12},{16,18},{18,... | collective-permute-start | bytes 584 | tf_op jit(solution)/shard_map/ppermute | solution.py:403
  5.7 8.9 %copy-start = (bf16[32,8,512]{2,1,0:T(8,128)(2,1)S(1)}, bf16[32,8,512]{2,1,0:T(8,128)(2,1)}, u32[]{:S(2)}) copy-start(bf16[32,8,512]{2,1,0:T(8,128)(2,1)} %param.7) | copy-start | bytes 786436
  5.7 15.8 %all-to-all-start = ((bf16[16,16,768]{2,1,0:T(8,128)(2,1)}), bf16[16,16,768]{2,1,0:T(8,128)(2,1)S(1)}, u32[]{:S(2)}, u32[]{:S(2)}) async-start(bf16[16,16,768]{2,1,0:T(8,128)(2,1)} %bitcast.3), calls=%async_computation | async-start | bytes 786432 | tf_op jit(solution)/shard_map/all_to_all | solution.py:467
  14.7 6.7 %collective-permute-start.2 = (bf16[128,512]{1,0:T(8,128)(2,1)S(1)}, bf16[128,512]{1,0:T(8,128)(2,1)S(1)}, u32[]{:S(2)}, u32[]{:S(2)}) collective-permute-start(bf16[128,512]{1,0:T(8,128)(2,1)S(1)} %get-tuple-element.37), channel_id=1, source_target_pairs={{0,1},{1,0},{2,3},{3,2},{4,5},{5,4},{6,7},{7,6},{8,9},{9,8},{10,11... | collective-permute-start | bytes 393224 | tf_op jit(solution)/shard_map/ppermute | solution.py:475
  16.9 0.7 %copy-start.2 = (s32[512,1]{0,1:T(1,128)S(1)}, s32[512,1]{0,1:T(1,128)}, u32[]{:S(2)}) copy-start(s32[512,1]{0,1:T(1,128)} %param.6) | copy-start | bytes 6148
  16.9 0.7 %copy-start.1 = (s32[3,16]{1,0:T(4,128)S(1)}, s32[3,16]{1,0:T(4,128)}, u32[]{:S(2)}) copy-start(s32[3,16]{1,0:T(4,128)} %pos_ref.1) | copy-start | bytes 580
  35.5 1.5 %collective-permute-start.3 = (bf16[128,768]{1,0:T(8,128)(2,1)S(1)}, bf16[128,768]{1,0:T(8,128)(2,1)S(1)}, u32[]{:S(2)}, u32[]{:S(2)}) collective-permute-start(bf16[128,768]{1,0:T(8,128)(2,1)S(1)} %shard_map.53), channel_id=1, source_target_pairs={{0,2},{2,0},{4,6},{6,4},{8,10},{10,8},{12,14},{14,12},{16,18},{18,... | collective-permute-start | bytes 589832 | tf_op jit(solution)/shard_map/ppermute | solution.py:403

commit v5 on v4

--- a/solution.py
+++ b/solution.py
@@ -30,10 +30,20 @@
     return lax.broadcasted_iota(jnp.int32, shape, dim)
 
 
+def over(at, size):
+    if size & (size - 1):
+        return at // size
+    return lax.shift_right_logical(at, jnp.int32(size.bit_length() - 1))
+
+
+def rest(at, size):
+    return at % size if size & (size - 1) else at & (size - 1)
+
+
 def rope_tables(pos_ref):
     tokens = pos_ref.shape[1]
     half = HD // 2
-    slots = iota((tokens, HD), 1) % half
+    slots = rest(iota((tokens, HD), 1), half)
     first = half // 4
     second = (half - first) // 2
     eye = (iota((tokens, tokens), 0) == iota((tokens, tokens), 1)).astype(BF16)
@@ -60,23 +70,23 @@
     count = tokens * KV
     off = start % LANES
     row = dest_ref[pl.ds(start // LANES, 1), :].astype(F32).astype(BF16)
-    wide = (iota((count, LANES), 1) == off + iota((count, LANES), 0) // KV).astype(BF16)
+    wide = (iota((count, LANES), 1) == off + over(iota((count, LANES), 0), KV)).astype(BF16)
     narrow = (iota((tokens, LANES), 1) == off + iota((tokens, LANES), 0)).astype(BF16)
     along = nt(jnp.broadcast_to(row, (8, LANES)), wide)[:1]
     down = nt(narrow, jnp.broadcast_to(row, (count, LANES)))
     lane = iota((tokens, count), 1)
-    earlier = (down == along) & (iota((tokens, count), 0) < lane // KV)
+    earlier = (down == along) & (iota((tokens, count), 0) < over(lane, KV))
     rank = jnp.sum(earlier.astype(F32), axis=0, keepdims=True)
     return (along * C + rank).astype(jnp.int32)
 
 
 def row_parts(at, tiles, local, sides):
-    group, at = at % local, at // local
-    rank, at = at % C, at // C
-    side, at = at % sides, at // sides
+    rank, at = rest(at, C), over(at, C)
+    side, at = rest(at, sides), over(at, sides)
+    group, at = rest(at, local), over(at, local)
     units = tiles // sides
     order = unit_order(units, sides)
-    place, head = at % units, at // units
+    place, head = rest(at, units), over(at, units)
     unit = place
     if order != list(range(units)):
         unit = sum(jnp.where(place == n, order[n], 0) for n in range(units))
@@ -100,7 +110,7 @@
     for other in range(sides):
         from_side = side + other - 2 * side * other
         slots = token_slots(dest_ref, tokens, tile - side + from_side)
-        lanes = (slots * sides + from_side) * KV + iota((1, count), 1) % KV
+        lanes = (slots * sides + from_side) * KV + rest(iota((1, count), 1), KV)
         parts.append((rows == lanes).astype(F32))
     return parts[0] if sides == 1 else jnp.concatenate(parts, 1)
 
@@ -168,32 +178,37 @@
 
 
 def fill_tables(pos_ref, dest_ref, table_refs, tiles, heads, local, sides):
-    cos_ref, sin_ref, gather_ref, valid_ref, *order_refs = table_refs
+    cos_ref, sin_ref, gather_ref, pick_ref, bias_ref = table_refs
     tokens = pos_ref.shape[1]
     seq = heads * tiles * C
-    total = seq * local
     cosv, sinv = rope_tables(pos_ref)
     cos_ref[...] = per_group(cosv)
     sin_ref[...] = per_group(sinv)
-    place = placement(dest_ref, tokens, tiles, local, sides, total)
+    place = placement(dest_ref, tokens, tiles, local, sides, seq * local)
     gather_ref[...] = jnp.transpose(place).astype(BF16)
     mine = lax.axis_index("tile")
-    slot = iota((seq, LANES), 0)
-    device = ((slot // C) % tiles) * heads + slot // (tiles * C)
+
+    def slot_of(at):
+        head, unit, side, rank, _ = row_parts(at, tiles, 1, sides)
+        return (head * tiles + unit * sides + side) * C + rank
+
+    slot = slot_of(iota((seq, LANES), 0))
+    device = rest(over(slot, C), tiles) * heads + over(slot, tiles * C)
 
     def tally(block, sums):
         hit = (dest_ref[pl.ds(block, 1), :] == mine).astype(F32).astype(BF16)
-        source = (block * LANES + iota((seq, LANES), 1)) // tokens
+        source = over(block * LANES + iota((seq, LANES), 1), tokens)
         return sums + nt((source == device).astype(F32).astype(BF16), jnp.broadcast_to(hit, (LANES, LANES)))
 
     counts = lax.fori_loop(0, dest_ref.shape[0], tally, jnp.zeros((seq, LANES), F32))
-    valid_ref[...] = (counts > (slot % C).astype(F32)).astype(F32)
-    if order_refs:
-        for ref, dim in zip(order_refs, (1, 0)):
-            at = iota((total, total), dim)
-            head, unit, side, rank, group = row_parts(at, tiles, local, sides)
-            by_group = group * seq + (head * tiles + unit * sides + side) * C + rank
-            ref[...] = (by_group == iota((total, total), 1 - dim)).astype(BF16)
+    taken = counts > rest(slot, C).astype(F32)
+    pick_ref[...] = ((slot[:, :1] == iota((seq, seq), 1)) & taken[:, :1]).astype(F32).astype(BF16)
+    key_ok = jnp.where(taken, 0.0, NEG)
+    if bias_ref.shape[1] == LANES:
+        bias_ref[...] = key_ok
+    else:
+        query = slot_of(rest(iota(bias_ref.shape, 1), seq))
+        bias_ref[...] = jnp.where(slot[:, :1] <= query, key_ok[:, :1], NEG)
 
 
 def split_cots(cot_ref, own_ref, other_ref, local):
@@ -201,7 +216,7 @@
     total, count = own_ref.shape[0], cot_ref.shape[0]
     slots = total // local
     row, lane = iota((total, count), 0), iota((total, count), 1)
-    base = (row % slots) * KV + row // slots
+    base = rest(row, slots) * KV + over(row, slots)
     cot = cot_ref[...]
     for ref, group in ((own_ref, head), (other_ref, 1 - head)):
         pick = (lane == base + group * local).astype(BF16)
@@ -255,9 +270,9 @@
         split_cots(cot_ref, own_ref, other_ref, local)
 
 
-def join_kernel(valid_ref, *refs, local):
+def join_kernel(pick_ref, *refs, local):
     cot_refs, (out_ref, whole) = refs[:-2], refs[-2:]
-    seq = valid_ref.shape[0]
+    seq = pick_ref.shape[0]
     block = min(BLOCK, seq)
     if len(cot_refs) == 2:
         half = seq // 2
@@ -269,86 +284,95 @@
     else:
         whole[...] = cot_refs[0][...]
     for first in range(0, seq, block):
-        ok = valid_ref[first : first + block, :] > 0.0
+        pick = pick_ref[first : first + block, :]
         for g in range(local):
+            rows = whole[g * seq : (g + 1) * seq, :]
+            part = jnp.dot(pick, rows, preferred_element_type=F32).astype(BF16)
             for q in range(QPK):
-                part = whole[g * seq + first : g * seq + first + block, q * HD : (q + 1) * HD]
                 at = (g * seq + first) * QPK + q * block
-                out_ref[at : at + block, :] = jnp.where(ok, part.astype(F32), 0.0).astype(BF16)
-
-
-def attend_kernel(rows_ref, valid_ref, cot_ref, *refs, local):
-    order_refs, (out_ref, rows_at, grads_at, sums_at) = refs[:-4], refs[-4:]
+                out_ref[at : at + block, :] = part[:, q * HD : (q + 1) * HD]
+
+
+def trade_halves(a, b):
+    first = iota(a.shape, 1) < 4
+    return jnp.where(first, a, pltpu.roll(b, 4, 1)), jnp.where(first, pltpu.roll(a, 4, 1), b)
+
+
+def by_group(rows, local):
+    if local == 1:
+        return [rows]
+    total, width = rows.shape
+    tiles = rows.astype(F32).reshape(total // (8 * local), 2, local // 2, 8, width)
+    parts = []
+    for pair in range(local // 2):
+        for x in trade_halves(tiles[:, 0, pair], tiles[:, 1, pair]):
+            parts.append(x.reshape(total // local, width).astype(BF16))
+    return parts
+
+
+def by_place(parts):
+    if len(parts) == 1:
+        return parts[0]
+    rows, width = parts[0].shape
+    tiles = [x.reshape(rows // 8, 8, width) for x in parts]
+    pairs = [trade_halves(tiles[n], tiles[n + 1]) for n in range(0, len(parts), 2)]
+    whole = jnp.stack([jnp.stack([pair[side] for pair in pairs], 1) for side in range(2)], 1)
+    return whole.reshape(rows * len(parts), width)
+
+
+def attend_kernel(rows_ref, bias_ref, cot_ref, out_ref, sums_at, *, local):
     total, width = rows_ref.shape
     seq = total // local
     block = min(BLOCK, seq)
     wide = QPK * block
     qcols = QPK * HD
     scale = HD ** (-0.5)
-    if order_refs:
-        for at in range(0, width, 2 * HD):
-            cols = slice(at, at + 2 * HD)
-            rows_at[:, cols] = jnp.dot(
-                order_refs[0][...], rows_ref[:, cols], preferred_element_type=F32
-            ).astype(BF16)
-    else:
-        rows_at, grads_at = rows_ref, out_ref
-    key_ok = jnp.where(valid_ref[:, :1] > 0.0, 0.0, NEG)
-
-    every = [slice(group * seq, (group + 1) * seq) for group in range(local)]
-
-    def step(first):
-        seen = iota((seq, wide), 0) <= first + iota((seq, wide), 1) % block
-        bias = jnp.where(seen, key_ok, NEG)
-        rows = [pl.ds(group * seq + first, block) for group in range(local)]
-        keys = [rows_at[at, qcols : qcols + HD] for at in every]
-        values = [rows_at[at, qcols + HD :] for at in every]
-        queries = [
-            jnp.concatenate([rows_at[at, q * HD : (q + 1) * HD] for q in range(QPK)], 0) for at in rows
-        ]
+
+    def step(first, arrived, bias):
+        at = slice(0, block) if seq == block else pl.ds(first, block)
+        keys = [x[:, qcols : qcols + HD] for x in arrived]
+        values = [x[:, qcols + HD :] for x in arrived]
+        asked = arrived if seq == block else [rows_ref[at, :]]
+        queries = [jnp.concatenate([x[:, q * HD : (q + 1) * HD] for q in range(QPK)], 0) for x in asked]
         cots = [cot_ref[pl.ds((group * seq + first) * QPK, wide), :] for group in range(local)]
-        scores = [nt(key, query) * scale + bias for key, query in zip(keys, queries)]
+        scores = [nt(key, query) * (scale * math.log2(math.e)) + bias for key, query in zip(keys, queries)]
         dprobs = [nt(value, cot) for value, cot in zip(values, cots)]
-        weights = [jnp.exp(x - jnp.max(x, axis=0, keepdims=True)) for x in scores]
-        probs = [
-            (x * (1.0 / jnp.sum(x, axis=0, keepdims=True))).astype(BF16) for x in weights
-        ]
+        weights = [jnp.exp2(x - jnp.max(x, axis=0, keepdims=True)) for x in scores]
+        probs = [(x * (1.0 / jnp.sum(x, axis=0, keepdims=True))).astype(BF16) for x in weights]
         broad = [x.astype(F32) for x in probs]
         deltas = [jnp.sum(x * y, axis=0, keepdims=True) for x, y in zip(broad, dprobs)]
         dscores = [(x * (y - z)).astype(BF16) for x, y, z in zip(broad, dprobs, deltas)]
-        for at, dscore, key in zip(rows, dscores, keys):
-            dquery = lax.dot_general(
-                dscore, key, (((0,), (0,)), ((), ())), preferred_element_type=F32
-            )
-            dquery = (dquery * scale).astype(BF16)
-            for q in range(QPK):
-                grads_at[at, q * HD : (q + 1) * HD] = dquery[q * block : (q + 1) * block]
+        dqueries = [
+            lax.dot_general(x, y, (((0,), (0,)), ((), ())), preferred_element_type=F32) * scale
+            for x, y in zip(dscores, keys)
+        ]
+        dqueries = [
+            jnp.concatenate([x[q * block : (q + 1) * block] for q in range(QPK)], 1) for x in dqueries
+        ]
         dkeys = [jnp.dot(x, y, preferred_element_type=F32) for x, y in zip(dscores, queries)]
         dvalues = [jnp.dot(x, y, preferred_element_type=F32) for x, y in zip(probs, cots)]
-        return dkeys, dvalues
+        return dqueries, dkeys, dvalues
 
     if seq == block:
-        dkeys, dvalues = step(0)
-    else:
-        sums_at[...] = jnp.zeros(sums_at.shape, F32)
-
-        @pl.loop(0, seq // block)
-        def _(index):
-            dkeys, dvalues = step(pl.multiple_of(index * block, block))
-            for group, at in enumerate(every):
-                sums_at[at, :HD] += dkeys[group]
-                sums_at[at, HD:] += dvalues[group]
-
-        dkeys, dvalues = [sums_at[at, :HD] for at in every], [sums_at[at, HD:] for at in every]
-    for at, dkey, dvalue in zip(every, dkeys, dvalues):
-        grads_at[at, qcols : qcols + HD] = (dkey * scale).astype(BF16)
-        grads_at[at, qcols + HD :] = dvalue.astype(BF16)
-    if order_refs:
-        for at in range(0, width, 2 * HD):
-            cols = slice(at, at + 2 * HD)
-            out_ref[:, cols] = jnp.dot(
-                order_refs[1][...], grads_at[:, cols], preferred_element_type=F32
-            ).astype(BF16)
+        arrived = by_group(rows_ref[...], local)
+        terms = zip(*step(0, arrived, bias_ref[...]))
+        parts = [jnp.concatenate([x, y * scale, z], 1) for x, y, z in terms]
+        out_ref[...] = by_place(parts).astype(BF16)
+        return
+    sums_at[...] = jnp.zeros(sums_at.shape, F32)
+
+    @pl.loop(0, seq // block)
+    def _(index):
+        first = pl.multiple_of(index * block, block)
+        seen = iota((seq, wide), 0) <= first + rest(iota((seq, wide), 1), block)
+        bias = jnp.where(seen, bias_ref[:, :1], NEG)
+        (dquery,), (dkey,), (dvalue,) = step(first, [rows_ref[...]], bias)
+        out_ref[pl.ds(first, block), :qcols] = dquery.astype(BF16)
+        sums_at[:, :HD] += dkey
+        sums_at[:, HD:] += dvalue
+
+    out_ref[:, qcols : qcols + HD] = (sums_at[:, :HD] * scale).astype(BF16)
+    out_ref[:, qcols + HD :] = sums_at[:, HD:].astype(BF16)
 
 
 def gather_kernel(rows_ref, gather_ref, out_ref, *, part):
@@ -422,8 +446,9 @@
         ((count, HD), F32),
         ((count, HD), F32),
         ((sides * count, total), BF16),
-        ((seq, LANES), F32),
-    ] + [((total, total), BF16)] * (2 if local * sides > 1 else 0)
+        ((seq, seq), BF16),
+        ((seq, QPK * BLOCK if sides == 2 and seq == BLOCK else LANES), F32),
+    ]
     early = []
     if sides == 2:
         early = call(
@@ -476,7 +501,7 @@
     else:
         moved = lax.all_to_all(out_grad, "head", split_axis=1, concat_axis=0, tiled=True)
         cots = [jnp.swapaxes(moved, 0, 1).reshape(total, qcols)]
-    cosv, sinv, gather, valid, *orders = call(
+    cosv, sinv, gather, pick, bias = call(
         kernel(table_kernel, tiles=tiles, heads=heads, local=local, sides=sides),
         table_outs,
         positions,
@@ -487,7 +512,7 @@
     cot = call(
         kernel(join_kernel, local=local),
         [((total * QPK, HD), BF16)],
-        valid,
+        pick,
         *cots,
         scratch=(pltpu.VMEM((total, qcols), BF16),),
     )
@@ -495,14 +520,9 @@
         kernel(attend_kernel, local=local),
         [((total, width), BF16)],
         incoming,
-        valid,
+        bias,
         cot,
-        *orders,
-        scratch=(
-            pltpu.VMEM((total, width), BF16),
-            pltpu.VMEM((total, width), BF16),
-            pltpu.VMEM((total, 2 * HD) if seq > BLOCK else (8, 2 * HD), F32),
-        ),
+        scratch=(pltpu.VMEM((seq if seq > BLOCK else 8, 2 * HD), F32),),
     )
     back = swap(grads)
 

time: 38.1 us -> 37.6 us (0.987)
  Pallas kernels: 7.6 us -> 7.09 us
    pallas_call x10, Pallas kernels: 7.6 us -> 7.09 us  [call(): pl.pallas_call(kernel, out_shape=shapes[0] if single else shapes, in_spec...]
where the time goes in v5:
time: 37.6 us; the launch traced here: 37.3 us
  blocking collectives  12.7 us (34%)
  starting transfers between devices  11 us (29%)
  Pallas kernels  7.09 us (19%)
  waiting for transfers between devices  4.94 us (13%)
  local copies, waits for them, and re-layouts  1.38 us (4%)
    all_to_all x1, blocking collectives, swap(): lax.all_to_all(parts, axes, split_axis=0, concat_axis=0, tiled=True, axis...  12.7 us
    all_to_all x1, starting transfers between devices, swap(): lax.all_to_all(parts, axes, split_axis=0, concat_axis=0, tiled=True, axis...  8.93 us
    pallas_call x10, Pallas kernels, call(): pl.pallas_call(kernel, out_shape=shapes[0] if single else shapes, in_spec...  7.09 us
    ppermute x1, waiting for transfers between devices, body(): cots = [own, lax.ppermute(other, 'head', [(0, 1), (1, 0)])]  3.73 us
    ppermute x1, starting transfers between devices, body(): cots = [own, lax.ppermute(other, 'head', [(0, 1), (1, 0)])]  1.53 us
    ppermute x3, waiting for transfers between devices, to_pair(): return lax.ppermute(x, 'tile', [(t, t ^ 1) for t in range(tiles)])  1.21 us
  transfers between devices with their start and end apart: 5, of which 2 were waited for; matrix products, arithmetic and copies ran while one was open for 2% of the time, Pallas kernels for 11%

profile of v5, /device:TPU:0, one launch (start us, length us, event | category | flops | bytes accessed | tf_op | source)
XLA Modules:
  0.0 37.3 jit_solution(9041625353093825315)
XLA Ops:
  0.0 0.5 %collective-permute-start = (bf16[128,768]{1,0:T(8,128)(2,1)}, bf16[128,768]{1,0:T(8,128)(2,1)S(1)}, u32[]{:S(2)}, u32[]{:S(2)}) collective-permute-start(bf16[128,768]{1,0:T(8,128)(2,1)} %bitcast.17), channel_id=1, source_target_pairs={{0,2},{2,0},{4,6},{6,4},{8,10},{10,8},{12,14},{14,12},{16,18},{18,... | collective-permute-start | bytes 589832 | tf_op jit(solution)/shard_map/ppermute | solution.py:427
  0.5 0.1 collective-permute-start.1
  0.5 1.3 %shard_map.46 = (bf16[128,768]{1,0:T(8,128)(2,1)S(1)}, bf16[256,256]{1,0:T(8,128)(2,1)S(1)}) custom-call(bf16[128,768]{1,0:T(8,128)(2,1)} %bitcast.18, s32[3,16]{1,0:T(4,128)} %pos_ref.1, s32[4,128]{1,0:T(4,128)} %bitcast.14), custom_call_target="tpu_custom_call" | custom-call | tf_op jit(solution)/shard_map/pallas_call | solution.py:402
  1.9 2.3 %shard_map.47 = (bf16[128,512]{1,0:T(8,128)(2,1)S(1)}, bf16[128,512]{1,0:T(8,128)(2,1)S(1)}, f32[128,128]{1,0:T(8,128)S(1)}, f32[128,128]{1,0:T(8,128)S(1)}, bf1...) custom-call(bf16[256,512]{1,0:T(8,128)(2,1)} %bitcast.12, s32[3,16]{1,0:T(4,128)} %pos_ref.1, ...), custom_call_target="tpu_custom_call" | custom-call | tf_op jit(solution)/shard_map/pallas_call | solution.py:402
  4.2 0.0 collective-permute-done.1.refs_1_
  4.2 0.0 collective-permute-done.refs_0_
  4.2 1.3 %shard_map.48 = bf16[256,768]{1,0:T(8,128)(2,1)} custom-call(bf16[128,768]{1,0:T(8,128)(2,1)S(1)} %get-tuple-element.21.rows_ref, bf16[256,256]{1,0:T(8,128)(2,1)S(1)} %get-tuple-element.22.place_ref, bf16[16,128]{1,0:T(8,128)(2,1)S(1)} %slice.6.after_ref, bf16[128,768]{1,0:T(8,128)(2,1)S(1)} %collective-permute-done.refs_0_, ...), custom_call_target="tpu_custom_call" | custom-call | tf_op jit(solution)/shard_map/pallas_call | solution.py:402
  5.5 0.0 copy-start
  5.5 8.9 %all-to-all-start = ((bf16[16,16,768]{2,1,0:T(8,128)(2,1)}), bf16[16,16,768]{2,1,0:T(8,128)(2,1)S(1)}, u32[]{:S(2)}, u32[]{:S(2)}) async-start(bf16[16,16,768]{2,1,0:T(8,128)(2,1)} %bitcast.3), calls=%async_computation | async-start | bytes 786432 | tf_op jit(solution)/shard_map/all_to_all | solution.py:492
  14.4 0.0 copy-done
  14.5 1.5 %collective-permute-start.2 = (bf16[128,512]{1,0:T(8,128)(2,1)S(1)}, bf16[128,512]{1,0:T(8,128)(2,1)S(1)}, u32[]{:S(2)}, u32[]{:S(2)}) collective-permute-start(bf16[128,512]{1,0:T(8,128)(2,1)S(1)} %get-tuple-element.35), channel_id=1, source_target_pairs={{0,1},{1,0},{2,3},{3,2},{4,5},{5,4},{6,7},{7,6},{8,9},{9,8},{10,11... | collective-permute-start | bytes 393224 | tf_op jit(solution)/shard_map/ppermute | solution.py:500
  16.0 0.7 %slice.8.after_ref = bf16[16,128]{1,0:T(8,128)(2,1)S(1)} slice(bf16[256,768]{1,0:T(8,128)(2,1)} %shard_map.48), slice={[0:16], [0:128]} | slice | bytes 8192 | tf_op jit(solution)/shard_map/slice | solution.py:509
  16.7 0.0 copy-start.2
  16.7 0.0 copy-start.1
  16.7 0.7 %copy-done.2 = s32[512,1]{0,1:T(1,128)S(1)} copy-done((s32[512,1]{0,1:T(1,128)S(1)}, s32[512,1]{0,1:T(1,128)}, u32[]{:S(2)}) %copy-start.2) | copy-done | bytes 2072
  17.4 0.0 copy-done.1
  17.4 3.7 %collective-permute-done.2.refs_1_ = bf16[128,512]{1,0:T(8,128)(2,1)S(1)} collective-permute-done((bf16[128,512]{1,0:T(8,128)(2,1)S(1)}, bf16[128,512]{1,0:T(8,128)(2,1)S(1)}, u32[]{:S(2)}, u32[]{:S(2)}) %collective-permute-start.2) | collective-permute-done | bytes 131104 | tf_op jit(solution)/shard_map/ppermute | solution.py:500
  21.2 0.2 shard_map.51.cot_ref
  21.4 0.0 all-to-all-done
  21.4 0.6 %shard_map.52 = bf16[256,768]{1,0:T(8,128)(2,1)S(1)} custom-call(bf16[256,768]{1,0:T(8,128)(2,1)S(1)} %bitcast.10, f32[64,256]{1,0:T(8,128)S(1)} %get-tuple-element.31.bias_ref, bf16[1024,128]{1,0:T(8,128)(2,1)S(1)} %shard_map.51.cot_ref), custom_call_target="tpu_custom_call" | custom-call | tf_op jit(solution)/shard_map/pallas_call | solution.py:402
  22.0 12.7 %all_to_all.10 = bf16[16,16,768]{2,1,0:T(8,128)(2,1)S(1)} all-to-all(bf16[16,16,768]{2,1,0:T(8,128)(2,1)S(1)} %bitcast.11), channel_id=1, replica_groups={{16,8,0,24,20,12,4,28,17,9,1,25,21,13,5,29},{18,10,2,26,22,14,6,30,19,1..., dimensions={0} | all-to-all | bytes 786432 | tf_op jit(solution)/shard_map/all_to_all | solution.py:492
  34.7 0.2 shard_map.53
  34.9 0.1 collective-permute-start.3
  35.0 0.2 shard_map.54.refs_1_
  35.2 1.2 %collective-permute-done.3.refs_0_ = bf16[128,768]{1,0:T(8,128)(2,1)S(1)} collective-permute-done((bf16[128,768]{1,0:T(8,128)(2,1)S(1)}, bf16[128,768]{1,0:T(8,128)(2,1)S(1)}, u32[]{:S(2)}, u32[]{:S(2)}) %collective-permute-start.3) | collective-permute-done | bytes 196640 | tf_op jit(solution)/shard_map/ppermute | solution.py:427
  36.4 0.8 %shard_map.55 = bf16[128,768]{1,0:T(8,128)(2,1)} custom-call(f32[128,128]{1,0:T(8,128)S(1)} %get-tuple-element.29.cos_ref, f32[128,128]{1,0:T(8,128)S(1)} %get-tuple-element.30.sin_ref, bf16[128,768]{1,0:T(8,128)(2,1)S(1)} %collective-permute-done.3.refs_0_, bf16[128,768]{1,0:T(8,128)(2,1)S(1)} %shard_map.54.refs_1_), custom_call_target="tpu_custom_call" | custom-call | tf_op jit(solution)/shard_map/pallas_call | solution.py:402
  (3 shorter events, 0.1 us)
Async XLA Ops:
  0.0 4.2 %collective-permute-start = (bf16[128,768]{1,0:T(8,128)(2,1)}, bf16[128,768]{1,0:T(8,128)(2,1)S(1)}, u32[]{:S(2)}, u32[]{:S(2)}) collective-permute-start(bf16[128,768]{1,0:T(8,128)(2,1)} %bitcast.17), channel_id=1, source_target_pairs={{0,2},{2,0},{4,6},{6,4},{8,10},{10,8},{12,14},{14,12},{16,18},{18,... | collective-permute-start | bytes 589832 | tf_op jit(solution)/shard_map/ppermute | solution.py:427
  0.5 3.8 %collective-permute-start.1 = (s32[3,16]{1,0:T(4,128)}, s32[3,16]{1,0:T(4,128)S(1)}, u32[]{:S(2)}, u32[]{:S(2)}) collective-permute-start(s32[3,16]{1,0:T(4,128)} %pos_ref.1), channel_id=1, source_target_pairs={{0,2},{2,0},{4,6},{6,4},{8,10},{10,8},{12,14},{14,12},{16,18},{18,... | collective-permute-start | bytes 584 | tf_op jit(solution)/shard_map/ppermute | solution.py:427
  5.5 8.9 %copy-start = (bf16[32,8,512]{2,1,0:T(8,128)(2,1)S(1)}, bf16[32,8,512]{2,1,0:T(8,128)(2,1)}, u32[]{:S(2)}) copy-start(bf16[32,8,512]{2,1,0:T(8,128)(2,1)} %param.7) | copy-start | bytes 786436
  5.5 15.9 %all-to-all-start = ((bf16[16,16,768]{2,1,0:T(8,128)(2,1)}), bf16[16,16,768]{2,1,0:T(8,128)(2,1)S(1)}, u32[]{:S(2)}, u32[]{:S(2)}) async-start(bf16[16,16,768]{2,1,0:T(8,128)(2,1)} %bitcast.3), calls=%async_computation | async-start | bytes 786432 | tf_op jit(solution)/shard_map/all_to_all | solution.py:492
  14.5 6.7 %collective-permute-start.2 = (bf16[128,512]{1,0:T(8,128)(2,1)S(1)}, bf16[128,512]{1,0:T(8,128)(2,1)S(1)}, u32[]{:S(2)}, u32[]{:S(2)}) collective-permute-start(bf16[128,512]{1,0:T(8,128)(2,1)S(1)} %get-tuple-element.35), channel_id=1, source_target_pairs={{0,1},{1,0},{2,3},{3,2},{4,5},{5,4},{6,7},{7,6},{8,9},{9,8},{10,11... | collective-permute-start | bytes 393224 | tf_op jit(solution)/shard_map/ppermute | solution.py:500
  16.7 0.7 %copy-start.2 = (s32[512,1]{0,1:T(1,128)S(1)}, s32[512,1]{0,1:T(1,128)}, u32[]{:S(2)}) copy-start(s32[512,1]{0,1:T(1,128)} %param.6) | copy-start | bytes 6148
  16.7 0.7 %copy-start.1 = (s32[3,16]{1,0:T(4,128)S(1)}, s32[3,16]{1,0:T(4,128)}, u32[]{:S(2)}) copy-start(s32[3,16]{1,0:T(4,128)} %pos_ref.1) | copy-start | bytes 580
  34.9 1.5 %collective-permute-start.3 = (bf16[128,768]{1,0:T(8,128)(2,1)S(1)}, bf16[128,768]{1,0:T(8,128)(2,1)S(1)}, u32[]{:S(2)}, u32[]{:S(2)}) collective-permute-start(bf16[128,768]{1,0:T(8,128)(2,1)S(1)} %shard_map.53), channel_id=1, source_target_pairs={{0,2},{2,0},{4,6},{6,4},{8,10},{10,8},{12,14},{14,12},{16,18},{18,... | collective-permute-start | bytes 589832 | tf_op jit(solution)/shard_map/ppermute | solution.py:427

commit v6 on v5

--- a/solution.py
+++ b/solution.py
@@ -115,10 +115,8 @@
     return parts[0] if sides == 1 else jnp.concatenate(parts, 1)
 
 
-def ready_kernel(
-    vis_hbm, pos_hbm, dest_hbm, rows_ref, place_ref, vis_ref, pos_ref, dest_ref, sems, *, tiles, local, sides
-):
-    pairs = ((dest_hbm, dest_ref), (pos_hbm, pos_ref), (vis_hbm, vis_ref))
+def ready_kernel(pos_hbm, dest_hbm, cos_ref, sin_ref, place_ref, pos_ref, dest_ref, sems, *, tiles, local, sides):
+    pairs = ((dest_hbm, dest_ref), (pos_hbm, pos_ref))
     loads = [pltpu.make_async_copy(a, b, sems.at[n]) for n, (a, b) in enumerate(pairs)]
     for load in loads:
         load.start()
@@ -126,9 +124,7 @@
     loads[0].wait()
     place_ref[...] = placement(dest_ref, tokens, tiles, local, sides, place_ref.shape[0]).astype(BF16)
     loads[1].wait()
-    cosv, sinv = rope_tables(pos_ref)
-    loads[2].wait()
-    turn(vis_ref, rows_ref, per_group(cosv), per_group(sinv))
+    cos_ref[...], sin_ref[...] = rope_tables(pos_ref)
 
 
 def turn(from_ref, to_ref, cosv, sinv):
@@ -140,17 +136,15 @@
         to_ref[:, at : at + HD] = x
 
 
-def pack_kernel(rows_ref, place_ref, after_ref, *refs):
+def pack_kernel(vis_ref, cos_ref, sin_ref, place_ref, after_ref, *refs):
     del after_ref
     others, (out_hbm, both_ref, out_ref, out_sems) = refs[:-4], refs[-4:]
-    count = rows_ref.shape[0]
+    count = vis_ref.shape[0]
+    turn(vis_ref, both_ref.at[:count, :], per_group(cos_ref[...]), per_group(sin_ref[...]))
     if others:
         vis_ref, pos_ref = others
-        both_ref[:count, :] = rows_ref[...]
         cosv, sinv = rope_tables(pos_ref)
         turn(vis_ref, both_ref.at[count:, :], per_group(cosv), per_group(sinv))
-    else:
-        both_ref = rows_ref
     stores = Stores(out_ref, out_hbm, out_sems)
     for at in stores.pieces():
         out_ref[at, :] = jnp.dot(place_ref[at, :], both_ref[...], preferred_element_type=F32).astype(BF16)
@@ -204,7 +198,7 @@
     taken = counts > rest(slot, C).astype(F32)
     pick_ref[...] = ((slot[:, :1] == iota((seq, seq), 1)) & taken[:, :1]).astype(F32).astype(BF16)
     key_ok = jnp.where(taken, 0.0, NEG)
-    if bias_ref.shape[1] == LANES:
+    if seq > BLOCK:
         bias_ref[...] = key_ok
     else:
         query = slot_of(rest(iota(bias_ref.shape, 1), seq))
@@ -419,6 +413,8 @@
     total = seq * local
     qcols = QPK * HD
     sides = 2 if heads == 2 and tiles % 2 == 0 else 1
+    if local > 1 and sides * C != 4:
+        raise ValueError("unsupported mesh")
     targets = destination.reshape(-1, LANES)
     rows = vision_rows.reshape(count, width)
     kernel = functools.partial
@@ -427,16 +423,15 @@
         return lax.ppermute(x, "tile", [(t, t ^ 1) for t in range(tiles)])
 
     others = [to_pair(rows), to_pair(positions)] if sides == 2 else []
-    turned, place = call(
+    cos_own, sin_own, place = call(
         kernel(ready_kernel, tiles=tiles, local=local, sides=sides),
-        [((count, width), BF16), ((total, sides * count), BF16)],
-        *(pltpu.with_memory_space_constraint(x, pltpu.HBM) for x in (rows, positions, targets)),
-        specs=[HBM] * 3,
+        [((tokens, HD), F32), ((tokens, HD), F32), ((total, sides * count), BF16)],
+        *(pltpu.with_memory_space_constraint(x, pltpu.HBM) for x in (positions, targets)),
+        specs=[HBM] * 2,
         scratch=(
-            pltpu.VMEM(rows.shape, BF16),
             pltpu.VMEM(positions.shape, jnp.int32),
             pltpu.VMEM(targets.shape, jnp.int32),
-            pltpu.SemaphoreType.DMA((3,)),
+            pltpu.SemaphoreType.DMA((2,)),
         ),
     )
     slots = out_grad.shape[0]
@@ -447,7 +442,7 @@
         ((count, HD), F32),
         ((sides * count, total), BF16),
         ((seq, seq), BF16),
-        ((seq, QPK * BLOCK if sides == 2 and seq == BLOCK else LANES), F32),
+        ((seq, LANES if seq > BLOCK else QPK * seq), F32),
     ]
     early = []
     if sides == 2:
@@ -466,7 +461,9 @@
     outgoing = call(
         pack_kernel,
         [((total, width), BF16)],
-        turned,
+        rows,
+        cos_own,
+        sin_own,
         place,
         early[0][:16, :LANES] if early else place[:16, :LANES],
         *others,

time: 37.6 us -> 37.6 us (level)
  no operation moved by 1% of the time
where the time goes in v6:
time: 37.6 us; the launch traced here: 37.2 us
  blocking collectives  12.7 us (34%)
  starting transfers between devices  11 us (29%)
  Pallas kernels  7 us (19%)
  waiting for transfers between devices  4.98 us (13%)
  local copies, waits for them, and re-layouts  1.38 us (4%)
    all_to_all x1, blocking collectives, swap(): lax.all_to_all(parts, axes, split_axis=0, concat_axis=0, tiled=True, axis...  12.7 us
    all_to_all x1, starting transfers between devices, swap(): lax.all_to_all(parts, axes, split_axis=0, concat_axis=0, tiled=True, axis...  8.93 us
    pallas_call x10, Pallas kernels, call(): pl.pallas_call(kernel, out_shape=shapes[0] if single else shapes, in_spec...  7 us
    ppermute x1, waiting for transfers between devices, body(): cots = [own, lax.ppermute(other, 'head', [(0, 1), (1, 0)])]  3.77 us
    ppermute x1, starting transfers between devices, body(): cots = [own, lax.ppermute(other, 'head', [(0, 1), (1, 0)])]  1.53 us
    ppermute x3, waiting for transfers between devices, to_pair(): return lax.ppermute(x, 'tile', [(t, t ^ 1) for t in range(tiles)])  1.21 us
  transfers between devices with their start and end apart: 5, of which 2 were waited for; matrix products, arithmetic and copies ran while one was open for 2% of the time, Pallas kernels for 11%

profile of v6, /device:TPU:0, one launch (start us, length us, event | category | flops | bytes accessed | tf_op | source)
XLA Modules:
  0.0 37.2 jit_solution(8042668352050566829)
XLA Ops:
  0.0 0.0 copy-start.1
  0.0 0.5 %collective-permute-start = (bf16[128,768]{1,0:T(8,128)(2,1)}, bf16[128,768]{1,0:T(8,128)(2,1)S(1)}, u32[]{:S(2)}, u32[]{:S(2)}) collective-permute-start(bf16[128,768]{1,0:T(8,128)(2,1)} %bitcast.14), channel_id=1, source_target_pairs={{0,2},{2,0},{4,6},{6,4},{8,10},{10,8},{12,14},{14,12},{16,18},{18,... | collective-permute-start | bytes 589832 | tf_op jit(solution)/shard_map/ppermute | solution.py:423
  0.5 0.1 collective-permute-start.1
  0.5 1.2 %shard_map.46 = (f32[16,128]{1,0:T(8,128)S(1)}, f32[16,128]{1,0:T(8,128)S(1)}, bf16[256,256]{1,0:T(8,128)(2,1)S(1)}) custom-call(s32[3,16]{1,0:T(4,128)} %pos_ref.1, s32[4,128]{1,0:T(4,128)} %bitcast.16), custom_call_target="tpu_custom_call" | custom-call | tf_op jit(solution)/shard_map/pallas_call | solution.py:396
  1.7 2.3 %shard_map.47 = (bf16[128,512]{1,0:T(8,128)(2,1)S(1)}, bf16[128,512]{1,0:T(8,128)(2,1)S(1)}, f32[128,128]{1,0:T(8,128)S(1)}, f32[128,128]{1,0:T(8,128)S(1)}, bf1...) custom-call(bf16[256,512]{1,0:T(8,128)(2,1)} %bitcast.12, s32[3,16]{1,0:T(4,128)} %pos_ref.1, ...), custom_call_target="tpu_custom_call" | custom-call | tf_op jit(solution)/shard_map/pallas_call | solution.py:396
  4.1 0.0 collective-permute-done.1.refs_1_
  4.1 0.0 collective-permute-done.refs_0_
  4.1 0.0 copy-done.1
  4.1 1.3 %shard_map.48 = bf16[256,768]{1,0:T(8,128)(2,1)} custom-call(bf16[128,768]{1,0:T(8,128)(2,1)S(1)} %bitcast.15, f32[16,128]{1,0:T(8,128)S(1)} %get-tuple-element.22.cos_ref, f32[16,128]{1,0:T(8,128)S(1)} %get-tuple-element.23.sin_ref, bf16[256,256]{1,0:T(8,128)(2,1)S(1)} %get-tuple-element.24.place_ref, bf16[16,128]{1,0:T(8,128)(2,1)S(1)} %slice.6.after_ref, ...), custom_call_target="tpu_custom_call" | custom-call | tf_op jit(solution)/shard_map/pallas_call | solution.py:396
  5.4 0.0 copy-start
  5.4 8.9 %all-to-all-start = ((bf16[16,16,768]{2,1,0:T(8,128)(2,1)}), bf16[16,16,768]{2,1,0:T(8,128)(2,1)S(1)}, u32[]{:S(2)}, u32[]{:S(2)}) async-start(bf16[16,16,768]{2,1,0:T(8,128)(2,1)} %bitcast.3), calls=%async_computation | async-start | bytes 786432 | tf_op jit(solution)/shard_map/all_to_all | solution.py:489
  14.4 0.0 copy-done
  14.4 1.5 %collective-permute-start.2 = (bf16[128,512]{1,0:T(8,128)(2,1)S(1)}, bf16[128,512]{1,0:T(8,128)(2,1)S(1)}, u32[]{:S(2)}, u32[]{:S(2)}) collective-permute-start(bf16[128,512]{1,0:T(8,128)(2,1)S(1)} %get-tuple-element.37), channel_id=1, source_target_pairs={{0,1},{1,0},{2,3},{3,2},{4,5},{5,4},{6,7},{7,6},{8,9},{9,8},{10,11... | collective-permute-start | bytes 393224 | tf_op jit(solution)/shard_map/ppermute | solution.py:497
  15.9 0.7 %slice.8.after_ref = bf16[16,128]{1,0:T(8,128)(2,1)S(1)} slice(bf16[256,768]{1,0:T(8,128)(2,1)} %shard_map.48), slice={[0:16], [0:128]} | slice | bytes 8192 | tf_op jit(solution)/shard_map/slice | solution.py:506
  16.6 0.0 copy-start.3
  16.6 0.0 copy-start.2
  16.6 0.7 %copy-done.3 = s32[512,1]{0,1:T(1,128)S(1)} copy-done((s32[512,1]{0,1:T(1,128)S(1)}, s32[512,1]{0,1:T(1,128)}, u32[]{:S(2)}) %copy-start.3) | copy-done | bytes 2072
  17.3 0.0 copy-done.2
  17.3 3.8 %collective-permute-done.2.refs_1_ = bf16[128,512]{1,0:T(8,128)(2,1)S(1)} collective-permute-done((bf16[128,512]{1,0:T(8,128)(2,1)S(1)}, bf16[128,512]{1,0:T(8,128)(2,1)S(1)}, u32[]{:S(2)}, u32[]{:S(2)}) %collective-permute-start.2) | collective-permute-done | bytes 131104 | tf_op jit(solution)/shard_map/ppermute | solution.py:497
  21.1 0.2 shard_map.51.cot_ref
  21.4 0.0 all-to-all-done
  21.4 0.6 %shard_map.52 = bf16[256,768]{1,0:T(8,128)(2,1)S(1)} custom-call(bf16[256,768]{1,0:T(8,128)(2,1)S(1)} %bitcast.10, f32[64,256]{1,0:T(8,128)S(1)} %get-tuple-element.33.bias_ref, bf16[1024,128]{1,0:T(8,128)(2,1)S(1)} %shard_map.51.cot_ref), custom_call_target="tpu_custom_call" | custom-call | tf_op jit(solution)/shard_map/pallas_call | solution.py:396
  22.0 12.7 %all_to_all.10 = bf16[16,16,768]{2,1,0:T(8,128)(2,1)S(1)} all-to-all(bf16[16,16,768]{2,1,0:T(8,128)(2,1)S(1)} %bitcast.11), channel_id=1, replica_groups={{16,8,0,24,20,12,4,28,17,9,1,25,21,13,5,29},{18,10,2,26,22,14,6,30,19,1..., dimensions={0} | all-to-all | bytes 786432 | tf_op jit(solution)/shard_map/all_to_all | solution.py:489
  34.7 0.2 shard_map.53
  34.9 0.1 collective-permute-start.3
  35.0 0.2 shard_map.54.refs_1_
  35.2 1.2 %collective-permute-done.3.refs_0_ = bf16[128,768]{1,0:T(8,128)(2,1)S(1)} collective-permute-done((bf16[128,768]{1,0:T(8,128)(2,1)S(1)}, bf16[128,768]{1,0:T(8,128)(2,1)S(1)}, u32[]{:S(2)}, u32[]{:S(2)}) %collective-permute-start.3) | collective-permute-done | bytes 196640 | tf_op jit(solution)/shard_map/ppermute | solution.py:423
  36.4 0.8 %shard_map.55 = bf16[128,768]{1,0:T(8,128)(2,1)} custom-call(f32[128,128]{1,0:T(8,128)S(1)} %get-tuple-element.31.cos_ref, f32[128,128]{1,0:T(8,128)S(1)} %get-tuple-element.32.sin_ref, bf16[128,768]{1,0:T(8,128)(2,1)S(1)} %collective-permute-done.3.refs_0_, bf16[128,768]{1,0:T(8,128)(2,1)S(1)} %shard_map.54.refs_1_), custom_call_target="tpu_custom_call" | custom-call | tf_op jit(solution)/shard_map/pallas_call | solution.py:396
  (3 shorter events, 0.1 us)
Async XLA Ops:
  0.0 4.1 %copy-start.1 = (bf16[16,8,768]{2,1,0:T(8,128)(2,1)S(1)}, bf16[16,8,768]{2,1,0:T(8,128)(2,1)}, u32[]{:S(2)}) copy-start(bf16[16,8,768]{2,1,0:T(8,128)(2,1)} %param.4) | copy-start | bytes 589828
  0.0 4.1 %collective-permute-start = (bf16[128,768]{1,0:T(8,128)(2,1)}, bf16[128,768]{1,0:T(8,128)(2,1)S(1)}, u32[]{:S(2)}, u32[]{:S(2)}) collective-permute-start(bf16[128,768]{1,0:T(8,128)(2,1)} %bitcast.14), channel_id=1, source_target_pairs={{0,2},{2,0},{4,6},{6,4},{8,10},{10,8},{12,14},{14,12},{16,18},{18,... | collective-permute-start | bytes 589832 | tf_op jit(solution)/shard_map/ppermute | solution.py:423
  0.5 3.6 %collective-permute-start.1 = (s32[3,16]{1,0:T(4,128)}, s32[3,16]{1,0:T(4,128)S(1)}, u32[]{:S(2)}, u32[]{:S(2)}) collective-permute-start(s32[3,16]{1,0:T(4,128)} %pos_ref.1), channel_id=1, source_target_pairs={{0,2},{2,0},{4,6},{6,4},{8,10},{10,8},{12,14},{14,12},{16,18},{18,... | collective-permute-start | bytes 584 | tf_op jit(solution)/shard_map/ppermute | solution.py:423
  5.4 8.9 %copy-start = (bf16[32,8,512]{2,1,0:T(8,128)(2,1)S(1)}, bf16[32,8,512]{2,1,0:T(8,128)(2,1)}, u32[]{:S(2)}) copy-start(bf16[32,8,512]{2,1,0:T(8,128)(2,1)} %param.7) | copy-start | bytes 786436
  5.4 15.9 %all-to-all-start = ((bf16[16,16,768]{2,1,0:T(8,128)(2,1)}), bf16[16,16,768]{2,1,0:T(8,128)(2,1)S(1)}, u32[]{:S(2)}, u32[]{:S(2)}) async-start(bf16[16,16,768]{2,1,0:T(8,128)(2,1)} %bitcast.3), calls=%async_computation | async-start | bytes 786432 | tf_op jit(solution)/shard_map/all_to_all | solution.py:489
  14.4 6.7 %collective-permute-start.2 = (bf16[128,512]{1,0:T(8,128)(2,1)S(1)}, bf16[128,512]{1,0:T(8,128)(2,1)S(1)}, u32[]{:S(2)}, u32[]{:S(2)}) collective-permute-start(bf16[128,512]{1,0:T(8,128)(2,1)S(1)} %get-tuple-element.37), channel_id=1, source_target_pairs={{0,1},{1,0},{2,3},{3,2},{4,5},{5,4},{6,7},{7,6},{8,9},{9,8},{10,11... | collective-permute-start | bytes 393224 | tf_op jit(solution)/shard_map/ppermute | solution.py:497
  16.6 0.7 %copy-start.3 = (s32[512,1]{0,1:T(1,128)S(1)}, s32[512,1]{0,1:T(1,128)}, u32[]{:S(2)}) copy-start(s32[512,1]{0,1:T(1,128)} %param.6) | copy-start | bytes 6148
  16.6 0.7 %copy-start.2 = (s32[3,16]{1,0:T(4,128)S(1)}, s32[3,16]{1,0:T(4,128)}, u32[]{:S(2)}) copy-start(s32[3,16]{1,0:T(4,128)} %pos_ref.1) | copy-start | bytes 580
  34.9 1.5 %collective-permute-start.3 = (bf16[128,768]{1,0:T(8,128)(2,1)S(1)}, bf16[128,768]{1,0:T(8,128)(2,1)S(1)}, u32[]{:S(2)}, u32[]{:S(2)}) collective-permute-start(bf16[128,768]{1,0:T(8,128)(2,1)S(1)} %shard_map.53), channel_id=1, source_target_pairs={{0,2},{2,0},{4,6},{6,4},{8,10},{10,8},{12,14},{14,12},{16,18},{18,... | collective-permute-start | bytes 589832 | tf_op jit(solution)/shard_map/ppermute | solution.py:423

commit v7 on v6

--- a/solution.py
+++ b/solution.py
@@ -40,13 +40,20 @@
     return at % size if size & (size - 1) else at & (size - 1)
 
 
-def rope_tables(pos_ref):
-    tokens = pos_ref.shape[1]
+def rope_parts(tokens):
     half = HD // 2
     slots = rest(iota((tokens, HD), 1), half)
-    first = half // 4
-    second = (half - first) // 2
+    freq = jnp.exp(-(2.0 * slots.astype(F32) / HD) * math.log(1000000.0))
+    sign = jnp.where(iota((tokens, HD), 1) < half, -1.0, 1.0)
     eye = (iota((tokens, tokens), 0) == iota((tokens, tokens), 1)).astype(BF16)
+    return slots, freq, sign, eye
+
+
+def rope_tables(pos_ref, parts=None):
+    tokens = pos_ref.shape[1]
+    slots, freq, sign, eye = parts or rope_parts(tokens)
+    first = HD // 2 // 4
+    second = (HD // 2 - first) // 2
     column = [
         nt(eye, jnp.broadcast_to(pos_ref[s : s + 1, :].astype(F32).astype(BF16), (HD, tokens)))
         for s in range(3)
@@ -54,9 +61,7 @@
     chosen = jnp.where(
         slots < first, column[0], jnp.where(slots < first + second, column[1], column[2])
     )
-    freq = jnp.exp(-(2.0 * slots.astype(F32) / HD) * math.log(1000000.0))
     angle = chosen * freq
-    sign = jnp.where(iota((tokens, HD), 1) < half, -1.0, 1.0)
     return jnp.cos(angle), jnp.sin(angle) * sign
 
 
@@ -65,13 +70,19 @@
     return jnp.broadcast_to(table[:, None, :], (tokens, KV, HD)).reshape(tokens * KV, HD)
 
 
-def token_slots(dest_ref, tokens, tile):
+def token_finders(tokens, tile):
     start = (tile * lax.axis_size("head") + lax.axis_index("head")) * tokens
     count = tokens * KV
     off = start % LANES
-    row = dest_ref[pl.ds(start // LANES, 1), :].astype(F32).astype(BF16)
     wide = (iota((count, LANES), 1) == off + over(iota((count, LANES), 0), KV)).astype(BF16)
     narrow = (iota((tokens, LANES), 1) == off + iota((tokens, LANES), 0)).astype(BF16)
+    return start // LANES, wide, narrow
+
+
+def token_slots(dest_ref, finders):
+    at, wide, narrow = finders
+    count, tokens = wide.shape[0], narrow.shape[0]
+    row = dest_ref[pl.ds(at, 1), :].astype(F32).astype(BF16)
     along = nt(jnp.broadcast_to(row, (8, LANES)), wide)[:1]
     down = nt(narrow, jnp.broadcast_to(row, (count, LANES)))
     lane = iota((tokens, count), 1)
@@ -99,20 +110,25 @@
     return list(range(units))
 
 
-def placement(dest_ref, tokens, tiles, local, sides, total):
-    count = tokens * KV
+def placement_parts(tokens, tiles, local, sides, total):
     tile = lax.axis_index("tile")
     side = tile % sides
     head, unit, at_side, rank, group = row_parts(iota((total, LANES), 0), tiles, local, sides)
     target = unit * sides + side
     rows = (((target * C + rank) * sides + at_side) * KV + head * local + group)[:, :1]
-    parts = []
-    for other in range(sides):
-        from_side = side + other - 2 * side * other
-        slots = token_slots(dest_ref, tokens, tile - side + from_side)
-        lanes = (slots * sides + from_side) * KV + rest(iota((1, count), 1), KV)
-        parts.append((rows == lanes).astype(F32))
-    return parts[0] if sides == 1 else jnp.concatenate(parts, 1)
+    from_sides = [side + other - 2 * side * other for other in range(sides)]
+    return rows, [(n, token_finders(tokens, tile - side + n)) for n in from_sides]
+
+
+def placement(dest_ref, parts):
+    rows, devices = parts
+    places = []
+    for from_side, finders in devices:
+        count = finders[1].shape[0]
+        slots = token_slots(dest_ref, finders)
+        lanes = (slots * len(devices) + from_side) * KV + rest(iota((1, count), 1), KV)
+        places.append((rows == lanes).astype(F32))
+    return places[0] if len(places) == 1 else jnp.concatenate(places, 1)
 
 
 def ready_kernel(pos_hbm, dest_hbm, cos_ref, sin_ref, place_ref, pos_ref, dest_ref, sems, *, tiles, local, sides):
@@ -121,10 +137,12 @@
     for load in loads:
         load.start()
     tokens = pos_ref.shape[1]
-    loads[0].wait()
-    place_ref[...] = placement(dest_ref, tokens, tiles, local, sides, place_ref.shape[0]).astype(BF16)
-    loads[1].wait()
-    cos_ref[...], sin_ref[...] = rope_tables(pos_ref)
+    place_parts = placement_parts(tokens, tiles, local, sides, place_ref.shape[0])
+    angle_parts = rope_parts(tokens)
+    for load in loads:
+        load.wait()
+    place_ref[...] = placement(dest_ref, place_parts).astype(BF16)
+    cos_ref[...], sin_ref[...] = rope_tables(pos_ref, angle_parts)
 
 
 def turn(from_ref, to_ref, cosv, sinv):
@@ -178,7 +196,7 @@
     cosv, sinv = rope_tables(pos_ref)
     cos_ref[...] = per_group(cosv)
     sin_ref[...] = per_group(sinv)
-    place = placement(dest_ref, tokens, tiles, local, sides, seq * local)
+    place = placement(dest_ref, placement_parts(tokens, tiles, local, sides, seq * local))
     gather_ref[...] = jnp.transpose(place).astype(BF16)
     mine = lax.axis_index("tile")
 
@@ -228,12 +246,14 @@
     def _():
         pairs = ((dest_hbm, dest_ref), (pos_hbm, pos_ref), (cot_hbm, cot_ref))
         loads = [pltpu.make_async_copy(a, b, sems.at[n]) for n, (a, b) in enumerate(pairs)]
-        for load in loads:
+        for load in loads[:2]:
             load.start()
-        for load in loads:
+        for load in loads[:2]:
             load.wait()
+        fill_tables(pos_ref, dest_ref, out_refs[2:], tiles, heads, local, sides)
+        loads[2].start()
+        loads[2].wait()
         split_cots(cot_ref, *out_refs[:2], local)
-        fill_tables(pos_ref, dest_ref, out_refs[2:], tiles, heads, local, sides)
 
 
 def table_kernel(pos_ref, dest_ref, after_ref, *refs, tiles, heads, local, sides):

time: 37.6 us -> 37.6 us (level)
  blocking collectives: 12.7 us -> 12.3 us
  Pallas kernels: 7 us -> 7.39 us
    pallas_call x10, Pallas kernels: 7 us -> 7.39 us  [call(): pl.pallas_call(kernel, out_shape=shapes[0] if single else shapes, in_spec...]
    all_to_all x1, blocking collectives: 12.7 us -> 12.3 us  [swap(): lax.all_to_all(parts, axes, split_axis=0, concat_axis=0, tiled=True, axis...]
  transfers between devices with their start and end apart: 5 -> 5, of which waited for: 2 -> 2; matrix products, arithmetic and copies ran while one was open for 2% -> 2% of each run, Pallas kernels for 11% -> 12%
where the time goes in v7:
time: 37.6 us; the launch traced here: 37.2 us
  blocking collectives  12.3 us (33%)
  starting transfers between devices  11 us (29%)
  Pallas kernels  7.39 us (20%)
  waiting for transfers between devices  4.94 us (13%)
  local copies, waits for them, and re-layouts  1.38 us (4%)
    all_to_all x1, blocking collectives, swap(): lax.all_to_all(parts, axes, split_axis=0, concat_axis=0, tiled=True, axis...  12.3 us
    all_to_all x1, starting transfers between devices, swap(): lax.all_to_all(parts, axes, split_axis=0, concat_axis=0, tiled=True, axis...  8.92 us
    pallas_call x10, Pallas kernels, call(): pl.pallas_call(kernel, out_shape=shapes[0] if single else shapes, in_spec...  7.39 us
    ppermute x1, waiting for transfers between devices, body(): cots = [own, lax.ppermute(other, 'head', [(0, 1), (1, 0)])]  3.73 us
    ppermute x1, starting transfers between devices, body(): cots = [own, lax.ppermute(other, 'head', [(0, 1), (1, 0)])]  1.53 us
    ppermute x3, waiting for transfers between devices, to_pair(): return lax.ppermute(x, 'tile', [(t, t ^ 1) for t in range(tiles)])  1.21 us
  transfers between devices with their start and end apart: 5, of which 2 were waited for; matrix products, arithmetic and copies ran while one was open for 2% of the time, Pallas kernels for 12%

profile of v7, /device:TPU:0, one launch (start us, length us, event | category | flops | bytes accessed | tf_op | source)
XLA Modules:
  0.0 37.2 jit_solution(13319827170992800638)
XLA Ops:
  0.0 0.0 copy-start.1
  0.0 0.5 %collective-permute-start = (bf16[128,768]{1,0:T(8,128)(2,1)}, bf16[128,768]{1,0:T(8,128)(2,1)S(1)}, u32[]{:S(2)}, u32[]{:S(2)}) collective-permute-start(bf16[128,768]{1,0:T(8,128)(2,1)} %bitcast.14), channel_id=1, source_target_pairs={{0,2},{2,0},{4,6},{6,4},{8,10},{10,8},{12,14},{14,12},{16,18},{18,... | collective-permute-start | bytes 589832 | tf_op jit(solution)/shard_map/ppermute | solution.py:443
  0.5 0.1 collective-permute-start.1
  0.5 1.0 %shard_map.46 = (f32[16,128]{1,0:T(8,128)S(1)}, f32[16,128]{1,0:T(8,128)S(1)}, bf16[256,256]{1,0:T(8,128)(2,1)S(1)}) custom-call(s32[3,16]{1,0:T(4,128)} %pos_ref.1, s32[4,128]{1,0:T(4,128)} %bitcast.16), custom_call_target="tpu_custom_call" | custom-call | tf_op jit(solution)/shard_map/pallas_call | solution.py:416
  1.5 2.9 %shard_map.47 = (bf16[128,512]{1,0:T(8,128)(2,1)S(1)}, bf16[128,512]{1,0:T(8,128)(2,1)S(1)}, f32[128,128]{1,0:T(8,128)S(1)}, f32[128,128]{1,0:T(8,128)S(1)}, bf1...) custom-call(bf16[256,512]{1,0:T(8,128)(2,1)} %bitcast.12, s32[3,16]{1,0:T(4,128)} %pos_ref.1, ...), custom_call_target="tpu_custom_call" | custom-call | tf_op jit(solution)/shard_map/pallas_call | solution.py:416
  4.5 0.0 collective-permute-done.1.refs_1_
  4.5 0.0 collective-permute-done.refs_0_
  4.5 0.0 copy-done.1
  4.5 1.3 %shard_map.48 = bf16[256,768]{1,0:T(8,128)(2,1)} custom-call(bf16[128,768]{1,0:T(8,128)(2,1)S(1)} %bitcast.15, f32[16,128]{1,0:T(8,128)S(1)} %get-tuple-element.22.cos_ref, f32[16,128]{1,0:T(8,128)S(1)} %get-tuple-element.23.sin_ref, bf16[256,256]{1,0:T(8,128)(2,1)S(1)} %get-tuple-element.24.place_ref, bf16[16,128]{1,0:T(8,128)(2,1)S(1)} %slice.6.after_ref, ...), custom_call_target="tpu_custom_call" | custom-call | tf_op jit(solution)/shard_map/pallas_call | solution.py:416
  5.8 0.0 copy-start
  5.8 8.9 %all-to-all-start = ((bf16[16,16,768]{2,1,0:T(8,128)(2,1)}), bf16[16,16,768]{2,1,0:T(8,128)(2,1)S(1)}, u32[]{:S(2)}, u32[]{:S(2)}) async-start(bf16[16,16,768]{2,1,0:T(8,128)(2,1)} %bitcast.3), calls=%async_computation | async-start | bytes 786432 | tf_op jit(solution)/shard_map/all_to_all | solution.py:509
  14.7 0.0 copy-done
  14.8 1.5 %collective-permute-start.2 = (bf16[128,512]{1,0:T(8,128)(2,1)S(1)}, bf16[128,512]{1,0:T(8,128)(2,1)S(1)}, u32[]{:S(2)}, u32[]{:S(2)}) collective-permute-start(bf16[128,512]{1,0:T(8,128)(2,1)S(1)} %get-tuple-element.37), channel_id=1, source_target_pairs={{0,1},{1,0},{2,3},{3,2},{4,5},{5,4},{6,7},{7,6},{8,9},{9,8},{10,11... | collective-permute-start | bytes 393224 | tf_op jit(solution)/shard_map/ppermute | solution.py:517
  16.3 0.7 %slice.8.after_ref = bf16[16,128]{1,0:T(8,128)(2,1)S(1)} slice(bf16[256,768]{1,0:T(8,128)(2,1)} %shard_map.48), slice={[0:16], [0:128]} | slice | bytes 8192 | tf_op jit(solution)/shard_map/slice | solution.py:526
  17.0 0.0 copy-start.3
  17.0 0.0 copy-start.2
  17.0 0.7 %copy-done.3 = s32[512,1]{0,1:T(1,128)S(1)} copy-done((s32[512,1]{0,1:T(1,128)S(1)}, s32[512,1]{0,1:T(1,128)}, u32[]{:S(2)}) %copy-start.3) | copy-done | bytes 2072
  17.7 0.0 copy-done.2
  17.7 3.7 %collective-permute-done.2.refs_1_ = bf16[128,512]{1,0:T(8,128)(2,1)S(1)} collective-permute-done((bf16[128,512]{1,0:T(8,128)(2,1)S(1)}, bf16[128,512]{1,0:T(8,128)(2,1)S(1)}, u32[]{:S(2)}, u32[]{:S(2)}) %collective-permute-start.2) | collective-permute-done | bytes 131104 | tf_op jit(solution)/shard_map/ppermute | solution.py:517
  21.5 0.2 shard_map.51.cot_ref
  21.7 0.0 all-to-all-done
  21.7 0.6 %shard_map.52 = bf16[256,768]{1,0:T(8,128)(2,1)S(1)} custom-call(bf16[256,768]{1,0:T(8,128)(2,1)S(1)} %bitcast.10, f32[64,256]{1,0:T(8,128)S(1)} %get-tuple-element.33.bias_ref, bf16[1024,128]{1,0:T(8,128)(2,1)S(1)} %shard_map.51.cot_ref), custom_call_target="tpu_custom_call" | custom-call | tf_op jit(solution)/shard_map/pallas_call | solution.py:416
  22.3 12.3 %all_to_all.10 = bf16[16,16,768]{2,1,0:T(8,128)(2,1)S(1)} all-to-all(bf16[16,16,768]{2,1,0:T(8,128)(2,1)S(1)} %bitcast.11), channel_id=1, replica_groups={{16,8,0,24,20,12,4,28,17,9,1,25,21,13,5,29},{18,10,2,26,22,14,6,30,19,1..., dimensions={0} | all-to-all | bytes 786432 | tf_op jit(solution)/shard_map/all_to_all | solution.py:509
  34.7 0.2 shard_map.53
  34.9 0.1 collective-permute-start.3
  35.0 0.2 shard_map.54.refs_1_
  35.2 1.2 %collective-permute-done.3.refs_0_ = bf16[128,768]{1,0:T(8,128)(2,1)S(1)} collective-permute-done((bf16[128,768]{1,0:T(8,128)(2,1)S(1)}, bf16[128,768]{1,0:T(8,128)(2,1)S(1)}, u32[]{:S(2)}, u32[]{:S(2)}) %collective-permute-start.3) | collective-permute-done | bytes 196640 | tf_op jit(solution)/shard_map/ppermute | solution.py:443
  36.4 0.8 %shard_map.55 = bf16[128,768]{1,0:T(8,128)(2,1)} custom-call(f32[128,128]{1,0:T(8,128)S(1)} %get-tuple-element.31.cos_ref, f32[128,128]{1,0:T(8,128)S(1)} %get-tuple-element.32.sin_ref, bf16[128,768]{1,0:T(8,128)(2,1)S(1)} %collective-permute-done.3.refs_0_, bf16[128,768]{1,0:T(8,128)(2,1)S(1)} %shard_map.54.refs_1_), custom_call_target="tpu_custom_call" | custom-call | tf_op jit(solution)/shard_map/pallas_call | solution.py:416
  (3 shorter events, 0.1 us)
Async XLA Ops:
  0.0 4.5 %copy-start.1 = (bf16[16,8,768]{2,1,0:T(8,128)(2,1)S(1)}, bf16[16,8,768]{2,1,0:T(8,128)(2,1)}, u32[]{:S(2)}) copy-start(bf16[16,8,768]{2,1,0:T(8,128)(2,1)} %param.4) | copy-start | bytes 589828
  0.0 4.5 %collective-permute-start = (bf16[128,768]{1,0:T(8,128)(2,1)}, bf16[128,768]{1,0:T(8,128)(2,1)S(1)}, u32[]{:S(2)}, u32[]{:S(2)}) collective-permute-start(bf16[128,768]{1,0:T(8,128)(2,1)} %bitcast.14), channel_id=1, source_target_pairs={{0,2},{2,0},{4,6},{6,4},{8,10},{10,8},{12,14},{14,12},{16,18},{18,... | collective-permute-start | bytes 589832 | tf_op jit(solution)/shard_map/ppermute | solution.py:443
  0.5 4.0 %collective-permute-start.1 = (s32[3,16]{1,0:T(4,128)}, s32[3,16]{1,0:T(4,128)S(1)}, u32[]{:S(2)}, u32[]{:S(2)}) collective-permute-start(s32[3,16]{1,0:T(4,128)} %pos_ref.1), channel_id=1, source_target_pairs={{0,2},{2,0},{4,6},{6,4},{8,10},{10,8},{12,14},{14,12},{16,18},{18,... | collective-permute-start | bytes 584 | tf_op jit(solution)/shard_map/ppermute | solution.py:443
  5.8 8.9 %copy-start = (bf16[32,8,512]{2,1,0:T(8,128)(2,1)S(1)}, bf16[32,8,512]{2,1,0:T(8,128)(2,1)}, u32[]{:S(2)}) copy-start(bf16[32,8,512]{2,1,0:T(8,128)(2,1)} %param.7) | copy-start | bytes 786436
  5.8 15.9 %all-to-all-start = ((bf16[16,16,768]{2,1,0:T(8,128)(2,1)}), bf16[16,16,768]{2,1,0:T(8,128)(2,1)S(1)}, u32[]{:S(2)}, u32[]{:S(2)}) async-start(bf16[16,16,768]{2,1,0:T(8,128)(2,1)} %bitcast.3), calls=%async_computation | async-start | bytes 786432 | tf_op jit(solution)/shard_map/all_to_all | solution.py:509
  14.8 6.7 %collective-permute-start.2 = (bf16[128,512]{1,0:T(8,128)(2,1)S(1)}, bf16[128,512]{1,0:T(8,128)(2,1)S(1)}, u32[]{:S(2)}, u32[]{:S(2)}) collective-permute-start(bf16[128,512]{1,0:T(8,128)(2,1)S(1)} %get-tuple-element.37), channel_id=1, source_target_pairs={{0,1},{1,0},{2,3},{3,2},{4,5},{5,4},{6,7},{7,6},{8,9},{9,8},{10,11... | collective-permute-start | bytes 393224 | tf_op jit(solution)/shard_map/ppermute | solution.py:517
  17.0 0.7 %copy-start.3 = (s32[512,1]{0,1:T(1,128)S(1)}, s32[512,1]{0,1:T(1,128)}, u32[]{:S(2)}) copy-start(s32[512,1]{0,1:T(1,128)} %param.6) | copy-start | bytes 6148
  17.0 0.7 %copy-start.2 = (s32[3,16]{1,0:T(4,128)S(1)}, s32[3,16]{1,0:T(4,128)}, u32[]{:S(2)}) copy-start(s32[3,16]{1,0:T(4,128)} %pos_ref.1) | copy-start | bytes 580
  34.9 1.5 %collective-permute-start.3 = (bf16[128,768]{1,0:T(8,128)(2,1)S(1)}, bf16[128,768]{1,0:T(8,128)(2,1)S(1)}, u32[]{:S(2)}, u32[]{:S(2)}) collective-permute-start(bf16[128,768]{1,0:T(8,128)(2,1)S(1)} %shard_map.53), channel_id=1, source_target_pairs={{0,2},{2,0},{4,6},{6,4},{8,10},{10,8},{12,14},{14,12},{16,18},{18,... | collective-permute-start | bytes 589832 | tf_op jit(solution)/shard_map/ppermute | solution.py:443

commit v8 on v7

--- a/solution.py
+++ b/solution.py
@@ -91,29 +91,32 @@
     return (along * C + rank).astype(jnp.int32)
 
 
-def row_parts(at, tiles, local, sides):
+def row_parts(at, tiles, local, sides, back=False):
     rank, at = rest(at, C), over(at, C)
     side, at = rest(at, sides), over(at, sides)
     group, at = rest(at, local), over(at, local)
     units = tiles // sides
-    order = unit_order(units, sides)
+    order = unit_order(units, sides, back)
     place, head = rest(at, units), over(at, units)
-    unit = place
-    if order != list(range(units)):
+    if order == [(n + order[0]) % units for n in range(units)]:
+        unit = rest(place + order[0], units)
+    else:
         unit = sum(jnp.where(place == n, order[n], 0) for n in range(units))
     return head, unit, side, rank, group
 
 
-def unit_order(units, sides):
-    if sides == 2 and units == 8:
+def unit_order(units, sides, back):
+    if sides == 1:
+        return list(range(units))
+    if back and units == 8:
         return [z * 2 + y for y in (0, 1) for z in (2, 1, 0, 3)]
-    return list(range(units))
-
-
-def placement_parts(tokens, tiles, local, sides, total):
+    return [(n + units // 2) % units for n in range(units)]
+
+
+def placement_parts(tokens, tiles, local, sides, total, back=False):
     tile = lax.axis_index("tile")
     side = tile % sides
-    head, unit, at_side, rank, group = row_parts(iota((total, LANES), 0), tiles, local, sides)
+    head, unit, at_side, rank, group = row_parts(iota((total, LANES), 0), tiles, local, sides, back)
     target = unit * sides + side
     rows = (((target * C + rank) * sides + at_side) * KV + head * local + group)[:, :1]
     from_sides = [side + other - 2 * side * other for other in range(sides)]
@@ -196,7 +199,7 @@
     cosv, sinv = rope_tables(pos_ref)
     cos_ref[...] = per_group(cosv)
     sin_ref[...] = per_group(sinv)
-    place = placement(dest_ref, placement_parts(tokens, tiles, local, sides, seq * local))
+    place = placement(dest_ref, placement_parts(tokens, tiles, local, sides, seq * local, True))
     gather_ref[...] = jnp.transpose(place).astype(BF16)
     mine = lax.axis_index("tile")
 
@@ -334,7 +337,7 @@
     return whole.reshape(rows * len(parts), width)
 
 
-def attend_kernel(rows_ref, bias_ref, cot_ref, out_ref, sums_at, *, local):
+def attend_kernel(rows_ref, bias_ref, cot_ref, out_ref, sums_at, *, local, places):
     total, width = rows_ref.shape
     seq = total // local
     block = min(BLOCK, seq)
@@ -371,7 +374,11 @@
         arrived = by_group(rows_ref[...], local)
         terms = zip(*step(0, arrived, bias_ref[...]))
         parts = [jnp.concatenate([x, y * scale, z], 1) for x, y, z in terms]
-        out_ref[...] = by_place(parts).astype(BF16)
+        grads = by_place(parts).astype(BF16)
+        if places != sorted(places):
+            size = total // len(places)
+            grads = jnp.concatenate([grads[n * size : (n + 1) * size] for n in places], 0)
+        out_ref[...] = grads
         return
     sums_at[...] = jnp.zeros(sums_at.shape, F32)
 
@@ -495,13 +502,13 @@
         ),
     )
 
-    def swap(rows):
+    def swap(rows, back=False):
         units = tiles // sides
         parts = rows.reshape(heads * units, -1, width)
         if sides == 1:
             axes, groups = ("head", "tile"), None
         else:
-            axes, order = ("tile", "head"), unit_order(units, sides)
+            axes, order = ("tile", "head"), unit_order(units, sides, back)
             groups = [
                 [(unit * sides + side) * heads + head for head in range(heads) for unit in order]
                 for side in range(sides)
@@ -533,18 +540,21 @@
         *cots,
         scratch=(pltpu.VMEM((total, qcols), BF16),),
     )
+    units = tiles // sides
+    there, back = (unit_order(units, sides, way) for way in (False, True))
+    places = [head * units + there.index(unit) for head in range(heads) for unit in back]
     grads = call(
-        kernel(attend_kernel, local=local),
+        kernel(attend_kernel, local=local, places=places),
         [((total, width), BF16)],
         incoming,
         bias,
         cot,
         scratch=(pltpu.VMEM((seq if seq > BLOCK else 8, 2 * HD), F32),),
     )
-    back = swap(grads)
+    returned = swap(grads, True)
 
     def gathered(part):
-        return call(kernel(gather_kernel, part=part), [((count, width), BF16)], back, gather)
+        return call(kernel(gather_kernel, part=part), [((count, width), BF16)], returned, gather)
 
     parts = [to_pair(gathered(1))] if sides == 2 else []
     parts.append(gathered(0))

time: 37.6 us -> 37.3 us (level)
  blocking collectives: 12.3 us -> 10.6 us
  waiting for transfers between devices: 4.94 us -> 6.42 us
    all_to_all x1, waiting for transfers between devices: 0.01 us -> 2 us  [swap(): lax.all_to_all(parts, axes, split_axis=0, concat_axis=0, tiled=True, axis...]
    all_to_all x1, blocking collectives: 12.3 us -> 10.6 us  [swap(): lax.all_to_all(parts, axes, split_axis=0, concat_axis=0, tiled=True, axis...]
    ppermute x1, waiting for transfers between devices: 3.73 us -> 3.2 us  [body(): cots = [own, lax.ppermute(other, 'head', [(0, 1), (1, 0)])]]
  transfers between devices with their start and end apart: 5 -> 5, of which waited for: 2 -> 3; matrix products, arithmetic and copies ran while one was open for 2% -> 2% of each run, Pallas kernels for 12% -> 12%
where the time goes in v8:
time: 37.3 us; the launch traced here: 36.9 us
  starting transfers between devices  11 us (29%)
  blocking collectives  10.6 us (28%)
  Pallas kernels  7.37 us (20%)
  waiting for transfers between devices  6.42 us (17%)
  local copies, waits for them, and re-layouts  1.38 us (4%)
    all_to_all x1, blocking collectives, swap(): lax.all_to_all(parts, axes, split_axis=0, concat_axis=0, tiled=True, axis...  10.6 us
    all_to_all x1, starting transfers between devices, swap(): lax.all_to_all(parts, axes, split_axis=0, concat_axis=0, tiled=True, axis...  8.92 us
    pallas_call x10, Pallas kernels, call(): pl.pallas_call(kernel, out_shape=shapes[0] if single else shapes, in_spec...  7.37 us
    ppermute x1, waiting for transfers between devices, body(): cots = [own, lax.ppermute(other, 'head', [(0, 1), (1, 0)])]  3.2 us
    all_to_all x1, waiting for transfers between devices, swap(): lax.all_to_all(parts, axes, split_axis=0, concat_axis=0, tiled=True, axis...  2 us
    ppermute x1, starting transfers between devices, body(): cots = [own, lax.ppermute(other, 'head', [(0, 1), (1, 0)])]  1.53 us
    ppermute x3, waiting for transfers between devices, to_pair(): return lax.ppermute(x, 'tile', [(t, t ^ 1) for t in range(tiles)])  1.21 us
  transfers between devices with their start and end apart: 5, of which 3 were waited for; matrix products, arithmetic and copies ran while one was open for 2% of the time, Pallas kernels for 12%

profile of v8, /device:TPU:0, one launch (start us, length us, event | category | flops | bytes accessed | tf_op | source)
XLA Modules:
  0.0 36.9 jit_solution(8211992241947578724)
XLA Ops:
  0.0 0.0 copy-start.1
  0.0 0.5 %collective-permute-start = (bf16[128,768]{1,0:T(8,128)(2,1)}, bf16[128,768]{1,0:T(8,128)(2,1)S(1)}, u32[]{:S(2)}, u32[]{:S(2)}) collective-permute-start(bf16[128,768]{1,0:T(8,128)(2,1)} %bitcast.14), channel_id=1, source_target_pairs={{0,2},{2,0},{4,6},{6,4},{8,10},{10,8},{12,14},{14,12},{16,18},{18,... | collective-permute-start | bytes 589832 | tf_op jit(solution)/shard_map/ppermute | solution.py:450
  0.5 0.1 collective-permute-start.1
  0.5 1.0 %shard_map.46 = (f32[16,128]{1,0:T(8,128)S(1)}, f32[16,128]{1,0:T(8,128)S(1)}, bf16[256,256]{1,0:T(8,128)(2,1)S(1)}) custom-call(s32[3,16]{1,0:T(4,128)} %pos_ref.1, s32[4,128]{1,0:T(4,128)} %bitcast.16), custom_call_target="tpu_custom_call" | custom-call | tf_op jit(solution)/shard_map/pallas_call | solution.py:423
  1.5 2.9 %shard_map.47 = (bf16[128,512]{1,0:T(8,128)(2,1)S(1)}, bf16[128,512]{1,0:T(8,128)(2,1)S(1)}, f32[128,128]{1,0:T(8,128)S(1)}, f32[128,128]{1,0:T(8,128)S(1)}, bf1...) custom-call(bf16[256,512]{1,0:T(8,128)(2,1)} %bitcast.12, s32[3,16]{1,0:T(4,128)} %pos_ref.1, ...), custom_call_target="tpu_custom_call" | custom-call | tf_op jit(solution)/shard_map/pallas_call | solution.py:423
  4.4 0.0 collective-permute-done.1.refs_1_
  4.5 0.0 collective-permute-done.refs_0_
  4.5 0.0 copy-done.1
  4.5 1.3 %shard_map.48 = bf16[256,768]{1,0:T(8,128)(2,1)} custom-call(bf16[128,768]{1,0:T(8,128)(2,1)S(1)} %bitcast.15, f32[16,128]{1,0:T(8,128)S(1)} %get-tuple-element.22.cos_ref, f32[16,128]{1,0:T(8,128)S(1)} %get-tuple-element.23.sin_ref, bf16[256,256]{1,0:T(8,128)(2,1)S(1)} %get-tuple-element.24.place_ref, bf16[16,128]{1,0:T(8,128)(2,1)S(1)} %slice.6.after_ref, ...), custom_call_target="tpu_custom_call" | custom-call | tf_op jit(solution)/shard_map/pallas_call | solution.py:423
  5.8 0.0 copy-start
  5.8 8.9 %all-to-all-start = ((bf16[16,16,768]{2,1,0:T(8,128)(2,1)}), bf16[16,16,768]{2,1,0:T(8,128)(2,1)S(1)}, u32[]{:S(2)}, u32[]{:S(2)}) async-start(bf16[16,16,768]{2,1,0:T(8,128)(2,1)} %bitcast.3), calls=%async_computation | async-start | bytes 786432 | tf_op jit(solution)/shard_map/all_to_all | solution.py:516
  14.7 0.0 copy-done
  14.8 1.5 %collective-permute-start.2 = (bf16[128,512]{1,0:T(8,128)(2,1)S(1)}, bf16[128,512]{1,0:T(8,128)(2,1)S(1)}, u32[]{:S(2)}, u32[]{:S(2)}) collective-permute-start(bf16[128,512]{1,0:T(8,128)(2,1)S(1)} %get-tuple-element.37), channel_id=1, source_target_pairs={{0,1},{1,0},{2,3},{3,2},{4,5},{5,4},{6,7},{7,6},{8,9},{9,8},{10,11... | collective-permute-start | bytes 393224 | tf_op jit(solution)/shard_map/ppermute | solution.py:524
  16.3 0.7 %slice.8.after_ref = bf16[16,128]{1,0:T(8,128)(2,1)S(1)} slice(bf16[256,768]{1,0:T(8,128)(2,1)} %shard_map.48), slice={[0:16], [0:128]} | slice | bytes 8192 | tf_op jit(solution)/shard_map/slice | solution.py:533
  17.0 0.0 copy-start.3
  17.0 0.0 copy-start.2
  17.0 0.7 %copy-done.3 = s32[512,1]{0,1:T(1,128)S(1)} copy-done((s32[512,1]{0,1:T(1,128)S(1)}, s32[512,1]{0,1:T(1,128)}, u32[]{:S(2)}) %copy-start.3) | copy-done | bytes 2072
  17.7 0.0 copy-done.2
  17.7 3.2 %collective-permute-done.2.refs_1_ = bf16[128,512]{1,0:T(8,128)(2,1)S(1)} collective-permute-done((bf16[128,512]{1,0:T(8,128)(2,1)S(1)}, bf16[128,512]{1,0:T(8,128)(2,1)S(1)}, u32[]{:S(2)}, u32[]{:S(2)}) %collective-permute-start.2) | collective-permute-done | bytes 131104 | tf_op jit(solution)/shard_map/ppermute | solution.py:524
  20.9 0.2 shard_map.51.cot_ref
  21.1 2.0 %all-to-all-done = bf16[16,16,768]{2,1,0:T(8,128)(2,1)S(1)} async-done(((bf16[16,16,768]{2,1,0:T(8,128)(2,1)}), bf16[16,16,768]{2,1,0:T(8,128)(2,1)S(1)}, u32[]{:S(2)}, u32[]{:S(2)}) %all-to-all-start) | async-done | bytes 393248 | tf_op jit(solution)/shard_map/all_to_all | solution.py:516
  23.2 0.6 %shard_map.52 = bf16[256,768]{1,0:T(8,128)(2,1)S(1)} custom-call(bf16[256,768]{1,0:T(8,128)(2,1)S(1)} %bitcast.10, f32[64,256]{1,0:T(8,128)S(1)} %get-tuple-element.33.bias_ref, bf16[1024,128]{1,0:T(8,128)(2,1)S(1)} %shard_map.51.cot_ref), custom_call_target="tpu_custom_call" | custom-call | tf_op jit(solution)/shard_map/pallas_call | solution.py:423
  23.8 10.6 %all_to_all.10 = bf16[16,16,768]{2,1,0:T(8,128)(2,1)S(1)} all-to-all(bf16[16,16,768]{2,1,0:T(8,128)(2,1)S(1)} %bitcast.11), channel_id=1, replica_groups={{16,8,0,24,20,12,4,28,17,9,1,25,21,13,5,29},{18,10,2,26,22,14,6,30,19,1..., dimensions={0} | all-to-all | bytes 786432 | tf_op jit(solution)/shard_map/all_to_all | solution.py:516
  34.4 0.2 shard_map.53
  34.6 0.1 collective-permute-start.3
  34.7 0.2 shard_map.54.refs_1_
  34.9 1.2 %collective-permute-done.3.refs_0_ = bf16[128,768]{1,0:T(8,128)(2,1)S(1)} collective-permute-done((bf16[128,768]{1,0:T(8,128)(2,1)S(1)}, bf16[128,768]{1,0:T(8,128)(2,1)S(1)}, u32[]{:S(2)}, u32[]{:S(2)}) %collective-permute-start.3) | collective-permute-done | bytes 196640 | tf_op jit(solution)/shard_map/ppermute | solution.py:450
  36.1 0.8 %shard_map.55 = bf16[128,768]{1,0:T(8,128)(2,1)} custom-call(f32[128,128]{1,0:T(8,128)S(1)} %get-tuple-element.31.cos_ref, f32[128,128]{1,0:T(8,128)S(1)} %get-tuple-element.32.sin_ref, bf16[128,768]{1,0:T(8,128)(2,1)S(1)} %collective-permute-done.3.refs_0_, bf16[128,768]{1,0:T(8,128)(2,1)S(1)} %shard_map.54.refs_1_), custom_call_target="tpu_custom_call" | custom-call | tf_op jit(solution)/shard_map/pallas_call | solution.py:423
  (3 shorter events, 0.1 us)
Async XLA Ops:
  0.0 4.5 %copy-start.1 = (bf16[16,8,768]{2,1,0:T(8,128)(2,1)S(1)}, bf16[16,8,768]{2,1,0:T(8,128)(2,1)}, u32[]{:S(2)}) copy-start(bf16[16,8,768]{2,1,0:T(8,128)(2,1)} %param.4) | copy-start | bytes 589828
  0.0 4.5 %collective-permute-start = (bf16[128,768]{1,0:T(8,128)(2,1)}, bf16[128,768]{1,0:T(8,128)(2,1)S(1)}, u32[]{:S(2)}, u32[]{:S(2)}) collective-permute-start(bf16[128,768]{1,0:T(8,128)(2,1)} %bitcast.14), channel_id=1, source_target_pairs={{0,2},{2,0},{4,6},{6,4},{8,10},{10,8},{12,14},{14,12},{16,18},{18,... | collective-permute-start | bytes 589832 | tf_op jit(solution)/shard_map/ppermute | solution.py:450
  0.5 4.0 %collective-permute-start.1 = (s32[3,16]{1,0:T(4,128)}, s32[3,16]{1,0:T(4,128)S(1)}, u32[]{:S(2)}, u32[]{:S(2)}) collective-permute-start(s32[3,16]{1,0:T(4,128)} %pos_ref.1), channel_id=1, source_target_pairs={{0,2},{2,0},{4,6},{6,4},{8,10},{10,8},{12,14},{14,12},{16,18},{18,... | collective-permute-start | bytes 584 | tf_op jit(solution)/shard_map/ppermute | solution.py:450
  5.8 8.9 %copy-start = (bf16[32,8,512]{2,1,0:T(8,128)(2,1)S(1)}, bf16[32,8,512]{2,1,0:T(8,128)(2,1)}, u32[]{:S(2)}) copy-start(bf16[32,8,512]{2,1,0:T(8,128)(2,1)} %param.7) | copy-start | bytes 786436
  5.8 17.4 %all-to-all-start = ((bf16[16,16,768]{2,1,0:T(8,128)(2,1)}), bf16[16,16,768]{2,1,0:T(8,128)(2,1)S(1)}, u32[]{:S(2)}, u32[]{:S(2)}) async-start(bf16[16,16,768]{2,1,0:T(8,128)(2,1)} %bitcast.3), calls=%async_computation | async-start | bytes 786432 | tf_op jit(solution)/shard_map/all_to_all | solution.py:516
  14.8 6.1 %collective-permute-start.2 = (bf16[128,512]{1,0:T(8,128)(2,1)S(1)}, bf16[128,512]{1,0:T(8,128)(2,1)S(1)}, u32[]{:S(2)}, u32[]{:S(2)}) collective-permute-start(bf16[128,512]{1,0:T(8,128)(2,1)S(1)} %get-tuple-element.37), channel_id=1, source_target_pairs={{0,1},{1,0},{2,3},{3,2},{4,5},{5,4},{6,7},{7,6},{8,9},{9,8},{10,11... | collective-permute-start | bytes 393224 | tf_op jit(solution)/shard_map/ppermute | solution.py:524
  17.0 0.7 %copy-start.3 = (s32[512,1]{0,1:T(1,128)S(1)}, s32[512,1]{0,1:T(1,128)}, u32[]{:S(2)}) copy-start(s32[512,1]{0,1:T(1,128)} %param.6) | copy-start | bytes 6148
  17.0 0.7 %copy-start.2 = (s32[3,16]{1,0:T(4,128)S(1)}, s32[3,16]{1,0:T(4,128)}, u32[]{:S(2)}) copy-start(s32[3,16]{1,0:T(4,128)} %pos_ref.1) | copy-start | bytes 580
  34.6 1.5 %collective-permute-start.3 = (bf16[128,768]{1,0:T(8,128)(2,1)S(1)}, bf16[128,768]{1,0:T(8,128)(2,1)S(1)}, u32[]{:S(2)}, u32[]{:S(2)}) collective-permute-start(bf16[128,768]{1,0:T(8,128)(2,1)S(1)} %shard_map.53), channel_id=1, source_target_pairs={{0,2},{2,0},{4,6},{6,4},{8,10},{10,8},{12,14},{14,12},{16,18},{18,... | collective-permute-start | bytes 589832 | tf_op jit(solution)/shard_map/ppermute | solution.py:450

commit v9 on v8

--- a/solution.py
+++ b/solution.py
@@ -109,7 +109,7 @@
     if sides == 1:
         return list(range(units))
     if back and units == 8:
-        return [z * 2 + y for y in (0, 1) for z in (2, 1, 0, 3)]
+        return [z * 2 for z in (2, 1, 0, 3)] + [z * 2 + 1 for z in (3, 2, 1, 0)]
     return [(n + units // 2) % units for n in range(units)]
 
 

time: 37.3 us -> 37.1 us (level)
  no operation moved by 1% of the time
where the time goes in v9:
time: 37.1 us; the launch traced here: 36.7 us
  starting transfers between devices  11 us (30%)
  blocking collectives  10.4 us (28%)
  Pallas kernels  7.37 us (20%)
  waiting for transfers between devices  6.42 us (17%)
  local copies, waits for them, and re-layouts  1.38 us (4%)
    all_to_all x1, blocking collectives, swap(): lax.all_to_all(parts, axes, split_axis=0, concat_axis=0, tiled=True, axis...  10.4 us
    all_to_all x1, starting transfers between devices, swap(): lax.all_to_all(parts, axes, split_axis=0, concat_axis=0, tiled=True, axis...  8.92 us
    pallas_call x10, Pallas kernels, call(): pl.pallas_call(kernel, out_shape=shapes[0] if single else shapes, in_spec...  7.37 us
    ppermute x1, waiting for transfers between devices, body(): cots = [own, lax.ppermute(other, 'head', [(0, 1), (1, 0)])]  3.2 us
    all_to_all x1, waiting for transfers between devices, swap(): lax.all_to_all(parts, axes, split_axis=0, concat_axis=0, tiled=True, axis...  2 us
    ppermute x1, starting transfers between devices, body(): cots = [own, lax.ppermute(other, 'head', [(0, 1), (1, 0)])]  1.53 us
    ppermute x3, waiting for transfers between devices, to_pair(): return lax.ppermute(x, 'tile', [(t, t ^ 1) for t in range(tiles)])  1.21 us
  transfers between devices with their start and end apart: 5, of which 3 were waited for; matrix products, arithmetic and copies ran while one was open for 2% of the time, Pallas kernels for 12%

profile of v9, /device:TPU:0, one launch (start us, length us, event | category | flops | bytes accessed | tf_op | source)
XLA Modules:
  0.0 36.7 jit_solution(4955899603683881102)
XLA Ops:
  0.0 0.0 copy-start.1
  0.0 0.5 %collective-permute-start = (bf16[128,768]{1,0:T(8,128)(2,1)}, bf16[128,768]{1,0:T(8,128)(2,1)S(1)}, u32[]{:S(2)}, u32[]{:S(2)}) collective-permute-start(bf16[128,768]{1,0:T(8,128)(2,1)} %bitcast.14), channel_id=1, source_target_pairs={{0,2},{2,0},{4,6},{6,4},{8,10},{10,8},{12,14},{14,12},{16,18},{18,... | collective-permute-start | bytes 589832 | tf_op jit(solution)/shard_map/ppermute | solution.py:450
  0.5 0.1 collective-permute-start.1
  0.5 1.0 %shard_map.46 = (f32[16,128]{1,0:T(8,128)S(1)}, f32[16,128]{1,0:T(8,128)S(1)}, bf16[256,256]{1,0:T(8,128)(2,1)S(1)}) custom-call(s32[3,16]{1,0:T(4,128)} %pos_ref.1, s32[4,128]{1,0:T(4,128)} %bitcast.16), custom_call_target="tpu_custom_call" | custom-call | tf_op jit(solution)/shard_map/pallas_call | solution.py:423
  1.5 2.9 %shard_map.47 = (bf16[128,512]{1,0:T(8,128)(2,1)S(1)}, bf16[128,512]{1,0:T(8,128)(2,1)S(1)}, f32[128,128]{1,0:T(8,128)S(1)}, f32[128,128]{1,0:T(8,128)S(1)}, bf1...) custom-call(bf16[256,512]{1,0:T(8,128)(2,1)} %bitcast.12, s32[3,16]{1,0:T(4,128)} %pos_ref.1, ...), custom_call_target="tpu_custom_call" | custom-call | tf_op jit(solution)/shard_map/pallas_call | solution.py:423
  4.4 0.0 collective-permute-done.1.refs_1_
  4.5 0.0 collective-permute-done.refs_0_
  4.5 0.0 copy-done.1
  4.5 1.3 %shard_map.48 = bf16[256,768]{1,0:T(8,128)(2,1)} custom-call(bf16[128,768]{1,0:T(8,128)(2,1)S(1)} %bitcast.15, f32[16,128]{1,0:T(8,128)S(1)} %get-tuple-element.22.cos_ref, f32[16,128]{1,0:T(8,128)S(1)} %get-tuple-element.23.sin_ref, bf16[256,256]{1,0:T(8,128)(2,1)S(1)} %get-tuple-element.24.place_ref, bf16[16,128]{1,0:T(8,128)(2,1)S(1)} %slice.6.after_ref, ...), custom_call_target="tpu_custom_call" | custom-call | tf_op jit(solution)/shard_map/pallas_call | solution.py:423
  5.8 0.0 copy-start
  5.8 8.9 %all-to-all-start = ((bf16[16,16,768]{2,1,0:T(8,128)(2,1)}), bf16[16,16,768]{2,1,0:T(8,128)(2,1)S(1)}, u32[]{:S(2)}, u32[]{:S(2)}) async-start(bf16[16,16,768]{2,1,0:T(8,128)(2,1)} %bitcast.3), calls=%async_computation | async-start | bytes 786432 | tf_op jit(solution)/shard_map/all_to_all | solution.py:516
  14.7 0.0 copy-done
  14.8 1.5 %collective-permute-start.2 = (bf16[128,512]{1,0:T(8,128)(2,1)S(1)}, bf16[128,512]{1,0:T(8,128)(2,1)S(1)}, u32[]{:S(2)}, u32[]{:S(2)}) collective-permute-start(bf16[128,512]{1,0:T(8,128)(2,1)S(1)} %get-tuple-element.37), channel_id=1, source_target_pairs={{0,1},{1,0},{2,3},{3,2},{4,5},{5,4},{6,7},{7,6},{8,9},{9,8},{10,11... | collective-permute-start | bytes 393224 | tf_op jit(solution)/shard_map/ppermute | solution.py:524
  16.3 0.7 %slice.8.after_ref = bf16[16,128]{1,0:T(8,128)(2,1)S(1)} slice(bf16[256,768]{1,0:T(8,128)(2,1)} %shard_map.48), slice={[0:16], [0:128]} | slice | bytes 8192 | tf_op jit(solution)/shard_map/slice | solution.py:533
  17.0 0.0 copy-start.3
  17.0 0.0 copy-start.2
  17.0 0.7 %copy-done.3 = s32[512,1]{0,1:T(1,128)S(1)} copy-done((s32[512,1]{0,1:T(1,128)S(1)}, s32[512,1]{0,1:T(1,128)}, u32[]{:S(2)}) %copy-start.3) | copy-done | bytes 2072
  17.7 0.0 copy-done.2
  17.7 3.2 %collective-permute-done.2.refs_1_ = bf16[128,512]{1,0:T(8,128)(2,1)S(1)} collective-permute-done((bf16[128,512]{1,0:T(8,128)(2,1)S(1)}, bf16[128,512]{1,0:T(8,128)(2,1)S(1)}, u32[]{:S(2)}, u32[]{:S(2)}) %collective-permute-start.2) | collective-permute-done | bytes 131104 | tf_op jit(solution)/shard_map/ppermute | solution.py:524
  20.9 0.2 shard_map.51.cot_ref
  21.1 2.0 %all-to-all-done = bf16[16,16,768]{2,1,0:T(8,128)(2,1)S(1)} async-done(((bf16[16,16,768]{2,1,0:T(8,128)(2,1)}), bf16[16,16,768]{2,1,0:T(8,128)(2,1)S(1)}, u32[]{:S(2)}, u32[]{:S(2)}) %all-to-all-start) | async-done | bytes 393248 | tf_op jit(solution)/shard_map/all_to_all | solution.py:516
  23.2 0.6 %shard_map.52 = bf16[256,768]{1,0:T(8,128)(2,1)S(1)} custom-call(bf16[256,768]{1,0:T(8,128)(2,1)S(1)} %bitcast.10, f32[64,256]{1,0:T(8,128)S(1)} %get-tuple-element.33.bias_ref, bf16[1024,128]{1,0:T(8,128)(2,1)S(1)} %shard_map.51.cot_ref), custom_call_target="tpu_custom_call" | custom-call | tf_op jit(solution)/shard_map/pallas_call | solution.py:423
  23.8 10.4 %all_to_all.10 = bf16[16,16,768]{2,1,0:T(8,128)(2,1)S(1)} all-to-all(bf16[16,16,768]{2,1,0:T(8,128)(2,1)S(1)} %bitcast.11), channel_id=1, replica_groups={{16,8,0,24,28,20,12,4,17,9,1,25,29,21,13,5},{18,10,2,26,30,22,14,6,19,1..., dimensions={0} | all-to-all | bytes 786432 | tf_op jit(solution)/shard_map/all_to_all | solution.py:516
  34.2 0.2 shard_map.53
  34.4 0.1 collective-permute-start.3
  34.5 0.2 shard_map.54.refs_1_
  34.7 1.2 %collective-permute-done.3.refs_0_ = bf16[128,768]{1,0:T(8,128)(2,1)S(1)} collective-permute-done((bf16[128,768]{1,0:T(8,128)(2,1)S(1)}, bf16[128,768]{1,0:T(8,128)(2,1)S(1)}, u32[]{:S(2)}, u32[]{:S(2)}) %collective-permute-start.3) | collective-permute-done | bytes 196640 | tf_op jit(solution)/shard_map/ppermute | solution.py:450
  35.9 0.8 %shard_map.55 = bf16[128,768]{1,0:T(8,128)(2,1)} custom-call(f32[128,128]{1,0:T(8,128)S(1)} %get-tuple-element.31.cos_ref, f32[128,128]{1,0:T(8,128)S(1)} %get-tuple-element.32.sin_ref, bf16[128,768]{1,0:T(8,128)(2,1)S(1)} %collective-permute-done.3.refs_0_, bf16[128,768]{1,0:T(8,128)(2,1)S(1)} %shard_map.54.refs_1_), custom_call_target="tpu_custom_call" | custom-call | tf_op jit(solution)/shard_map/pallas_call | solution.py:423
  (3 shorter events, 0.1 us)
Async XLA Ops:
  0.0 4.5 %copy-start.1 = (bf16[16,8,768]{2,1,0:T(8,128)(2,1)S(1)}, bf16[16,8,768]{2,1,0:T(8,128)(2,1)}, u32[]{:S(2)}) copy-start(bf16[16,8,768]{2,1,0:T(8,128)(2,1)} %param.4) | copy-start | bytes 589828
  0.0 4.5 %collective-permute-start = (bf16[128,768]{1,0:T(8,128)(2,1)}, bf16[128,768]{1,0:T(8,128)(2,1)S(1)}, u32[]{:S(2)}, u32[]{:S(2)}) collective-permute-start(bf16[128,768]{1,0:T(8,128)(2,1)} %bitcast.14), channel_id=1, source_target_pairs={{0,2},{2,0},{4,6},{6,4},{8,10},{10,8},{12,14},{14,12},{16,18},{18,... | collective-permute-start | bytes 589832 | tf_op jit(solution)/shard_map/ppermute | solution.py:450
  0.5 4.0 %collective-permute-start.1 = (s32[3,16]{1,0:T(4,128)}, s32[3,16]{1,0:T(4,128)S(1)}, u32[]{:S(2)}, u32[]{:S(2)}) collective-permute-start(s32[3,16]{1,0:T(4,128)} %pos_ref.1), channel_id=1, source_target_pairs={{0,2},{2,0},{4,6},{6,4},{8,10},{10,8},{12,14},{14,12},{16,18},{18,... | collective-permute-start | bytes 584 | tf_op jit(solution)/shard_map/ppermute | solution.py:450
  5.8 8.9 %copy-start = (bf16[32,8,512]{2,1,0:T(8,128)(2,1)S(1)}, bf16[32,8,512]{2,1,0:T(8,128)(2,1)}, u32[]{:S(2)}) copy-start(bf16[32,8,512]{2,1,0:T(8,128)(2,1)} %param.7) | copy-start | bytes 786436
  5.8 17.4 %all-to-all-start = ((bf16[16,16,768]{2,1,0:T(8,128)(2,1)}), bf16[16,16,768]{2,1,0:T(8,128)(2,1)S(1)}, u32[]{:S(2)}, u32[]{:S(2)}) async-start(bf16[16,16,768]{2,1,0:T(8,128)(2,1)} %bitcast.3), calls=%async_computation | async-start | bytes 786432 | tf_op jit(solution)/shard_map/all_to_all | solution.py:516
  14.8 6.1 %collective-permute-start.2 = (bf16[128,512]{1,0:T(8,128)(2,1)S(1)}, bf16[128,512]{1,0:T(8,128)(2,1)S(1)}, u32[]{:S(2)}, u32[]{:S(2)}) collective-permute-start(bf16[128,512]{1,0:T(8,128)(2,1)S(1)} %get-tuple-element.37), channel_id=1, source_target_pairs={{0,1},{1,0},{2,3},{3,2},{4,5},{5,4},{6,7},{7,6},{8,9},{9,8},{10,11... | collective-permute-start | bytes 393224 | tf_op jit(solution)/shard_map/ppermute | solution.py:524
  17.0 0.7 %copy-start.3 = (s32[512,1]{0,1:T(1,128)S(1)}, s32[512,1]{0,1:T(1,128)}, u32[]{:S(2)}) copy-start(s32[512,1]{0,1:T(1,128)} %param.6) | copy-start | bytes 6148
  17.0 0.7 %copy-start.2 = (s32[3,16]{1,0:T(4,128)S(1)}, s32[3,16]{1,0:T(4,128)}, u32[]{:S(2)}) copy-start(s32[3,16]{1,0:T(4,128)} %pos_ref.1) | copy-start | bytes 580
  34.4 1.5 %collective-permute-start.3 = (bf16[128,768]{1,0:T(8,128)(2,1)S(1)}, bf16[128,768]{1,0:T(8,128)(2,1)S(1)}, u32[]{:S(2)}, u32[]{:S(2)}) collective-permute-start(bf16[128,768]{1,0:T(8,128)(2,1)S(1)} %shard_map.53), channel_id=1, source_target_pairs={{0,2},{2,0},{4,6},{6,4},{8,10},{10,8},{12,14},{14,12},{16,18},{18,... | collective-permute-start | bytes 589832 | tf_op jit(solution)/shard_map/ppermute | solution.py:450

commit v10 on v9

--- a/solution.py
+++ b/solution.py
@@ -249,14 +249,12 @@
     def _():
         pairs = ((dest_hbm, dest_ref), (pos_hbm, pos_ref), (cot_hbm, cot_ref))
         loads = [pltpu.make_async_copy(a, b, sems.at[n]) for n, (a, b) in enumerate(pairs)]
-        for load in loads[:2]:
+        for load in loads:
             load.start()
-        for load in loads[:2]:
+        for load in loads:
             load.wait()
+        split_cots(cot_ref, *out_refs[:2], local)
         fill_tables(pos_ref, dest_ref, out_refs[2:], tiles, heads, local, sides)
-        loads[2].start()
-        loads[2].wait()
-        split_cots(cot_ref, *out_refs[:2], local)
 
 
 def table_kernel(pos_ref, dest_ref, after_ref, *refs, tiles, heads, local, sides):

time: 37.1 us -> 37.1 us (level)
  Pallas kernels: 7.37 us -> 6.8 us
  waiting for transfers between devices: 6.42 us -> 6.99 us
    pallas_call x10, Pallas kernels: 7.37 us -> 6.8 us  [call(): pl.pallas_call(kernel, out_shape=shapes[0] if single else shapes, in_spec...]
    ppermute x1, waiting for transfers between devices: 3.2 us -> 3.67 us  [body(): cots = [own, lax.ppermute(other, 'head', [(0, 1), (1, 0)])]]
  transfers between devices with their start and end apart: 5 -> 5, of which waited for: 3 -> 3; matrix products, arithmetic and copies ran while one was open for 2% -> 2% of each run, Pallas kernels for 12% -> 10%
where the time goes in v10:
time: 37.1 us; the launch traced here: 36.7 us
  starting transfers between devices  11 us (30%)
  blocking collectives  10.4 us (28%)
  waiting for transfers between devices  6.99 us (19%)
  Pallas kernels  6.8 us (18%)
  local copies, waits for them, and re-layouts  1.38 us (4%)
    all_to_all x1, blocking collectives, swap(): lax.all_to_all(parts, axes, split_axis=0, concat_axis=0, tiled=True, axis...  10.4 us
    all_to_all x1, starting transfers between devices, swap(): lax.all_to_all(parts, axes, split_axis=0, concat_axis=0, tiled=True, axis...  8.92 us
    pallas_call x10, Pallas kernels, call(): pl.pallas_call(kernel, out_shape=shapes[0] if single else shapes, in_spec...  6.8 us
    ppermute x1, waiting for transfers between devices, body(): cots = [own, lax.ppermute(other, 'head', [(0, 1), (1, 0)])]  3.67 us
    all_to_all x1, waiting for transfers between devices, swap(): lax.all_to_all(parts, axes, split_axis=0, concat_axis=0, tiled=True, axis...  2.11 us
    ppermute x1, starting transfers between devices, body(): cots = [own, lax.ppermute(other, 'head', [(0, 1), (1, 0)])]  1.53 us
    ppermute x3, waiting for transfers between devices, to_pair(): return lax.ppermute(x, 'tile', [(t, t ^ 1) for t in range(tiles)])  1.21 us
  transfers between devices with their start and end apart: 5, of which 3 were waited for; matrix products, arithmetic and copies ran while one was open for 2% of the time, Pallas kernels for 10%

profile of v10, /device:TPU:0, one launch (start us, length us, event | category | flops | bytes accessed | tf_op | source)
XLA Modules:
  0.0 36.7 jit_solution(9109776156760120202)
XLA Ops:
  0.0 0.0 copy-start.1
  0.0 0.5 %collective-permute-start = (bf16[128,768]{1,0:T(8,128)(2,1)}, bf16[128,768]{1,0:T(8,128)(2,1)S(1)}, u32[]{:S(2)}, u32[]{:S(2)}) collective-permute-start(bf16[128,768]{1,0:T(8,128)(2,1)} %bitcast.14), channel_id=1, source_target_pairs={{0,2},{2,0},{4,6},{6,4},{8,10},{10,8},{12,14},{14,12},{16,18},{18,... | collective-permute-start | bytes 589832 | tf_op jit(solution)/shard_map/ppermute | solution.py:448
  0.5 0.1 collective-permute-start.1
  0.5 1.0 %shard_map.46 = (f32[16,128]{1,0:T(8,128)S(1)}, f32[16,128]{1,0:T(8,128)S(1)}, bf16[256,256]{1,0:T(8,128)(2,1)S(1)}) custom-call(s32[3,16]{1,0:T(4,128)} %pos_ref.1, s32[4,128]{1,0:T(4,128)} %bitcast.16), custom_call_target="tpu_custom_call" | custom-call | tf_op jit(solution)/shard_map/pallas_call | solution.py:421
  1.5 2.3 %shard_map.47 = (bf16[128,512]{1,0:T(8,128)(2,1)S(1)}, bf16[128,512]{1,0:T(8,128)(2,1)S(1)}, f32[128,128]{1,0:T(8,128)S(1)}, f32[128,128]{1,0:T(8,128)S(1)}, bf1...) custom-call(bf16[256,512]{1,0:T(8,128)(2,1)} %bitcast.12, s32[3,16]{1,0:T(4,128)} %pos_ref.1, ...), custom_call_target="tpu_custom_call" | custom-call | tf_op jit(solution)/shard_map/pallas_call | solution.py:421
  3.9 0.0 collective-permute-done.1.refs_1_
  3.9 0.0 collective-permute-done.refs_0_
  3.9 0.0 copy-done.1
  3.9 1.3 %shard_map.48 = bf16[256,768]{1,0:T(8,128)(2,1)} custom-call(bf16[128,768]{1,0:T(8,128)(2,1)S(1)} %bitcast.15, f32[16,128]{1,0:T(8,128)S(1)} %get-tuple-element.22.cos_ref, f32[16,128]{1,0:T(8,128)S(1)} %get-tuple-element.23.sin_ref, bf16[256,256]{1,0:T(8,128)(2,1)S(1)} %get-tuple-element.24.place_ref, bf16[16,128]{1,0:T(8,128)(2,1)S(1)} %slice.6.after_ref, ...), custom_call_target="tpu_custom_call" | custom-call | tf_op jit(solution)/shard_map/pallas_call | solution.py:421
  5.2 0.0 copy-start
  5.2 8.9 %all-to-all-start = ((bf16[16,16,768]{2,1,0:T(8,128)(2,1)}), bf16[16,16,768]{2,1,0:T(8,128)(2,1)S(1)}, u32[]{:S(2)}, u32[]{:S(2)}) async-start(bf16[16,16,768]{2,1,0:T(8,128)(2,1)} %bitcast.3), calls=%async_computation | async-start | bytes 786432 | tf_op jit(solution)/shard_map/all_to_all | solution.py:514
  14.2 0.0 copy-done
  14.2 1.5 %collective-permute-start.2 = (bf16[128,512]{1,0:T(8,128)(2,1)S(1)}, bf16[128,512]{1,0:T(8,128)(2,1)S(1)}, u32[]{:S(2)}, u32[]{:S(2)}) collective-permute-start(bf16[128,512]{1,0:T(8,128)(2,1)S(1)} %get-tuple-element.37), channel_id=1, source_target_pairs={{0,1},{1,0},{2,3},{3,2},{4,5},{5,4},{6,7},{7,6},{8,9},{9,8},{10,11... | collective-permute-start | bytes 393224 | tf_op jit(solution)/shard_map/ppermute | solution.py:522
  15.7 0.7 %slice.8.after_ref = bf16[16,128]{1,0:T(8,128)(2,1)S(1)} slice(bf16[256,768]{1,0:T(8,128)(2,1)} %shard_map.48), slice={[0:16], [0:128]} | slice | bytes 8192 | tf_op jit(solution)/shard_map/slice | solution.py:531
  16.4 0.0 copy-start.3
  16.4 0.0 copy-start.2
  16.4 0.7 %copy-done.3 = s32[512,1]{0,1:T(1,128)S(1)} copy-done((s32[512,1]{0,1:T(1,128)S(1)}, s32[512,1]{0,1:T(1,128)}, u32[]{:S(2)}) %copy-start.3) | copy-done | bytes 2072
  17.1 0.0 copy-done.2
  17.1 3.7 %collective-permute-done.2.refs_1_ = bf16[128,512]{1,0:T(8,128)(2,1)S(1)} collective-permute-done((bf16[128,512]{1,0:T(8,128)(2,1)S(1)}, bf16[128,512]{1,0:T(8,128)(2,1)S(1)}, u32[]{:S(2)}, u32[]{:S(2)}) %collective-permute-start.2) | collective-permute-done | bytes 131104 | tf_op jit(solution)/shard_map/ppermute | solution.py:522
  20.8 0.2 shard_map.51.cot_ref
  21.0 2.1 %all-to-all-done = bf16[16,16,768]{2,1,0:T(8,128)(2,1)S(1)} async-done(((bf16[16,16,768]{2,1,0:T(8,128)(2,1)}), bf16[16,16,768]{2,1,0:T(8,128)(2,1)S(1)}, u32[]{:S(2)}, u32[]{:S(2)}) %all-to-all-start) | async-done | bytes 393248 | tf_op jit(solution)/shard_map/all_to_all | solution.py:514
  23.2 0.6 %shard_map.52 = bf16[256,768]{1,0:T(8,128)(2,1)S(1)} custom-call(bf16[256,768]{1,0:T(8,128)(2,1)S(1)} %bitcast.10, f32[64,256]{1,0:T(8,128)S(1)} %get-tuple-element.33.bias_ref, bf16[1024,128]{1,0:T(8,128)(2,1)S(1)} %shard_map.51.cot_ref), custom_call_target="tpu_custom_call" | custom-call | tf_op jit(solution)/shard_map/pallas_call | solution.py:421
  23.8 10.4 %all_to_all.10 = bf16[16,16,768]{2,1,0:T(8,128)(2,1)S(1)} all-to-all(bf16[16,16,768]{2,1,0:T(8,128)(2,1)S(1)} %bitcast.11), channel_id=1, replica_groups={{16,8,0,24,28,20,12,4,17,9,1,25,29,21,13,5},{18,10,2,26,30,22,14,6,19,1..., dimensions={0} | all-to-all | bytes 786432 | tf_op jit(solution)/shard_map/all_to_all | solution.py:514
  34.2 0.2 shard_map.53
  34.4 0.1 collective-permute-start.3
  34.5 0.2 shard_map.54.refs_1_
  34.7 1.2 %collective-permute-done.3.refs_0_ = bf16[128,768]{1,0:T(8,128)(2,1)S(1)} collective-permute-done((bf16[128,768]{1,0:T(8,128)(2,1)S(1)}, bf16[128,768]{1,0:T(8,128)(2,1)S(1)}, u32[]{:S(2)}, u32[]{:S(2)}) %collective-permute-start.3) | collective-permute-done | bytes 196640 | tf_op jit(solution)/shard_map/ppermute | solution.py:448
  35.9 0.8 %shard_map.55 = bf16[128,768]{1,0:T(8,128)(2,1)} custom-call(f32[128,128]{1,0:T(8,128)S(1)} %get-tuple-element.31.cos_ref, f32[128,128]{1,0:T(8,128)S(1)} %get-tuple-element.32.sin_ref, bf16[128,768]{1,0:T(8,128)(2,1)S(1)} %collective-permute-done.3.refs_0_, bf16[128,768]{1,0:T(8,128)(2,1)S(1)} %shard_map.54.refs_1_), custom_call_target="tpu_custom_call" | custom-call | tf_op jit(solution)/shard_map/pallas_call | solution.py:421
  (3 shorter events, 0.1 us)
Async XLA Ops:
  0.0 3.9 %copy-start.1 = (bf16[16,8,768]{2,1,0:T(8,128)(2,1)S(1)}, bf16[16,8,768]{2,1,0:T(8,128)(2,1)}, u32[]{:S(2)}) copy-start(bf16[16,8,768]{2,1,0:T(8,128)(2,1)} %param.4) | copy-start | bytes 589828
  0.0 3.9 %collective-permute-start = (bf16[128,768]{1,0:T(8,128)(2,1)}, bf16[128,768]{1,0:T(8,128)(2,1)S(1)}, u32[]{:S(2)}, u32[]{:S(2)}) collective-permute-start(bf16[128,768]{1,0:T(8,128)(2,1)} %bitcast.14), channel_id=1, source_target_pairs={{0,2},{2,0},{4,6},{6,4},{8,10},{10,8},{12,14},{14,12},{16,18},{18,... | collective-permute-start | bytes 589832 | tf_op jit(solution)/shard_map/ppermute | solution.py:448
  0.5 3.4 %collective-permute-start.1 = (s32[3,16]{1,0:T(4,128)}, s32[3,16]{1,0:T(4,128)S(1)}, u32[]{:S(2)}, u32[]{:S(2)}) collective-permute-start(s32[3,16]{1,0:T(4,128)} %pos_ref.1), channel_id=1, source_target_pairs={{0,2},{2,0},{4,6},{6,4},{8,10},{10,8},{12,14},{14,12},{16,18},{18,... | collective-permute-start | bytes 584 | tf_op jit(solution)/shard_map/ppermute | solution.py:448
  5.2 8.9 %copy-start = (bf16[32,8,512]{2,1,0:T(8,128)(2,1)S(1)}, bf16[32,8,512]{2,1,0:T(8,128)(2,1)}, u32[]{:S(2)}) copy-start(bf16[32,8,512]{2,1,0:T(8,128)(2,1)} %param.7) | copy-start | bytes 786436
  5.2 17.9 %all-to-all-start = ((bf16[16,16,768]{2,1,0:T(8,128)(2,1)}), bf16[16,16,768]{2,1,0:T(8,128)(2,1)S(1)}, u32[]{:S(2)}, u32[]{:S(2)}) async-start(bf16[16,16,768]{2,1,0:T(8,128)(2,1)} %bitcast.3), calls=%async_computation | async-start | bytes 786432 | tf_op jit(solution)/shard_map/all_to_all | solution.py:514
  14.2 6.6 %collective-permute-start.2 = (bf16[128,512]{1,0:T(8,128)(2,1)S(1)}, bf16[128,512]{1,0:T(8,128)(2,1)S(1)}, u32[]{:S(2)}, u32[]{:S(2)}) collective-permute-start(bf16[128,512]{1,0:T(8,128)(2,1)S(1)} %get-tuple-element.37), channel_id=1, source_target_pairs={{0,1},{1,0},{2,3},{3,2},{4,5},{5,4},{6,7},{7,6},{8,9},{9,8},{10,11... | collective-permute-start | bytes 393224 | tf_op jit(solution)/shard_map/ppermute | solution.py:522
  16.4 0.7 %copy-start.3 = (s32[512,1]{0,1:T(1,128)S(1)}, s32[512,1]{0,1:T(1,128)}, u32[]{:S(2)}) copy-start(s32[512,1]{0,1:T(1,128)} %param.6) | copy-start | bytes 6148
  16.4 0.7 %copy-start.2 = (s32[3,16]{1,0:T(4,128)S(1)}, s32[3,16]{1,0:T(4,128)}, u32[]{:S(2)}) copy-start(s32[3,16]{1,0:T(4,128)} %pos_ref.1) | copy-start | bytes 580
  34.4 1.5 %collective-permute-start.3 = (bf16[128,768]{1,0:T(8,128)(2,1)S(1)}, bf16[128,768]{1,0:T(8,128)(2,1)S(1)}, u32[]{:S(2)}, u32[]{:S(2)}) collective-permute-start(bf16[128,768]{1,0:T(8,128)(2,1)S(1)} %shard_map.53), channel_id=1, source_target_pairs={{0,2},{2,0},{4,6},{6,4},{8,10},{10,8},{12,14},{14,12},{16,18},{18,... | collective-permute-start | bytes 589832 | tf_op jit(solution)/shard_map/ppermute | solution.py:448

commit v11 on v9

--- a/solution.py
+++ b/solution.py
@@ -249,12 +249,11 @@
     def _():
         pairs = ((dest_hbm, dest_ref), (pos_hbm, pos_ref), (cot_hbm, cot_ref))
         loads = [pltpu.make_async_copy(a, b, sems.at[n]) for n, (a, b) in enumerate(pairs)]
-        for load in loads[:2]:
+        for load in loads:
             load.start()
         for load in loads[:2]:
             load.wait()
         fill_tables(pos_ref, dest_ref, out_refs[2:], tiles, heads, local, sides)
-        loads[2].start()
         loads[2].wait()
         split_cots(cot_ref, *out_refs[:2], local)
 

time: 37.1 us -> 38.3 us (1.032)
  blocking collectives: 10.4 us -> 11.7 us
  Pallas kernels: 7.37 us -> 6.65 us
  waiting for transfers between devices: 6.42 us -> 7.13 us
    all_to_all x1, blocking collectives: 10.4 us -> 11.7 us  [swap(): lax.all_to_all(parts, axes, split_axis=0, concat_axis=0, tiled=True, axis...]
    pallas_call x10, Pallas kernels: 7.37 us -> 6.65 us  [call(): pl.pallas_call(kernel, out_shape=shapes[0] if single else shapes, in_spec...]
    ppermute x1, waiting for transfers between devices: 3.2 us -> 3.7 us  [body(): cots = [own, lax.ppermute(other, 'head', [(0, 1), (1, 0)])]]
  transfers between devices with their start and end apart: 5 -> 5, of which waited for: 3 -> 3; matrix products, arithmetic and copies ran while one was open for 2% -> 2% of each run, Pallas kernels for 12% -> 10%
where the time goes in v11:
time: 38.3 us; the launch traced here: 38 us
  blocking collectives  11.7 us (31%)
  starting transfers between devices  11 us (29%)
  waiting for transfers between devices  7.13 us (19%)
  Pallas kernels  6.65 us (17%)
  local copies, waits for them, and re-layouts  1.38 us (4%)
    all_to_all x1, blocking collectives, swap(): lax.all_to_all(parts, axes, split_axis=0, concat_axis=0, tiled=True, axis...  11.7 us
    all_to_all x1, starting transfers between devices, swap(): lax.all_to_all(parts, axes, split_axis=0, concat_axis=0, tiled=True, axis...  8.92 us
    pallas_call x10, Pallas kernels, call(): pl.pallas_call(kernel, out_shape=shapes[0] if single else shapes, in_spec...  6.65 us
    ppermute x1, waiting for transfers between devices, body(): cots = [own, lax.ppermute(other, 'head', [(0, 1), (1, 0)])]  3.7 us
    all_to_all x1, waiting for transfers between devices, swap(): lax.all_to_all(parts, axes, split_axis=0, concat_axis=0, tiled=True, axis...  2.22 us
    ppermute x1, starting transfers between devices, body(): cots = [own, lax.ppermute(other, 'head', [(0, 1), (1, 0)])]  1.53 us
    ppermute x3, waiting for transfers between devices, to_pair(): return lax.ppermute(x, 'tile', [(t, t ^ 1) for t in range(tiles)])  1.21 us
  transfers between devices with their start and end apart: 5, of which 3 were waited for; matrix products, arithmetic and copies ran while one was open for 2% of the time, Pallas kernels for 10%

profile of v11, /device:TPU:0, one launch (start us, length us, event | category | flops | bytes accessed | tf_op | source)
XLA Modules:
  0.0 38.0 jit_solution(11394869075279014658)
XLA Ops:
  0.0 0.0 copy-start.1
  0.0 0.5 %collective-permute-start = (bf16[128,768]{1,0:T(8,128)(2,1)}, bf16[128,768]{1,0:T(8,128)(2,1)S(1)}, u32[]{:S(2)}, u32[]{:S(2)}) collective-permute-start(bf16[128,768]{1,0:T(8,128)(2,1)} %bitcast.14), channel_id=1, source_target_pairs={{0,2},{2,0},{4,6},{6,4},{8,10},{10,8},{12,14},{14,12},{16,18},{18,... | collective-permute-start | bytes 589832 | tf_op jit(solution)/shard_map/ppermute | solution.py:449
  0.5 0.1 collective-permute-start.1
  0.5 1.0 %shard_map.46 = (f32[16,128]{1,0:T(8,128)S(1)}, f32[16,128]{1,0:T(8,128)S(1)}, bf16[256,256]{1,0:T(8,128)(2,1)S(1)}) custom-call(s32[3,16]{1,0:T(4,128)} %pos_ref.1, s32[4,128]{1,0:T(4,128)} %bitcast.16), custom_call_target="tpu_custom_call" | custom-call | tf_op jit(solution)/shard_map/pallas_call | solution.py:422
  1.5 2.2 %shard_map.47 = (bf16[128,512]{1,0:T(8,128)(2,1)S(1)}, bf16[128,512]{1,0:T(8,128)(2,1)S(1)}, f32[128,128]{1,0:T(8,128)S(1)}, f32[128,128]{1,0:T(8,128)S(1)}, bf1...) custom-call(bf16[256,512]{1,0:T(8,128)(2,1)} %bitcast.12, s32[3,16]{1,0:T(4,128)} %pos_ref.1, ...), custom_call_target="tpu_custom_call" | custom-call | tf_op jit(solution)/shard_map/pallas_call | solution.py:422
  3.7 0.0 collective-permute-done.1.refs_1_
  3.7 0.0 collective-permute-done.refs_0_
  3.8 0.0 copy-done.1
  3.8 1.3 %shard_map.48 = bf16[256,768]{1,0:T(8,128)(2,1)} custom-call(bf16[128,768]{1,0:T(8,128)(2,1)S(1)} %bitcast.15, f32[16,128]{1,0:T(8,128)S(1)} %get-tuple-element.22.cos_ref, f32[16,128]{1,0:T(8,128)S(1)} %get-tuple-element.23.sin_ref, bf16[256,256]{1,0:T(8,128)(2,1)S(1)} %get-tuple-element.24.place_ref, bf16[16,128]{1,0:T(8,128)(2,1)S(1)} %slice.6.after_ref, ...), custom_call_target="tpu_custom_call" | custom-call | tf_op jit(solution)/shard_map/pallas_call | solution.py:422
  5.1 0.0 copy-start
  5.1 8.9 %all-to-all-start = ((bf16[16,16,768]{2,1,0:T(8,128)(2,1)}), bf16[16,16,768]{2,1,0:T(8,128)(2,1)S(1)}, u32[]{:S(2)}, u32[]{:S(2)}) async-start(bf16[16,16,768]{2,1,0:T(8,128)(2,1)} %bitcast.3), calls=%async_computation | async-start | bytes 786432 | tf_op jit(solution)/shard_map/all_to_all | solution.py:515
  14.0 0.0 copy-done
  14.1 1.5 %collective-permute-start.2 = (bf16[128,512]{1,0:T(8,128)(2,1)S(1)}, bf16[128,512]{1,0:T(8,128)(2,1)S(1)}, u32[]{:S(2)}, u32[]{:S(2)}) collective-permute-start(bf16[128,512]{1,0:T(8,128)(2,1)S(1)} %get-tuple-element.37), channel_id=1, source_target_pairs={{0,1},{1,0},{2,3},{3,2},{4,5},{5,4},{6,7},{7,6},{8,9},{9,8},{10,11... | collective-permute-start | bytes 393224 | tf_op jit(solution)/shard_map/ppermute | solution.py:523
  15.6 0.7 %slice.8.after_ref = bf16[16,128]{1,0:T(8,128)(2,1)S(1)} slice(bf16[256,768]{1,0:T(8,128)(2,1)} %shard_map.48), slice={[0:16], [0:128]} | slice | bytes 8192 | tf_op jit(solution)/shard_map/slice | solution.py:532
  16.3 0.0 copy-start.3
  16.3 0.0 copy-start.2
  16.3 0.7 %copy-done.3 = s32[512,1]{0,1:T(1,128)S(1)} copy-done((s32[512,1]{0,1:T(1,128)S(1)}, s32[512,1]{0,1:T(1,128)}, u32[]{:S(2)}) %copy-start.3) | copy-done | bytes 2072
  17.0 0.0 copy-done.2
  17.0 3.7 %collective-permute-done.2.refs_1_ = bf16[128,512]{1,0:T(8,128)(2,1)S(1)} collective-permute-done((bf16[128,512]{1,0:T(8,128)(2,1)S(1)}, bf16[128,512]{1,0:T(8,128)(2,1)S(1)}, u32[]{:S(2)}, u32[]{:S(2)}) %collective-permute-start.2) | collective-permute-done | bytes 131104 | tf_op jit(solution)/shard_map/ppermute | solution.py:523
  20.7 0.2 shard_map.51.cot_ref
  20.9 2.2 %all-to-all-done = bf16[16,16,768]{2,1,0:T(8,128)(2,1)S(1)} async-done(((bf16[16,16,768]{2,1,0:T(8,128)(2,1)}), bf16[16,16,768]{2,1,0:T(8,128)(2,1)S(1)}, u32[]{:S(2)}, u32[]{:S(2)}) %all-to-all-start) | async-done | bytes 393248 | tf_op jit(solution)/shard_map/all_to_all | solution.py:515
  23.2 0.6 %shard_map.52 = bf16[256,768]{1,0:T(8,128)(2,1)S(1)} custom-call(bf16[256,768]{1,0:T(8,128)(2,1)S(1)} %bitcast.10, f32[64,256]{1,0:T(8,128)S(1)} %get-tuple-element.33.bias_ref, bf16[1024,128]{1,0:T(8,128)(2,1)S(1)} %shard_map.51.cot_ref), custom_call_target="tpu_custom_call" | custom-call | tf_op jit(solution)/shard_map/pallas_call | solution.py:422
  23.8 11.7 %all_to_all.10 = bf16[16,16,768]{2,1,0:T(8,128)(2,1)S(1)} all-to-all(bf16[16,16,768]{2,1,0:T(8,128)(2,1)S(1)} %bitcast.11), channel_id=1, replica_groups={{16,8,0,24,28,20,12,4,17,9,1,25,29,21,13,5},{18,10,2,26,30,22,14,6,19,1..., dimensions={0} | all-to-all | bytes 786432 | tf_op jit(solution)/shard_map/all_to_all | solution.py:515
  35.5 0.2 shard_map.53
  35.7 0.1 collective-permute-start.3
  35.8 0.2 shard_map.54.refs_1_
  36.0 1.2 %collective-permute-done.3.refs_0_ = bf16[128,768]{1,0:T(8,128)(2,1)S(1)} collective-permute-done((bf16[128,768]{1,0:T(8,128)(2,1)S(1)}, bf16[128,768]{1,0:T(8,128)(2,1)S(1)}, u32[]{:S(2)}, u32[]{:S(2)}) %collective-permute-start.3) | collective-permute-done | bytes 196640 | tf_op jit(solution)/shard_map/ppermute | solution.py:449
  37.2 0.8 %shard_map.55 = bf16[128,768]{1,0:T(8,128)(2,1)} custom-call(f32[128,128]{1,0:T(8,128)S(1)} %get-tuple-element.31.cos_ref, f32[128,128]{1,0:T(8,128)S(1)} %get-tuple-element.32.sin_ref, bf16[128,768]{1,0:T(8,128)(2,1)S(1)} %collective-permute-done.3.refs_0_, bf16[128,768]{1,0:T(8,128)(2,1)S(1)} %shard_map.54.refs_1_), custom_call_target="tpu_custom_call" | custom-call | tf_op jit(solution)/shard_map/pallas_call | solution.py:422
  (3 shorter events, 0.1 us)
Async XLA Ops:
  0.0 3.8 %copy-start.1 = (bf16[16,8,768]{2,1,0:T(8,128)(2,1)S(1)}, bf16[16,8,768]{2,1,0:T(8,128)(2,1)}, u32[]{:S(2)}) copy-start(bf16[16,8,768]{2,1,0:T(8,128)(2,1)} %param.4) | copy-start | bytes 589828
  0.0 3.7 %collective-permute-start = (bf16[128,768]{1,0:T(8,128)(2,1)}, bf16[128,768]{1,0:T(8,128)(2,1)S(1)}, u32[]{:S(2)}, u32[]{:S(2)}) collective-permute-start(bf16[128,768]{1,0:T(8,128)(2,1)} %bitcast.14), channel_id=1, source_target_pairs={{0,2},{2,0},{4,6},{6,4},{8,10},{10,8},{12,14},{14,12},{16,18},{18,... | collective-permute-start | bytes 589832 | tf_op jit(solution)/shard_map/ppermute | solution.py:449
  0.5 3.3 %collective-permute-start.1 = (s32[3,16]{1,0:T(4,128)}, s32[3,16]{1,0:T(4,128)S(1)}, u32[]{:S(2)}, u32[]{:S(2)}) collective-permute-start(s32[3,16]{1,0:T(4,128)} %pos_ref.1), channel_id=1, source_target_pairs={{0,2},{2,0},{4,6},{6,4},{8,10},{10,8},{12,14},{14,12},{16,18},{18,... | collective-permute-start | bytes 584 | tf_op jit(solution)/shard_map/ppermute | solution.py:449
  5.1 8.9 %copy-start = (bf16[32,8,512]{2,1,0:T(8,128)(2,1)S(1)}, bf16[32,8,512]{2,1,0:T(8,128)(2,1)}, u32[]{:S(2)}) copy-start(bf16[32,8,512]{2,1,0:T(8,128)(2,1)} %param.7) | copy-start | bytes 786436
  5.1 18.1 %all-to-all-start = ((bf16[16,16,768]{2,1,0:T(8,128)(2,1)}), bf16[16,16,768]{2,1,0:T(8,128)(2,1)S(1)}, u32[]{:S(2)}, u32[]{:S(2)}) async-start(bf16[16,16,768]{2,1,0:T(8,128)(2,1)} %bitcast.3), calls=%async_computation | async-start | bytes 786432 | tf_op jit(solution)/shard_map/all_to_all | solution.py:515
  14.1 6.6 %collective-permute-start.2 = (bf16[128,512]{1,0:T(8,128)(2,1)S(1)}, bf16[128,512]{1,0:T(8,128)(2,1)S(1)}, u32[]{:S(2)}, u32[]{:S(2)}) collective-permute-start(bf16[128,512]{1,0:T(8,128)(2,1)S(1)} %get-tuple-element.37), channel_id=1, source_target_pairs={{0,1},{1,0},{2,3},{3,2},{4,5},{5,4},{6,7},{7,6},{8,9},{9,8},{10,11... | collective-permute-start | bytes 393224 | tf_op jit(solution)/shard_map/ppermute | solution.py:523
  16.3 0.7 %copy-start.3 = (s32[512,1]{0,1:T(1,128)S(1)}, s32[512,1]{0,1:T(1,128)}, u32[]{:S(2)}) copy-start(s32[512,1]{0,1:T(1,128)} %param.6) | copy-start | bytes 6148
  16.3 0.7 %copy-start.2 = (s32[3,16]{1,0:T(4,128)S(1)}, s32[3,16]{1,0:T(4,128)}, u32[]{:S(2)}) copy-start(s32[3,16]{1,0:T(4,128)} %pos_ref.1) | copy-start | bytes 580
  35.7 1.5 %collective-permute-start.3 = (bf16[128,768]{1,0:T(8,128)(2,1)S(1)}, bf16[128,768]{1,0:T(8,128)(2,1)S(1)}, u32[]{:S(2)}, u32[]{:S(2)}) collective-permute-start(bf16[128,768]{1,0:T(8,128)(2,1)S(1)} %shard_map.53), channel_id=1, source_target_pairs={{0,2},{2,0},{4,6},{6,4},{8,10},{10,8},{12,14},{14,12},{16,18},{18,... | collective-permute-start | bytes 589832 | tf_op jit(solution)/shard_map/ppermute | solution.py:449
